TPU v7x, 256 devices: a whole 4x4x8 slice. The times are simulated.
256 devices in a mesh: grp: 16 (over z, core), atm: 16 (over y, x).
Axes of the slice: x: 4, y: 4, z: 8, core: 2. Of those that a mesh axis runs over, the one named last changes fastest.
Arguments:
- atoms: float32 [2, 65536, 128], P(None, ('grp', 'atm')), may hold values from -6 to 6
- kinds: int32 [2, 65536], P(None, ('grp', 'atm')), may hold values from 0 to 3
- member: int32 [2, 65536], P(None, ('grp', 'atm')), may hold values from 0 to 7
- targets: float32 [2, 128], replicated, may hold values from -900 to 900
- weights: float32 [128, 128], replicated, may hold values from -0.5 to 0.5
- bias: float32 [128], replicated, may hold values from -0.5 to 0.5
- readout: float32 [4, 128], replicated, may hold values from -0.5 to 0.5
- covariance: float32 [16384, 16384], P('grp', 'atm'), as said below
Outputs:
- posterior: float32 [16384, 16384], P('grp', 'atm')
- weights_out: float32 [128, 128], replicated
Inputs may be any that keep to these rules, and one draw needn't show every extreme that they name: `covariance`: symmetric and positive definite.
All inputs are finite; a program needn't handle non-finite values.
Results may differ from a plain program's by a relative error of at most 0.0007.
Values sent between devices are 32-bit elements; how exact they have to be, the bound alone decides.
No kernel may reach another device: no remote copies, remote signals or barrier semaphores. Data moves between devices by JAX's collectives and lax.ppermute only.
A program may use at most 64 MiB of HBM per device.

v0:
```python
import jax
import jax.numpy as jnp
from jax import lax
from jax.sharding import PartitionSpec as P

FEATURES = 128
GROUP_LOCAL = 8
STEPS = 2


forget_rate = 0.98


def local_terms(atoms, kinds, member, weights, bias, readout):
    precise = lax.Precision.HIGHEST
    preact = jnp.dot(atoms, weights, precision=precise, preferred_element_type=jnp.float32) + bias
    hidden = jnp.tanh(preact)
    type_hot = (kinds[:, None] == jnp.arange(readout.shape[0])[None, :]).astype(jnp.float32)
    vectors = jnp.dot(type_hot, readout, precision=precise)
    atom_energy = jnp.sum(hidden * vectors, axis=1)
    slope = (1.0 - hidden * hidden) * vectors
    group_hot = (member[:, None] == jnp.arange(GROUP_LOCAL)[None, :]).astype(jnp.float32)
    energies = jnp.dot(atom_energy, group_hot, precision=precise)
    masked = atoms[:, None, :] * group_hot[:, :, None]
    grads = jnp.einsum("agi,ac->gic", masked, slope, precision=precise)
    return (energies, grads.reshape(GROUP_LOCAL, FEATURES * FEATURES))


def body(atoms, kinds, member, targets, weights, bias, readout, covariance):
    precise = lax.Precision.HIGHEST
    col_index = lax.axis_index("atm")
    group_total = GROUP_LOCAL * lax.axis_size("grp")
    col_width = covariance.shape[1]
    identity = jnp.eye(group_total, dtype=jnp.float32)
    current = weights
    covar = covariance
    for update_idx in range(STEPS):
        energies, partial_value = local_terms(
            atoms[update_idx], kinds[update_idx], member[update_idx], current, bias, readout
        )
        summed = lax.psum(energies, "atm")
        predicted = lax.all_gather(summed, "grp", axis=0, tiled=True)
        mismatch = targets[update_idx] - predicted
        grad_block = lax.psum_scatter(partial_value, "atm", scatter_dimension=1, tiled=True)
        grad_columns = lax.all_gather(grad_block, "grp", axis=0, tiled=True)
        row_terms = lax.dot_general(
            covar,
            grad_columns,
            (((1,), (1,)), ((), ())),
            precision=precise,
            preferred_element_type=jnp.float32,
        )
        row_gains = lax.psum(row_terms, "atm")
        full_gains = lax.all_gather(row_gains, "grp", axis=0, tiled=True)
        col_gains = lax.dynamic_slice_in_dim(full_gains, col_index * col_width, col_width, 0)
        curvature = lax.psum(jnp.dot(grad_columns, col_gains, precision=precise), "atm")
        innovation = 0.5 * (curvature + curvature.T) + forget_rate * identity
        factor = jnp.linalg.cholesky(innovation)
        inverse = jax.scipy.linalg.cho_solve((factor, True), identity)
        coefficient = jnp.dot(inverse, mismatch, precision=precise)
        change = jnp.dot(full_gains, coefficient, precision=precise)
        current = current + change.reshape(FEATURES, FEATURES)
        scaled = jnp.dot(row_gains, inverse, precision=precise)
        downdate = lax.dot_general(
            scaled,
            col_gains,
            (((1,), (1,)), ((), ())),
            precision=precise,
            preferred_element_type=jnp.float32,
        )
        covar = (covar - downdate) / forget_rate
    return (covar, current)


def solution(mesh):
    return jax.shard_map(
        body,
        mesh=mesh,
        in_specs=(
            P(None, ("grp", "atm"), None),
            P(None, ("grp", "atm")),
            P(None, ("grp", "atm")),
            P(),
            P(),
            P(),
            P(),
            P("grp", "atm"),
        ),
        out_specs=(P("grp", "atm"), P()),
        check_vma=False,
    )
```

profile of v0, /device:TPU:1, one launch (start us, length us, event | category | flops | bytes accessed | tf_op | source)
XLA Modules:
  0.0 792.7 jit_solution(14846708267292088303)
XLA Ops:
  7.2 0.8 fusion.59
  8.0 0.8 fusion.60
  8.8 1.0 slice_bitcast_fusion
  10.2 1.3 multiply_reduce_fusion.1
  11.5 1.0 convolution_bitcast_fusion.1
  12.5 1.1 copy.27
  13.6 79.5 %reduce-scatter.3.cloned.1.call-done = f32[8,1024]{1,0:T(8,128)} async-done(((f32[8,16384]{1,0:T(8,128)}), f32[8,1024]{1,0:T(8,128)}) %reduce-scatter.3.cloned.1.call-update) | async-done | bytes 32784 | tf_op jit(solution)/shard_map/reduce_scatter | solution.py:44
  93.2 21.2 %all_gather.18 = f32[128,1024]{1,0:T(8,128)S(1)} all-gather(f32[8,1024]{1,0:T(8,128)} %reduce-scatter.3.cloned.1.call-done), channel_id=1, replica_groups=mesh['grp'=16,'atm'=16] {'grp'}, dimensions={0}, use_global_device_ids=true | all-gather | bytes 557056 | tf_op jit(solution)/shard_map/all_gather | solution.py:45
  114.4 7.3 convolution_bitcast_fusion.2
  121.8 90.4 %all-reduce.7.cloned.1.call-done = f32[1024,128]{0,1:T(8,128)} async-done(((f32[1024,128]{0,1:T(8,128)}), f32[1024,128]{0,1:T(8,128)}) %all-reduce.7.cloned.1.call-update) | async-done | bytes 524304 | tf_op jit(solution)/shard_map/psum | solution.py:53
  212.4 0.3 fusion.24
  212.7 58.4 %all-gather.3.cloned.1.call-done = f32[16384,128]{0,1:T(8,128)} async-done(((f32[1024,128]{0,1:T(8,128)}), f32[16384,128]{0,1:T(8,128)}) %all-gather.3.cloned.1.call-update) | async-done | bytes 8388624 | tf_op jit(solution)/shard_map/all_gather | solution.py:54
  271.1 2.3 fusion.13
  273.5 33.2 %psum.44 = f32[8]{0:T(128)S(1)} all-reduce(f32[8]{0:T(128)S(1)} %convolution_bitcast_fusion.6), channel_id=1, replica_groups=mesh['grp'=16,'atm'=16] {'atm'}, use_global_device_ids=true, to_apply=%region_6.0 | all-reduce | flops 8 | bytes 64 | tf_op jit(solution)/shard_map/psum | solution.py:41
  306.8 0.6 dynamic-slice
  308.3 30.7 %all-reduce = f32[128]{0:T(128)S(1)} all-reduce(f32[128]{0:T(128)S(1)} %dynamic-update-slice.2), channel_id=1, replica_groups=mesh['grp'=16,'atm'=16] {'grp'}, use_global_device_ids=true, to_apply=%add | all-reduce | flops 128 | bytes 1024
  339.0 23.4 %all-reduce.9.cloned.1.call-done = f32[128,128]{1,0:T(8,128)} async-done(((f32[128,128]{1,0:T(8,128)}), f32[128,128]{1,0:T(8,128)}) %all-reduce.9.cloned.1.call-update) | async-done | bytes 65552 | tf_op jit(solution)/shard_map/psum | solution.py:56
  362.4 0.9 copy.12
  363.3 0.9 select_add_fusion.1
  364.3 11.7 %cholesky.44 = f32[128,128]{1,0:T(8,128)S(1)} custom-call(f32[128,128]{1,0:T(8,128)S(1)} %fusion.39), custom_call_target="Cholesky" | custom-call | tf_op jit(solution)/shard_map/jit(cholesky)/cholesky | solution.py:58
  376.0 0.6 compare_reduce_fusion.1
  376.7 0.7 fusion.29
  377.4 9.8 %custom-call.8 = f32[1,128,128]{1,2,0:T(8,128)S(1)} custom-call(f32[1,128,128]{2,1,0:T(8,128)S(1)} %fusion.29), custom_call_target="InvertDiagBlocksLowerTriangular" | custom-call | tf_op jit(solution)/shard_map/jit(_cho_solve)/triangular_solve | solution.py:59
  387.9 6.9 fusion.62
  394.9 0.3 multiply_reduce_fusion
  395.2 1.0 convolution_bitcast_fusion
  396.2 1.2 copy.26
  397.6 1.0 fusion.61
  398.6 6.8 subtract_multiply_fusion.1
  405.4 68.8 %reduce-scatter.5.cloned.1.call-done = f32[8,1024]{1,0:T(8,128)} async-done(((f32[8,16384]{1,0:T(8,128)}), f32[8,1024]{1,0:T(8,128)}) %reduce-scatter.5.cloned.1.call-update) | async-done | bytes 32784 | tf_op jit(solution)/shard_map/reduce_scatter | solution.py:44
  474.3 21.2 %all_gather.21 = f32[128,1024]{1,0:T(8,128)S(1)} all-gather(f32[8,1024]{1,0:T(8,128)} %reduce-scatter.5.cloned.1.call-done), channel_id=1, replica_groups=mesh['grp'=16,'atm'=16] {'grp'}, dimensions={0}, use_global_device_ids=true | all-gather | bytes 557056 | tf_op jit(solution)/shard_map/all_gather | solution.py:45
  495.5 6.4 fusion.63
  501.9 90.4 %all-reduce.11.cloned.1.call-done = f32[1024,128]{1,0:T(8,128)} async-done(((f32[1024,128]{1,0:T(8,128)}), f32[1024,128]{1,0:T(8,128)}) %all-reduce.11.cloned.1.call-update) | async-done | bytes 524304 | tf_op jit(solution)/shard_map/psum | solution.py:53
  592.4 59.0 %all-gather.5.cloned.1.call-done = f32[16384,128]{1,0:T(8,128)} async-done(((f32[1024,128]{1,0:T(8,128)}), f32[16384,128]{1,0:T(8,128)}) %all-gather.5.cloned.1.call-update) | async-done | bytes 8388624 | tf_op jit(solution)/shard_map/all_gather | solution.py:54
  651.4 2.3 fusion.10
  653.8 33.2 %psum.47 = f32[8]{0:T(128)S(1)} all-reduce(f32[8]{0:T(128)S(1)} %convolution_bitcast_fusion.5), channel_id=1, replica_groups=mesh['grp'=16,'atm'=16] {'atm'}, use_global_device_ids=true, to_apply=%region_11.14 | all-reduce | flops 8 | bytes 64 | tf_op jit(solution)/shard_map/psum | solution.py:41
  687.3 30.5 %all-reduce.1 = f32[128]{0:T(128)S(1)} all-reduce(f32[128]{0:T(128)S(1)} %dynamic-update-slice.3), channel_id=1, replica_groups=mesh['grp'=16,'atm'=16] {'grp'}, use_global_device_ids=true, to_apply=%add.1 | all-reduce | flops 128 | bytes 1024
  717.7 25.4 %all-reduce.13.cloned.1.call-done = f32[128,128]{1,0:T(8,128)} async-done(((f32[128,128]{1,0:T(8,128)}), f32[128,128]{1,0:T(8,128)}) %all-reduce.13.cloned.1.call-update) | async-done | bytes 65552 | tf_op jit(solution)/shard_map/psum | solution.py:56
  743.1 0.9 copy.16
  744.0 0.9 select_add_fusion
  745.0 11.7 %cholesky.55 = f32[128,128]{1,0:T(8,128)S(1)} custom-call(f32[128,128]{1,0:T(8,128)S(1)} %fusion.34), custom_call_target="Cholesky" | custom-call | tf_op jit(solution)/shard_map/jit(cholesky)/cholesky | solution.py:58
  756.7 0.6 compare_reduce_fusion
  757.4 0.7 fusion.30
  758.1 9.8 %custom-call.9 = f32[1,128,128]{1,2,0:T(8,128)S(1)} custom-call(f32[1,128,128]{2,1,0:T(8,128)S(1)} %fusion.30), custom_call_target="InvertDiagBlocksLowerTriangular" | custom-call | tf_op jit(solution)/shard_map/jit(_cho_solve)/triangular_solve | solution.py:59
  768.6 9.6 %fusion.65 = f32[1,16384]{1,0:T(1,128)S(1)} fusion(f32[16384,128]{1,0:T(8,128)} %all-gather.5.cloned.1.call-done, f32[128,1]{0,1:T(1,128)S(1)} %convolution_bitcast_fusion.3), kind=kOutput, calls=%fused_computation.103 | convolution fusion | flops 25165824 | bytes 8454656 | tf_op jit(solution)/shard_map/dot_general | solution.py:61
  778.2 0.6 add.76
  778.8 0.6 fusion.64
  779.4 6.3 subtract_multiply_fusion
  (58 shorter events, 3.5 us)
Async XLA Ops:
  7.2 2.7 copy-start
  7.2 86.0 %reduce-scatter.3.cloned.1.call-start = ((), (), s32[]{:S(2)}) async-start(), calls=%async_computation.2 | async-start | bytes 557056 | tf_op jit(solution)/shard_map/reduce_scatter | solution.py:44
  13.6 293.2 %copy-start.8 = (u32[256]{0:T(256)S(1)}, u32[256]{0:T(256)}, u32[]{:S(2)}) copy-start(u32[256]{0:T(256)} %constant.60) | copy-start | bytes 3076
  13.6 198.6 %all-reduce.7.cloned.1.call-start = ((), (), s32[]{:S(2)}) async-start(), calls=%async_computation.3 | async-start | bytes 1048576 | tf_op jit(solution)/shard_map/psum | solution.py:53
  114.4 273.3 %copy-start.6 = (f32[2,128]{1,0:T(2,128)S(1)}, f32[2,128]{1,0:T(2,128)}, u32[]{:S(2)}) copy-start(f32[2,128]{1,0:T(2,128)} %param.14) | copy-start | bytes 3076
  121.7 149.4 %all-gather.3.cloned.1.call-start = ((), (), s32[]{:S(2)}) async-start(), calls=%async_computation.4 | async-start | bytes 8912896 | tf_op jit(solution)/shard_map/all_gather | solution.py:54
  212.2 150.2 %all-reduce.9.cloned.1.call-start = ((), (), s32[]{:S(2)}) async-start(), calls=%async_computation.5 | async-start | bytes 131072 | tf_op jit(solution)/shard_map/psum | solution.py:56
  273.4 200.8 %reduce-scatter.5.cloned.1.call-start = ((), (), s32[]{:S(2)}) async-start(), calls=%async_computation.6 | async-start | bytes 557056 | tf_op jit(solution)/shard_map/reduce_scatter | solution.py:44
  387.9 6.9 copy-start.5
  387.9 7.0 copy-start.4
  387.9 7.0 copy-start.7
  387.9 9.7 %copy-start.2 = (f32[1024,128]{0,1:T(8,128)S(1)}, f32[1024,128]{0,1:T(8,128)}, u32[]{:S(2)}) copy-start(f32[1024,128]{0,1:T(8,128)} %all-reduce.7.cloned.1.call-done) | copy-start | bytes 1572868
  397.4 194.9 %all-reduce.11.cloned.1.call-start = ((), (), s32[]{:S(2)}) async-start(), calls=%async_computation.7 | async-start | bytes 1048576 | tf_op jit(solution)/shard_map/psum | solution.py:53
  501.9 149.5 %all-gather.5.cloned.1.call-start = ((), (), s32[]{:S(2)}) async-start(), calls=%async_computation.8 | async-start | bytes 8912896 | tf_op jit(solution)/shard_map/all_gather | solution.py:54
  592.3 150.8 %all-reduce.13.cloned.1.call-start = ((), (), s32[]{:S(2)}) async-start(), calls=%async_computation.9 | async-start | bytes 131072 | tf_op jit(solution)/shard_map/psum | solution.py:56
  768.5 10.3 %copy-start.3 = (f32[1024,128]{1,0:T(8,128)S(1)}, f32[1024,128]{1,0:T(8,128)}, u32[]{:S(2)}) copy-start(f32[1024,128]{1,0:T(8,128)} %all-reduce.11.cloned.1.call-done) | copy-start | bytes 1572868
  768.6 10.8 %copy-start.1 = (f32[1024,1024]{1,0:T(8,128)S(1)}, f32[1024,1024]{1,0:T(8,128)}, u32[]{:S(2)}) copy-start(f32[1024,1024]{1,0:T(8,128)} %subtract_multiply_fusion.1) | copy-start | bytes 12582916
Sparse Core Ops, SparseCore 0:
  13.7 79.4 reduce-scatter.2
  121.9 90.2 all-reduce.6
  214.0 57.0 all-gather.2
  274.8 87.5 all-reduce.8
  397.5 76.6 reduce-scatter.4
  502.0 90.2 all-reduce.10
  594.3 57.0 all-gather.4
  655.5 87.5 all-reduce.12
where the time goes:
time: 799 us; the launch traced here: 793 us
  waiting for transfers between devices  495 us (62%)
  blocking collectives  170 us (21%)
  matrix products  55.2 us (7%)
  other arithmetic  48.1 us (6%)
  between operations  15.4 us (2%)
  local copies, waits for them, and re-layouts  8.15 us (1%)
    psum x2, waiting for transfers between devices, body(): row_gains = lax.psum(row_terms, 'atm')  181 us
    reduce_scatter x2, waiting for transfers between devices, body(): lax.psum_scatter(partial_value, 'atm', scatter_dimension=1, tiled=True)  148 us
    all_gather x2, waiting for transfers between devices, body(): full_gains = lax.all_gather(row_gains, 'grp', axis=0, tiled=True)  117 us
    psum x2, blocking collectives, body(): summed = lax.psum(energies, 'atm')  66.5 us
    unnamed x2, blocking collectives  61.2 us
    psum x2, waiting for transfers between devices, body(): lax.psum(jnp.dot(grad_columns, col_gains, precision=precise), 'atm')  48.7 us
    all_gather x2, blocking collectives, body(): grad_columns = lax.all_gather(grad_block, 'grp', axis=0, tiled=True)  42.4 us
    another operation x6, other arithmetic, body(): factor = jnp.linalg.cholesky(innovation)  24.8 us
  transfers between devices with their start and end apart: 8, of which 8 were waited for; matrix products, arithmetic and copies ran while one was open for 1% of the time, Pallas kernels for 0%

commit v1 on v0

v1 whole, which is shorter than its diff:
```python
import jax
import jax.numpy as jnp
from jax import lax
from jax.sharding import PartitionSpec as P

FEATURES = 128
GROUP_LOCAL = 8
STEPS = 2

forget_rate = 0.98
precise = lax.Precision.HIGHEST


def local_terms(atoms, kinds, member, weights, bias, readout):
    preact = jnp.dot(atoms, weights, precision=precise, preferred_element_type=jnp.float32) + bias
    hidden = jnp.tanh(preact)
    type_hot = (kinds[:, None] == jnp.arange(readout.shape[0])[None, :]).astype(jnp.float32)
    vectors = jnp.dot(type_hot, readout, precision=precise)
    atom_energy = jnp.sum(hidden * vectors, axis=1)
    slope = (1.0 - hidden * hidden) * vectors
    group_hot = (member[:, None] == jnp.arange(GROUP_LOCAL)[None, :]).astype(jnp.float32)
    energies = jnp.dot(atom_energy, group_hot, precision=precise)
    masked = atoms[:, None, :] * group_hot[:, :, None]
    grads = jnp.einsum("agi,ac->gic", masked, slope, precision=precise)
    return (energies, grads.reshape(GROUP_LOCAL, FEATURES * FEATURES))


def exchange(chunks, axis):
    return lax.all_to_all(chunks, axis, 0, 0, tiled=True)


def spread(x, axis):
    return exchange(jnp.broadcast_to(x[None], (lax.axis_size(axis),) + x.shape), axis)


def swap(x, rows, cols):
    pairs = [(i * cols + j, j * cols + i) for i in range(rows) for j in range(cols)]
    return lax.ppermute(x, ("grp", "atm"), pairs)


def body(atoms, kinds, member, targets, weights, bias, readout, covariance):
    rows, cols = lax.axis_size("grp"), lax.axis_size("atm")
    group_total = GROUP_LOCAL * rows
    width = covariance.shape[1]
    lanes = FEATURES
    identity = jnp.eye(group_total, dtype=jnp.float32)
    current = weights
    covar = covariance
    for step in range(STEPS):
        energies, grads = local_terms(atoms[step], kinds[step], member[step], current, bias, readout)
        parts = grads.reshape(GROUP_LOCAL, cols, width).transpose(1, 0, 2)
        extra = jnp.broadcast_to(energies[None, :, None], (cols, GROUP_LOCAL, lanes))
        chunk = exchange(jnp.concatenate([parts, extra], axis=2), "atm").sum(axis=0)
        stacked = lax.all_gather(chunk, "grp", axis=0, tiled=True)
        jac = stacked[:, :width]
        mismatch = targets[step] - stacked[:, width]
        terms = lax.dot_general(jac, covar, (((1,), (1,)), ((), ())), precision=precise)
        own = exchange(terms.reshape(cols, group_total // cols, width), "atm").sum(axis=0)
        row_gains = lax.all_gather(own, "atm", axis=0, tiled=True)
        other = swap(own, rows, cols)
        part = lax.dot_general(other, jac, (((1,), (1,)), ((), ())), precision=precise)
        part = spread(part, "atm").sum(axis=0)
        stacked = lax.all_gather(jnp.concatenate([other, part], axis=1), "grp", axis=0, tiled=True)
        col_gains = stacked[:, :width]
        curvature = stacked[:, width:]
        innovation = 0.5 * (curvature + curvature.T) + forget_rate * identity
        factor = jnp.linalg.cholesky(innovation)
        inverse = jax.scipy.linalg.cho_solve((factor, True), identity)
        coefficient = jnp.dot(inverse, mismatch, precision=precise)
        change = jnp.dot(coefficient[None, :], col_gains, precision=precise)
        change = spread(change.reshape(width // FEATURES, FEATURES), "atm")
        current = current + change.reshape(FEATURES, FEATURES)
        scaled = jnp.dot(inverse, col_gains, precision=precise)
        downdate = lax.dot_general(row_gains, scaled, (((0,), (0,)), ((), ())), precision=precise)
        covar = (covar - downdate) / forget_rate
    return (covar, current)


def solution(mesh):
    return jax.shard_map(
        body,
        mesh=mesh,
        in_specs=(
            P(None, ("grp", "atm"), None),
            P(None, ("grp", "atm")),
            P(None, ("grp", "atm")),
            P(),
            P(),
            P(),
            P(),
            P("grp", "atm"),
        ),
        out_specs=(P("grp", "atm"), P()),
        check_vma=False,
    )
```

time: 799 us -> 322 us (0.40)
  waiting for transfers between devices: 495 us -> 22.9 us
  starting transfers between devices: 0.5 us -> 43.9 us
  matrix products: 55.2 us -> 36.1 us
  between operations: 15.4 us -> 1.03 us
    psum x4 -> x0, waiting for transfers between devices: 229 us -> none  [the longest x2 181 us: body(): row_gains = lax.psum(row_terms, 'atm')]
    reduce_scatter x2 -> x0, waiting for transfers between devices: 148 us -> none  [body(): lax.psum_scatter(partial_value, 'atm', scatter_dimension=1, tiled=True)]
    all_gather x2 -> x0, waiting for transfers between devices: 117 us -> none  [body(): full_gains = lax.all_gather(row_gains, 'grp', axis=0, tiled=True)]
    all_gather x2 -> x6, blocking collectives: 42.4 us -> 130 us  [the longest x2 48 us: body(): stacked = lax.all_gather(chunk, 'grp', axis=0, tiled=True)]
    psum x2 -> x0, blocking collectives: 66.5 us -> none  [body(): summed = lax.psum(energies, 'atm')]
    unnamed x2 -> x0, blocking collectives: 61.2 us -> none
    all_to_all x0 -> x6, starting transfers between devices: none -> 36.9 us  [exchange(): return lax.all_to_all(chunks, axis, 0, 0, tiled=True)]
    all_to_all x0 -> x2, blocking collectives: none -> 33.1 us  [exchange(): return lax.all_to_all(chunks, axis, 0, 0, tiled=True)]
  transfers between devices with their start and end apart: 8 -> 8, of which waited for: 8 -> 5; matrix products, arithmetic and copies ran while one was open for 1% -> 5% of each run, Pallas kernels for 0% -> 0%
where the time goes in v1:
time: 322 us; the launch traced here: 321 us
  blocking collectives  163 us (51%)
  other arithmetic  47.5 us (15%)
  starting transfers between devices  43.9 us (14%)
  matrix products  36.1 us (11%)
  waiting for transfers between devices  22.9 us (7%)
  local copies, waits for them, and re-layouts  6.83 us (2%)
    all_gather x2, blocking collectives, body(): stacked = lax.all_gather(chunk, 'grp', axis=0, tiled=True)  48 us
    all_gather x2, blocking collectives, body(): lax.all_gather(jnp.concatenate([other, part], axis=1), 'grp', axis=0, til...  43.4 us
    all_gather x2, blocking collectives, body(): row_gains = lax.all_gather(own, 'atm', axis=0, tiled=True)  38.5 us
    all_to_all x6, starting transfers between devices, exchange(): return lax.all_to_all(chunks, axis, 0, 0, tiled=True)  36.9 us
    all_to_all x2, blocking collectives, exchange(): return lax.all_to_all(chunks, axis, 0, 0, tiled=True)  33.1 us
    another operation x6, other arithmetic, body(): factor = jnp.linalg.cholesky(innovation)  24.8 us
    another operation x4, other arithmetic, body(): inverse = jax.scipy.linalg.cho_solve((factor, True), identity)  20.9 us
    all_to_all x6, waiting for transfers between devices, exchange(): return lax.all_to_all(chunks, axis, 0, 0, tiled=True)  19.3 us
  transfers between devices with their start and end apart: 8, of which 5 were waited for; matrix products, arithmetic and copies ran while one was open for 5% of the time, Pallas kernels for 0%

profile of v1, /device:TPU:1, one launch (start us, length us, event | category | flops | bytes accessed | tf_op | source)
XLA Modules:
  0.0 321.3 jit_solution(15444785724199431916)
XLA Ops:
  0.6 0.8 fusion.68
  1.4 0.8 fusion.67
  2.2 1.0 slice_bitcast_fusion.2
  3.6 1.3 multiply_reduce_fusion.1
  4.9 1.0 fusion.5
  6.5 18.6 %all_to_all.40 = f32[16,8,1152]{2,1,0:T(8,128)S(1)} all-to-all(f32[16,8,1152]{2,1,0:T(8,128)S(1)} %pad_maximum_fusion), channel_id=1, replica_groups=mesh['grp'=16,'atm'=16] {'atm'}, dimensions={0} | all-to-all | bytes 1179648 | tf_op jit(solution)/shard_map/all_to_all | solution.py:29
  25.2 23.4 %all_gather.18 = f32[128,1152]{1,0:T(8,128)S(1)} all-gather(f32[8,1152]{1,0:T(8,128)S(1)} %reduce_sum.73), channel_id=1, replica_groups=mesh['grp'=16,'atm'=16] {'grp'}, dimensions={0}, use_global_device_ids=true | all-gather | bytes 626688 | tf_op jit(solution)/shard_map/all_gather | solution.py:54
  48.6 7.3 %convolution_bitcast_fusion.1 = f32[16,8,1024]{2,1,0:T(8,128)} fusion(f32[1024,1024]{1,0:T(8,128)} %param.18, f32[128,1152]{1,0:T(8,128)S(1)} %all_gather.18), kind=kOutput, calls=%fused_computation.3 | convolution fusion | flops 1610612736 | bytes 5242880 | tf_op jit(solution)/shard_map/dot_general | solution.py:57
  56.0 3.7 %all-to-all-start.1 = ((f32[16,8,1024]{2,1,0:T(8,128)}), f32[16,8,1024]{2,1,0:T(8,128)S(1)}, u32[]{:S(2)}, u32[]{:S(2)}) async-start(f32[16,8,1024]{2,1,0:T(8,128)} %convolution_bitcast_fusion.1), calls=%async_computation.1 | async-start | bytes 1048576 | tf_op jit(solution)/shard_map/all_to_all | solution.py:29
  60.0 10.9 %all-to-all-done.1 = f32[16,8,1024]{2,1,0:T(8,128)S(1)} async-done(((f32[16,8,1024]{2,1,0:T(8,128)}), f32[16,8,1024]{2,1,0:T(8,128)S(1)}, u32[]{:S(2)}, u32[]{:S(2)}) %all-to-all-start.1) | async-done | bytes 524320 | tf_op jit(solution)/shard_map/all_to_all | solution.py:29
  70.9 3.3 %collective-permute-start = (f32[8,1024]{1,0:T(8,128)S(1)}, f32[8,1024]{1,0:T(8,128)S(1)}, u32[]{:S(2)}, u32[]{:S(2)}) collective-permute-start(f32[8,1024]{1,0:T(8,128)S(1)} %reduce_sum.74), channel_id=1, source_target_pairs={{0,0},{1,16},{2,32},{3,48},{4,64},{5,80},{6,96},{7,112},{8,128},{9... | collective-permute-start | bytes 98312 | tf_op jit(solution)/shard_map/ppermute | solution.py:38
  74.4 2.1 collective-permute-done
  77.0 0.7 broadcast_in_dim.14
  77.6 10.1 %all-to-all-start.2 = ((f32[16,8,128]{2,1,0:T(8,128)}), f32[16,8,128]{2,1,0:T(8,128)S(1)}, u32[]{:S(2)}, u32[]{:S(2)}) async-start(f32[16,8,128]{2,1,0:T(8,128)} %broadcast_in_dim.14), calls=%async_computation.2 | async-start | bytes 131072 | tf_op jit(solution)/shard_map/all_to_all | solution.py:29
  87.8 6.4 %all-to-all-done.2 = f32[16,8,128]{2,1,0:T(8,128)S(1)} async-done(((f32[16,8,128]{2,1,0:T(8,128)}), f32[16,8,128]{2,1,0:T(8,128)S(1)}, u32[]{:S(2)}, u32[]{:S(2)}) %all-to-all-start.2) | async-done | bytes 65568 | tf_op jit(solution)/shard_map/all_to_all | solution.py:29
  94.3 19.8 %all_gather.20 = f32[128,1152]{1,0:T(8,128)S(1)} all-gather(f32[8,1152]{1,0:T(8,128)S(1)} %pad_maximum_fusion.2), channel_id=1, replica_groups=mesh['grp'=16,'atm'=16] {'grp'}, dimensions={0}, use_global_device_ids=true | all-gather | bytes 626688 | tf_op jit(solution)/shard_map/all_gather | solution.py:63
  114.3 11.7 %cholesky.44 = f32[128,128]{1,0:T(8,128)S(1)} custom-call(f32[128,128]{1,0:T(8,128)S(1)} %fusion.51), custom_call_target="Cholesky" | custom-call | tf_op jit(solution)/shard_map/jit(cholesky)/cholesky | solution.py:67
  126.0 0.6 compare_reduce_fusion.1
  126.7 0.7 fusion.41
  127.3 9.8 %custom-call.8 = f32[1,128,128]{1,2,0:T(8,128)S(1)} custom-call(f32[1,128,128]{2,1,0:T(8,128)S(1)} %fusion.41), custom_call_target="InvertDiagBlocksLowerTriangular" | custom-call | tf_op jit(solution)/shard_map/jit(_cho_solve)/triangular_solve | solution.py:68
  138.3 0.6 broadcast_in_dim.15
  138.9 3.5 %all-to-all-start.3 = ((f32[16,8,128]{2,1,0:T(8,128)}), f32[16,8,128]{2,1,0:T(8,128)S(1)}, u32[]{:S(2)}, u32[]{:S(2)}) async-start(f32[16,8,128]{2,1,0:T(8,128)} %broadcast_in_dim.15), calls=%async_computation.3 | async-start | bytes 131072 | tf_op jit(solution)/shard_map/all_to_all | solution.py:29
  142.4 19.1 %all_gather.19 = f32[128,1024]{1,0:T(8,128)S(1)} all-gather(f32[8,1024]{1,0:T(8,128)S(1)} %reduce_sum.74), channel_id=1, replica_groups=mesh['grp'=16,'atm'=16] {'atm'}, dimensions={0}, use_global_device_ids=true | all-gather | bytes 557056 | tf_op jit(solution)/shard_map/all_gather | solution.py:59
  161.9 1.0 fusion.3
  163.5 0.9 pad_maximum_fusion.1
  164.3 4.5 %all-to-all-start.4 = ((f32[16,8,1152]{2,1,0:T(8,128)}), f32[16,8,1152]{2,1,0:T(8,128)S(1)}, u32[]{:S(2)}, u32[]{:S(2)}) async-start(f32[16,8,1152]{2,1,0:T(8,128)} %pad_maximum_fusion.1), calls=%async_computation.4 | async-start | bytes 1179648 | tf_op jit(solution)/shard_map/all_to_all | solution.py:29
  168.8 0.6 fusion.22
  169.4 6.7 %subtract_multiply_fusion.1 = f32[1024,1024]{1,0:T(8,128)} fusion(f32[1024,1024]{1,0:T(8,128)} %param.18, f32[128,1024]{1,0:T(8,128)S(1)} %all_gather.19, f32[128,1024]{1,0:T(8,128)S(1)} %fusion.22), kind=kOutput, calls=%fused_computation.1 | convolution fusion | flops 1612709888 | bytes 9437184 | tf_op jit(solution)/shard_map/dot_general | solution.py:74
  176.1 2.0 all-to-all-done.4
  178.2 24.6 %all_gather.21 = f32[128,1152]{1,0:T(8,128)S(1)} all-gather(f32[8,1152]{1,0:T(8,128)S(1)} %reduce_sum.77), channel_id=1, replica_groups=mesh['grp'=16,'atm'=16] {'grp'}, dimensions={0}, use_global_device_ids=true | all-gather | bytes 626688 | tf_op jit(solution)/shard_map/all_gather | solution.py:54
  202.8 6.6 %convolution_bitcast_fusion = f32[16,8,1024]{2,1,0:T(8,128)S(1)} fusion(f32[1024,1024]{1,0:T(8,128)} %subtract_multiply_fusion.1, f32[128,1152]{1,0:T(8,128)S(1)} %all_gather.21), kind=kOutput, calls=%fused_computation.2 | convolution fusion | flops 1610612736 | bytes 5242880 | tf_op jit(solution)/shard_map/dot_general | solution.py:57
  209.3 14.5 %all_to_all.41 = f32[16,8,1024]{2,1,0:T(8,128)S(1)} all-to-all(f32[16,8,1024]{2,1,0:T(8,128)S(1)} %convolution_bitcast_fusion), channel_id=1, replica_groups=mesh['grp'=16,'atm'=16] {'atm'}, dimensions={0} | all-to-all | bytes 1048576 | tf_op jit(solution)/shard_map/all_to_all | solution.py:29
  223.9 3.7 %collective-permute-start.1 = (f32[8,1024]{1,0:T(8,128)S(1)}, f32[8,1024]{1,0:T(8,128)S(1)}, u32[]{:S(2)}, u32[]{:S(2)}) collective-permute-start(f32[8,1024]{1,0:T(8,128)S(1)} %reduce_sum.78), channel_id=1, source_target_pairs={{0,0},{1,16},{2,32},{3,48},{4,64},{5,80},{6,96},{7,112},{8,128},{9... | collective-permute-start | bytes 98312 | tf_op jit(solution)/shard_map/ppermute | solution.py:38
  227.6 1.5 collective-permute-done.1
  229.1 0.5 fusion.19
  229.6 0.7 broadcast_in_dim.17
  230.3 10.5 %all-to-all-start.6 = ((f32[16,8,128]{2,1,0:T(8,128)}), f32[16,8,128]{2,1,0:T(8,128)S(1)}, u32[]{:S(2)}, u32[]{:S(2)}) async-start(f32[16,8,128]{2,1,0:T(8,128)} %broadcast_in_dim.17), calls=%async_computation.6 | async-start | bytes 131072 | tf_op jit(solution)/shard_map/all_to_all | solution.py:29
  240.8 19.4 %all_gather.22 = f32[128,1024]{1,0:T(8,128)S(1)} all-gather(f32[8,1024]{1,0:T(8,128)S(1)} %reduce_sum.78), channel_id=1, replica_groups=mesh['grp'=16,'atm'=16] {'atm'}, dimensions={0}, use_global_device_ids=true | all-gather | bytes 557056 | tf_op jit(solution)/shard_map/all_gather | solution.py:59
  260.2 23.6 %all_gather.23 = f32[128,1152]{1,0:T(8,128)S(1)} all-gather(f32[8,1152]{1,0:T(8,128)S(1)} %pad_maximum_fusion.3), channel_id=1, replica_groups=mesh['grp'=16,'atm'=16] {'grp'}, dimensions={0}, use_global_device_ids=true | all-gather | bytes 626688 | tf_op jit(solution)/shard_map/all_gather | solution.py:63
  284.1 11.7 %cholesky.55 = f32[128,128]{1,0:T(8,128)S(1)} custom-call(f32[128,128]{1,0:T(8,128)S(1)} %fusion.46), custom_call_target="Cholesky" | custom-call | tf_op jit(solution)/shard_map/jit(cholesky)/cholesky | solution.py:67
  295.8 0.6 compare_reduce_fusion
  296.5 0.7 fusion.42
  297.1 9.8 %custom-call.9 = f32[1,128,128]{1,2,0:T(8,128)S(1)} custom-call(f32[1,128,128]{2,1,0:T(8,128)S(1)} %fusion.42), custom_call_target="InvertDiagBlocksLowerTriangular" | custom-call | tf_op jit(solution)/shard_map/jit(_cho_solve)/triangular_solve | solution.py:68
  307.4 0.6 fusion.17
  308.6 0.6 broadcast_in_dim.18
  309.3 4.7 %all-to-all-start.7 = ((f32[16,8,128]{2,1,0:T(8,128)}), f32[16,8,128]{2,1,0:T(8,128)S(1)}, u32[]{:S(2)}, u32[]{:S(2)}) async-start(f32[16,8,128]{2,1,0:T(8,128)} %broadcast_in_dim.18), calls=%async_computation.7 | async-start | bytes 131072 | tf_op jit(solution)/shard_map/all_to_all | solution.py:29
  313.9 6.7 %subtract_multiply_fusion = f32[1024,1024]{1,0:T(8,128)} fusion(f32[1024,1024]{1,0:T(8,128)} %subtract_multiply_fusion.1, f32[128,1024]{1,0:T(8,128)S(1)} %all_gather.22, f32[128,1024]{1,0:T(8,128)S(1)} %fusion.17), kind=kOutput, calls=%fused_computation | convolution fusion | flops 1612709888 | bytes 9437184 | tf_op jit(solution)/shard_map/dot_general | solution.py:74
  320.7 0.6 bitcast_add_fusion
  (60 shorter events, 5.9 us)
Async XLA Ops:
  0.6 2.6 copy-start
  48.6 89.1 %copy-start.3 = (f32[2,128]{1,0:T(2,128)S(1)}, f32[2,128]{1,0:T(2,128)}, u32[]{:S(2)}) copy-start(f32[2,128]{1,0:T(2,128)} %param.14) | copy-start | bytes 3076
  55.9 105.5 %copy-start.1 = (f32[2,256,128]{2,1,0:T(8,128)S(1)}, f32[2,256,128]{2,1,0:T(8,128)}, u32[]{:S(2)}) copy-start(f32[2,256,128]{2,1,0:T(8,128)} %param.11) | copy-start | bytes 786436
  56.0 105.6 %copy-start.2 = (f32[128,128]{1,0:T(8,128)S(1)}, f32[128,128]{1,0:T(8,128)}, u32[]{:S(2)}) copy-start(f32[128,128]{1,0:T(8,128)} %param.15) | copy-start | bytes 196612
  56.0 105.6 %copy-start.4 = (f32[128]{0:T(128)S(1)}, f32[128]{0:T(128)}, u32[]{:S(2)}) copy-start(f32[128]{0:T(128)} %param.16) | copy-start | bytes 1540
  56.0 14.9 %all-to-all-start.1 = ((f32[16,8,1024]{2,1,0:T(8,128)}), f32[16,8,1024]{2,1,0:T(8,128)S(1)}, u32[]{:S(2)}, u32[]{:S(2)}) async-start(f32[16,8,1024]{2,1,0:T(8,128)} %convolution_bitcast_fusion.1), calls=%async_computation.1 | async-start | bytes 1048576 | tf_op jit(solution)/shard_map/all_to_all | solution.py:29
  70.9 5.6 %collective-permute-start = (f32[8,1024]{1,0:T(8,128)S(1)}, f32[8,1024]{1,0:T(8,128)S(1)}, u32[]{:S(2)}, u32[]{:S(2)}) collective-permute-start(f32[8,1024]{1,0:T(8,128)S(1)} %reduce_sum.74), channel_id=1, source_target_pairs={{0,0},{1,16},{2,32},{3,48},{4,64},{5,80},{6,96},{7,112},{8,128},{9... | collective-permute-start | bytes 98312 | tf_op jit(solution)/shard_map/ppermute | solution.py:38
  77.6 16.6 %all-to-all-start.2 = ((f32[16,8,128]{2,1,0:T(8,128)}), f32[16,8,128]{2,1,0:T(8,128)S(1)}, u32[]{:S(2)}, u32[]{:S(2)}) async-start(f32[16,8,128]{2,1,0:T(8,128)} %broadcast_in_dim.14), calls=%async_computation.2 | async-start | bytes 131072 | tf_op jit(solution)/shard_map/all_to_all | solution.py:29
  138.9 22.6 %all-to-all-start.3 = ((f32[16,8,128]{2,1,0:T(8,128)}), f32[16,8,128]{2,1,0:T(8,128)S(1)}, u32[]{:S(2)}, u32[]{:S(2)}) async-start(f32[16,8,128]{2,1,0:T(8,128)} %broadcast_in_dim.15), calls=%async_computation.3 | async-start | bytes 131072 | tf_op jit(solution)/shard_map/all_to_all | solution.py:29
  164.3 13.8 %all-to-all-start.4 = ((f32[16,8,1152]{2,1,0:T(8,128)}), f32[16,8,1152]{2,1,0:T(8,128)S(1)}, u32[]{:S(2)}, u32[]{:S(2)}) async-start(f32[16,8,1152]{2,1,0:T(8,128)} %pad_maximum_fusion.1), calls=%async_computation.4 | async-start | bytes 1179648 | tf_op jit(solution)/shard_map/all_to_all | solution.py:29
  223.9 5.2 %collective-permute-start.1 = (f32[8,1024]{1,0:T(8,128)S(1)}, f32[8,1024]{1,0:T(8,128)S(1)}, u32[]{:S(2)}, u32[]{:S(2)}) collective-permute-start(f32[8,1024]{1,0:T(8,128)S(1)} %reduce_sum.78), channel_id=1, source_target_pairs={{0,0},{1,16},{2,32},{3,48},{4,64},{5,80},{6,96},{7,112},{8,128},{9... | collective-permute-start | bytes 98312 | tf_op jit(solution)/shard_map/ppermute | solution.py:38
  230.3 29.9 %all-to-all-start.6 = ((f32[16,8,128]{2,1,0:T(8,128)}), f32[16,8,128]{2,1,0:T(8,128)S(1)}, u32[]{:S(2)}, u32[]{:S(2)}) async-start(f32[16,8,128]{2,1,0:T(8,128)} %broadcast_in_dim.17), calls=%async_computation.6 | async-start | bytes 131072 | tf_op jit(solution)/shard_map/all_to_all | solution.py:29
  309.3 11.4 %all-to-all-start.7 = ((f32[16,8,128]{2,1,0:T(8,128)}), f32[16,8,128]{2,1,0:T(8,128)S(1)}, u32[]{:S(2)}, u32[]{:S(2)}) async-start(f32[16,8,128]{2,1,0:T(8,128)} %broadcast_in_dim.18), calls=%async_computation.7 | async-start | bytes 131072 | tf_op jit(solution)/shard_map/all_to_all | solution.py:29

commit v2 on v1

v2 whole, which is shorter than its diff:
```python
import jax
import jax.numpy as jnp
from jax import lax
from jax.experimental import pallas as pl
from jax.experimental.pallas import tpu as pltpu
from jax.sharding import PartitionSpec as P

FEATURES = 128
GROUP_LOCAL = 8
STEPS = 2
SUB = 8

forget_rate = 0.98
precise = lax.Precision.HIGHEST
three = lax.Precision.HIGH


def dot(a, b, contract, precision):
    return lax.dot_general(
        a, b, ((contract[0], contract[1]), ((), ())), precision=precision, preferred_element_type=jnp.float32
    )


def block_inverse(p):
    m = len(p)
    if m == 1:
        return [[1.0 / p[0][0]]]
    if m == 2:
        a, b, d = p[0][0], p[0][1], p[1][1]
        r = 1.0 / (a * d - b * b)
        return [[d * r, -b * r], [-b * r, a * r]]
    h = m // 2
    top = [[p[i][j] for j in range(h)] for i in range(h)]
    side = [[p[i][h + j] for j in range(h)] for i in range(h)]
    ti = block_inverse(top)
    ts = [[sum(ti[i][k] * side[k][j] for k in range(h)) for j in range(h)] for i in range(h)]
    schur = [[None] * h for _ in range(h)]
    for i in range(h):
        for j in range(i, h):
            schur[i][j] = p[h + i][h + j] - sum(side[k][i] * ts[k][j] for k in range(h))
            schur[j][i] = schur[i][j]
    si = block_inverse(schur)
    tss = [[sum(ts[i][k] * si[k][j] for k in range(h)) for j in range(h)] for i in range(h)]
    out = [[None] * m for _ in range(m)]
    for i in range(h):
        for j in range(h):
            out[i][h + j] = -tss[i][j]
            out[h + j][i] = -tss[i][j]
            out[h + i][h + j] = si[i][j]
            if j >= i:
                out[i][j] = ti[i][j] + sum(tss[i][k] * ts[j][k] for k in range(h))
                out[j][i] = out[i][j]
    return out


def sweep_inverse(tiles):
    n = tiles[0].shape[1]
    full = (SUB, n)
    lane = lax.broadcasted_iota(jnp.int32, full, 1)
    sub = lax.broadcasted_iota(jnp.int32, full, 0)
    for t in range(n // SUB):
        k = t * SUB
        inside = (lane >= k) & (lane < k + SUB)
        rows = [jnp.broadcast_to(tiles[t][u : u + 1, :], full) for u in range(SUB)]
        cols = [[jnp.broadcast_to(x[:, k + u : k + u + 1], full) for u in range(SUB)] for x in tiles]
        piv = [[None] * SUB for _ in range(SUB)]
        for u in range(SUB):
            for v in range(u, SUB):
                piv[u][v] = jnp.broadcast_to(cols[t][v][u : u + 1, :], full)
                piv[v][u] = piv[u][v]
        inv = block_inverse(piv)
        rows = [jnp.where(inside, (lane == k + u).astype(jnp.float32), rows[u]) for u in range(SUB)]
        w = [sum(inv[u][v] * rows[v] for v in range(SUB)) for u in range(SUB)]
        new = []
        for i, x in enumerate(tiles):
            if i == t:
                y = w[0]
                for u in range(1, SUB):
                    y = jnp.where(sub == u, w[u], y)
            else:
                y = jnp.where(inside, 0.0, x)
                for u in range(SUB):
                    y = y - cols[i][u] * w[u]
            new.append(y)
        tiles = new
    return tiles


def update_kernel(stacked_ref, mismatch_ref, inverse_ref, change_ref):
    n = mismatch_ref.shape[0]
    width = stacked_ref.shape[1] - n
    curvature = stacked_ref[:, width:]
    row = lax.broadcasted_iota(jnp.int32, (n, n), 0)
    col = lax.broadcasted_iota(jnp.int32, (n, n), 1)
    innovation = 0.5 * (curvature + curvature.T) + jnp.where(row == col, forget_rate, 0.0)
    tiles = sweep_inverse([innovation[SUB * i : SUB * i + SUB] for i in range(n // SUB)])
    total = jnp.zeros((SUB, n), jnp.float32)
    for i, x in enumerate(tiles):
        inverse_ref[SUB * i : SUB * i + SUB, :] = x
        total = total + x * mismatch_ref[SUB * i : SUB * i + SUB, :]
    coefficient = jnp.broadcast_to(jnp.sum(total, axis=0, keepdims=True), (SUB, n))
    moved = jnp.dot(coefficient, stacked_ref[:, :width], precision=precise, preferred_element_type=jnp.float32)
    sub = lax.broadcasted_iota(jnp.int32, (SUB, FEATURES), 0)
    change = moved[:, :FEATURES]
    for r in range(1, width // FEATURES):
        change = jnp.where(sub == r, moved[:, r * FEATURES : (r + 1) * FEATURES], change)
    for j in range(change_ref.shape[0]):
        change_ref[j] = change


def solve_update(stacked, mismatch, copies):
    n = mismatch.shape[0]
    vmem = pl.BlockSpec(memory_space=pltpu.VMEM)
    return pl.pallas_call(
        update_kernel,
        out_shape=(
            jax.ShapeDtypeStruct((n, n), jnp.float32),
            jax.ShapeDtypeStruct((copies, SUB, FEATURES), jnp.float32),
        ),
        in_specs=[vmem, vmem],
        out_specs=(vmem, vmem),
        name="inverse_and_change",
    )(stacked, mismatch)


def exchange(chunks, axis):
    return lax.all_to_all(chunks, axis, 0, 0, tiled=True)


def spread(x, axis):
    return exchange(jnp.broadcast_to(x[None], (lax.axis_size(axis),) + x.shape), axis)


def swap(x, rows, cols):
    pairs = [(i * cols + j, j * cols + i) for i in range(rows) for j in range(cols)]
    return lax.ppermute(x, ("grp", "atm"), pairs)


def gather_rows(own):
    twice = jnp.concatenate([own, own], axis=0)
    got = lax.all_gather(twice, "atm", axis=0, tiled=False)
    return got[:, : own.shape[0]].reshape(-1, own.shape[1])


def vectors_of(kinds, readout):
    type_hot = (kinds[:, None] == jnp.arange(readout.shape[0])[None, :]).astype(jnp.float32)
    return jnp.dot(type_hot, readout, precision=precise)


def group_hot_of(member):
    return (jnp.arange(GROUP_LOCAL)[:, None] == member[None, :]).astype(jnp.float32)


def layer(atoms, weights, bias, vectors):
    hidden = jnp.tanh(jnp.dot(atoms, weights, precision=precise, preferred_element_type=jnp.float32) + bias)
    return hidden * vectors, (1.0 - hidden * hidden) * vectors


def first_chunk(atoms, kinds, member, weights, bias, readout, cols, width):
    energy, slope = layer(atoms, weights, bias, vectors_of(kinds, readout))
    group_hot = group_hot_of(member)
    energies = jnp.sum(dot(group_hot, energy, ((1,), (0,)), precise), axis=1)
    masked = atoms[:, None, :] * group_hot.T[:, :, None]
    grads = jnp.einsum("agi,ac->gic", masked, slope, precision=precise)
    parts = grads.reshape(GROUP_LOCAL, cols, width).transpose(1, 0, 2)
    extra = jnp.broadcast_to(energies[None, :, None], (cols, GROUP_LOCAL, FEATURES))
    return exchange(jnp.concatenate([parts, extra], axis=2), "atm").sum(axis=0)


def gather_atoms(atoms, kinds, member):
    pad = jnp.zeros((4, FEATURES), jnp.float32)
    extra = [x.astype(jnp.float32).reshape(-1, FEATURES) for x in (kinds, member)]
    got = lax.all_gather(jnp.concatenate([atoms, *extra, pad], axis=0), "atm", axis=0, tiled=False)
    local = atoms.shape[0]
    lines = local // FEATURES
    kinds = got[:, local : local + lines].reshape(-1)
    member = got[:, local + lines : local + 2 * lines].reshape(-1)
    return got[:, :local].reshape(-1, FEATURES), kinds, member


def later_terms(gathered, readout, col_index, width):
    atoms, kinds, member = gathered
    group_hot = group_hot_of(member)
    count = width // FEATURES
    part = lax.dynamic_slice_in_dim(atoms, col_index * count, count, 1).T
    masked = (group_hot[:, None, :] * part[None, :, :]).reshape(GROUP_LOCAL * count, -1)
    return atoms, vectors_of(kinds, readout), group_hot, masked


def later_chunk(terms, weights, bias, width):
    atoms, vectors, group_hot, masked = terms
    energy, slope = layer(atoms, weights, bias, vectors)
    energies = jnp.sum(dot(group_hot, energy, ((1,), (0,)), precise), axis=1, keepdims=True)
    grads = dot(masked, slope, ((1,), (0,)), precise).reshape(GROUP_LOCAL, width)
    return jnp.concatenate([grads, jnp.broadcast_to(energies, (GROUP_LOCAL, FEATURES))], axis=1)


def together(*values):
    return lax.optimization_barrier(values)


def body(atoms, kinds, member, targets, weights, bias, readout, covariance):
    rows, cols = lax.axis_size("grp"), lax.axis_size("atm")
    col_index = lax.axis_index("atm")
    group_total = GROUP_LOCAL * rows
    width = covariance.shape[1]
    current = weights
    gathered = gather_atoms(atoms[1], kinds[1], member[1])
    row_gains, scaled = [], []
    for step in range(STEPS):
        if step == 0:
            chunk = first_chunk(atoms[0], kinds[0], member[0], current, bias, readout, cols, width)
        else:
            chunk = later_chunk(later, current, bias, width)
        stacked = lax.all_gather(chunk, "grp", axis=0, tiled=True)
        jac = stacked[:, :width]
        mismatch = targets[step][:, None] - stacked[:, width:]
        terms = dot(jac, covariance, ((1,), (1,)), three)
        for gains, part in zip(row_gains, scaled):
            terms = (terms - dot(dot(jac, part, ((1,), (1,)), precise), gains, ((1,), (0,)), precise)) / forget_rate
        own = exchange(terms.reshape(cols, group_total // cols, width), "atm").sum(axis=0)
        if step == 0:
            own, *gathered = together(own, *gathered)
            later = later_terms(gathered, readout, col_index, width)
        row_gains.append(gather_rows(own))
        other = swap(own, rows, cols)
        part = dot(other, jac, ((1,), (1,)), precise)
        part = spread(part, "atm").sum(axis=0)
        if step == 0:
            part, *later = together(part, *later)
        stacked = lax.all_gather(jnp.concatenate([other, part], axis=1), "grp", axis=0, tiled=True)
        inverse, change = solve_update(stacked, mismatch, cols)
        current = current + exchange(change, "atm").reshape(FEATURES, FEATURES)
        scaled.append(dot(inverse, stacked[:, :width], ((1,), (0,)), precise))
    left = jnp.concatenate(row_gains, axis=0)
    right = jnp.concatenate([x / forget_rate ** (STEPS - i) for i, x in enumerate(scaled)], axis=0)
    covar = covariance / forget_rate**STEPS - dot(left, right, ((0,), (0,)), three)
    return (covar, current)


def solution(mesh):
    return jax.shard_map(
        body,
        mesh=mesh,
        in_specs=(
            P(None, ("grp", "atm"), None),
            P(None, ("grp", "atm")),
            P(None, ("grp", "atm")),
            P(),
            P(),
            P(),
            P(),
            P("grp", "atm"),
        ),
        out_specs=(P("grp", "atm"), P()),
        check_vma=False,
    )
```

time: 322 us -> 273 us (0.85)
  blocking collectives: 163 us -> 100 us
  other arithmetic: 47.5 us -> 7.77 us
  Pallas kernels: 0 us -> 18.3 us
  waiting for transfers between devices: 22.9 us -> 40.5 us
  between operations: 1.03 us -> 14.1 us
  local copies, waits for them, and re-layouts: 6.83 us -> 12.3 us
    another operation x10 -> x0, other arithmetic: 45.7 us -> none  [the longest x6 24.8 us: body(): factor = jnp.linalg.cholesky(innovation)]
    all_gather x2 -> x0, blocking collectives: 38.5 us -> none  [body(): row_gains = lax.all_gather(own, 'atm', axis=0, tiled=True)]
    all_to_all x6, waiting for transfers between devices: 19.3 us -> 39.5 us  [exchange(): return lax.all_to_all(chunks, axis, 0, 0, tiled=True)]
    all_to_all x2 -> x1, blocking collectives: 33.1 us -> 13.9 us  [exchange(): return lax.all_to_all(chunks, axis, 0, 0, tiled=True)]
    pallas_call x0 -> x2, Pallas kernels: none -> 18.3 us  [solve_update(): pl.pallas_call(update_kernel, out_shape=(jax.ShapeDtypeStruct((n, n), jnp...]
    all_gather x2, blocking collectives: 48 us -> 43.8 us  [body(): stacked = lax.all_gather(chunk, 'grp', axis=0, tiled=True)]
    transpose x0 -> x2, local copies, waits for them, and re-layouts: none -> 4.08 us  [later_terms(): part = lax.dynamic_slice_in_dim(atoms, col_index * count, count, 1).T]
    dot_general x20 -> x17, matrix products: 35.2 us -> 35.9 us  [the longest x12 28.4 us: dot(): lax.dot_general(a, b, ((contract[0], contract[1]), ((), ())), precision=p...]
  transfers between devices with their start and end apart: 8 -> 11, of which waited for: 5 -> 7; matrix products, arithmetic and copies ran while one was open for 5% -> 13% of each run, Pallas kernels for 0% -> 7%
where the time goes in v2:
time: 273 us; the launch traced here: 271 us
  blocking collectives  100 us (37%)
  starting transfers between devices  42.6 us (16%)
  waiting for transfers between devices  40.5 us (15%)
  matrix products  35.9 us (13%)
  Pallas kernels  18.3 us (7%)
  between operations  14.1 us (5%)
  local copies, waits for them, and re-layouts  12.3 us (5%)
  other arithmetic  7.77 us (3%)
    all_gather x2, blocking collectives, body(): stacked = lax.all_gather(chunk, 'grp', axis=0, tiled=True)  43.8 us
    all_gather x2, blocking collectives, body(): lax.all_gather(jnp.concatenate([other, part], axis=1), 'grp', axis=0, til...  42.3 us
    all_to_all x6, waiting for transfers between devices, exchange(): return lax.all_to_all(chunks, axis, 0, 0, tiled=True)  39.5 us
    all_to_all x6, starting transfers between devices, exchange(): return lax.all_to_all(chunks, axis, 0, 0, tiled=True)  35.5 us
    dot_general x12, matrix products, dot(): lax.dot_general(a, b, ((contract[0], contract[1]), ((), ())), precision=p...  28.4 us
    pallas_call x2, Pallas kernels, solve_update(): pl.pallas_call(update_kernel, out_shape=(jax.ShapeDtypeStruct((n, n), jnp...  18.3 us
    all_to_all x1, blocking collectives, exchange(): return lax.all_to_all(chunks, axis, 0, 0, tiled=True)  13.9 us
    ppermute x2, starting transfers between devices, swap(): return lax.ppermute(x, ('grp', 'atm'), pairs)  7 us
  transfers between devices with their start and end apart: 11, of which 7 were waited for; matrix products, arithmetic and copies ran while one was open for 13% of the time, Pallas kernels for 7%

profile of v2, /device:TPU:1, one launch (start us, length us, event | category | flops | bytes accessed | tf_op | source)
XLA Modules:
  0.0 271.5 jit_solution(8442478247470936630)
XLA Ops:
  7.2 0.8 slice_convert_fusion.1
  8.0 0.8 slice_convert_fusion
  8.7 1.0 slice_bitcast_fusion.2
  9.8 0.8 maximum_maximum_fusion
  11.0 1.2 fusion.9
  12.2 1.0 fusion.20
  14.0 0.9 pad_maximum_fusion
  14.8 7.6 %all-to-all-start = ((f32[16,8,1152]{2,1,0:T(8,128)}), f32[16,8,1152]{2,1,0:T(8,128)S(1)}, u32[]{:S(2)}, u32[]{:S(2)}) async-start(f32[16,8,1152]{2,1,0:T(8,128)} %pad_maximum_fusion), calls=%async_computation | async-start | bytes 1179648 | tf_op jit(solution)/shard_map/all_to_all | solution.py:127
  22.4 11.1 %all-to-all-done = f32[16,8,1152]{2,1,0:T(8,128)S(1)} async-done(((f32[16,8,1152]{2,1,0:T(8,128)}), f32[16,8,1152]{2,1,0:T(8,128)S(1)}, u32[]{:S(2)}, u32[]{:S(2)}) %all-to-all-start) | async-done | bytes 589856 | tf_op jit(solution)/shard_map/all_to_all | solution.py:127
  33.6 24.9 %all_gather.30 = f32[128,1152]{1,0:T(8,128)S(1)} all-gather(f32[8,1152]{1,0:T(8,128)S(1)} %reduce_sum.64), channel_id=1, replica_groups=mesh['grp'=16,'atm'=16] {'grp'}, dimensions={0}, use_global_device_ids=true | all-gather | bytes 626688 | tf_op jit(solution)/shard_map/all_gather | solution.py:215
  58.5 5.3 %convolution_bitcast_fusion = f32[16,8,1024]{2,1,0:T(8,128)} fusion(f32[1024,1024]{1,0:T(8,128)} %param.15, f32[128,1152]{1,0:T(8,128)S(1)} %all_gather.30), kind=kOutput, calls=%fused_computation.14 | convolution fusion | flops 805306368 | bytes 5242880 | tf_op jit(solution)/shard_map/dot_general | solution.py:19
  63.8 3.6 %all-to-all-start.1 = ((f32[16,8,1024]{2,1,0:T(8,128)}), f32[16,8,1024]{2,1,0:T(8,128)S(1)}, u32[]{:S(2)}, u32[]{:S(2)}) async-start(f32[16,8,1024]{2,1,0:T(8,128)} %convolution_bitcast_fusion), calls=%async_computation.1 | async-start | bytes 1048576 | tf_op jit(solution)/shard_map/all_to_all | solution.py:127
  67.4 0.7 slice_subtract_fusion.1.mismatch_ref
  68.1 10.4 %all-to-all-done.1 = f32[16,8,1024]{2,1,0:T(8,128)S(1)} async-done(((f32[16,8,1024]{2,1,0:T(8,128)}), f32[16,8,1024]{2,1,0:T(8,128)S(1)}, u32[]{:S(2)}, u32[]{:S(2)}) %all-to-all-start.1) | async-done | bytes 524320 | tf_op jit(solution)/shard_map/all_to_all | solution.py:127
  78.6 0.9 fusion.53
  79.5 1.7 slice.77
  81.3 3.3 %collective-permute-start = (f32[8,1024]{1,0:T(8,128)S(1)}, f32[8,1024]{1,0:T(8,128)S(1)}, u32[]{:S(2)}, u32[]{:S(2)}) collective-permute-start(f32[8,1024]{1,0:T(8,128)S(1)} %reduce_sum.65), channel_id=1, source_target_pairs={{0,0},{1,16},{2,32},{3,48},{4,64},{5,80},{6,96},{7,112},{8,128},{9... | collective-permute-start | bytes 98312 | tf_op jit(solution)/shard_map/ppermute | solution.py:136
  85.3 1.9 dynamic-slice_bitcast_fusion
  87.2 2.2 copy.17
  89.5 1.1 multiply_bitcast_fusion
  91.7 6.6 %all-to-all-start.2 = ((f32[16,8,128]{2,1,0:T(8,128)}), f32[16,8,128]{2,1,0:T(8,128)S(1)}, u32[]{:S(2)}, u32[]{:S(2)}) async-start(f32[16,8,128]{2,1,0:T(8,128)} %broadcast_in_dim.12), calls=%async_computation.2 | async-start | bytes 131072 | tf_op jit(solution)/shard_map/all_to_all | solution.py:127
  98.3 3.2 %fusion.43 = f32[4096,128]{1,0:T(8,128)} fusion(f32[4,128]{1,0:T(4,128)S(1)} %copy-done, f32[4096]{0:T(1024)S(1)} %bitcast.67, f32[4]{0:T(128)S(1)} %iota_convert_fusion.1), kind=kOutput, calls=%fused_computation.66 | convolution fusion | flops 25182208 | bytes 2115600 | tf_op jit(solution)/shard_map/dot_general | solution.py:147
  101.5 3.3 %all-to-all-done.2 = f32[16,8,128]{2,1,0:T(8,128)S(1)} async-done(((f32[16,8,128]{2,1,0:T(8,128)}), f32[16,8,128]{2,1,0:T(8,128)S(1)}, u32[]{:S(2)}, u32[]{:S(2)}) %all-to-all-start.2) | async-done | bytes 65568 | tf_op jit(solution)/shard_map/all_to_all | solution.py:127
  104.8 21.1 %all_gather.35.stacked_ref = f32[128,1152]{1,0:T(8,128)} all-gather(f32[8,1152]{1,0:T(8,128)S(1)} %pad_maximum_fusion.3), channel_id=1, replica_groups=mesh['grp'=16,'atm'=16] {'grp'}, dimensions={0}, use_global_device_ids=true | all-gather | bytes 626688 | tf_op jit(solution)/shard_map/all_gather | solution.py:231
  125.9 9.2 %inverse_and_change.2 = (f32[128,128]{1,0:T(8,128)}, f32[16,8,128]{2,1,0:T(8,128)}) custom-call(f32[128,1152]{1,0:T(8,128)} %all_gather.35.stacked_ref, f32[128,128]{1,0:T(8,128)} %slice_subtract_fusion.1.mismatch_ref), custom_call_target="tpu_custom_call" | custom-call | tf_op jit(solution)/shard_map/inverse_and_change/pallas_call | solution.py:114
  135.1 3.5 %all-to-all-start.3 = ((f32[16,8,128]{2,1,0:T(8,128)}), f32[16,8,128]{2,1,0:T(8,128)S(1)}, u32[]{:S(2)}, u32[]{:S(2)}) async-start(f32[16,8,128]{2,1,0:T(8,128)} %get-tuple-element.22), calls=%async_computation.3 | async-start | bytes 131072 | tf_op jit(solution)/shard_map/all_to_all | solution.py:127
  138.7 2.6 broadcast_multiply_fusion
  141.3 3.8 %all-to-all-done.3 = f32[16,8,128]{2,1,0:T(8,128)S(1)} async-done(((f32[16,8,128]{2,1,0:T(8,128)}), f32[16,8,128]{2,1,0:T(8,128)S(1)}, u32[]{:S(2)}, u32[]{:S(2)}) %all-to-all-start.3) | async-done | bytes 65568 | tf_op jit(solution)/shard_map/all_to_all | solution.py:127
  145.1 1.8 fusion
  146.9 1.3 copy-done.3
  148.2 1.6 fusion.3
  149.9 3.0 %fusion.10 = f32[8]{0:T(128)S(1)} fusion(f32[8,4096]{1,0:T(8,128)S(1)} %compare_convert_fusion, f32[4096,128]{1,0:T(8,128)} %copy-done.3, f32[4096,128]{1,0:T(8,128)S(1)} %copy-done.2), kind=kOutput, calls=%fused_computation.17 | convolution fusion | flops 50856952 | bytes 4325408 | tf_op jit(solution)/shard_map/dot_general | solution.py:19
  152.9 18.9 %all_gather.36 = f32[128,1152]{1,0:T(8,128)S(1)} all-gather(f32[8,1152]{1,0:T(8,128)S(1)} %pad_maximum_fusion.4), channel_id=1, replica_groups=mesh['grp'=16,'atm'=16] {'grp'}, dimensions={0}, use_global_device_ids=true | all-gather | bytes 626688 | tf_op jit(solution)/shard_map/all_gather | solution.py:215
  172.5 1.6 fusion.52
  174.1 4.4 %fusion.8 = f32[16,8,1024]{2,1,0:T(8,128)S(1)} fusion(f32[128,1024]{1,0:T(8,128)S(1)} %fusion.52, f32[1024,1024]{1,0:T(8,128)} %param.15, f32[128,1152]{1,0:T(8,128)S(1)} %all_gather.36), kind=kOutput, calls=%fused_computation.12 | convolution fusion | flops 805568512 | bytes 5767168 | tf_op jit(solution)/shard_map/dot_general | solution.py:19
  178.5 13.9 %all_to_all.35 = f32[16,8,1024]{2,1,0:T(8,128)S(1)} all-to-all(f32[16,8,1024]{2,1,0:T(8,128)S(1)} %fusion.8), channel_id=1, replica_groups=mesh['grp'=16,'atm'=16] {'atm'}, dimensions={0} | all-to-all | bytes 1048576 | tf_op jit(solution)/shard_map/all_to_all | solution.py:127
  193.1 3.7 %collective-permute-start.1 = (f32[8,1024]{1,0:T(8,128)S(1)}, f32[8,1024]{1,0:T(8,128)S(1)}, u32[]{:S(2)}, u32[]{:S(2)}) collective-permute-start(f32[8,1024]{1,0:T(8,128)S(1)} %reduce_sum.68), channel_id=1, source_target_pairs={{0,0},{1,16},{2,32},{3,48},{4,64},{5,80},{6,96},{7,112},{8,128},{9... | collective-permute-start | bytes 98312 | tf_op jit(solution)/shard_map/ppermute | solution.py:136
  196.8 0.7 slice_subtract_fusion.mismatch_ref
  197.5 0.9 collective-permute-done.1
  199.6 10.5 %all-to-all-start.5 = ((f32[16,8,128]{2,1,0:T(8,128)}), f32[16,8,128]{2,1,0:T(8,128)S(1)}, u32[]{:S(2)}, u32[]{:S(2)}) async-start(f32[16,8,128]{2,1,0:T(8,128)} %broadcast_in_dim.14), calls=%async_computation.5 | async-start | bytes 131072 | tf_op jit(solution)/shard_map/all_to_all | solution.py:127
  210.1 6.4 %all-to-all-done.5 = f32[16,8,128]{2,1,0:T(8,128)S(1)} async-done(((f32[16,8,128]{2,1,0:T(8,128)}), f32[16,8,128]{2,1,0:T(8,128)S(1)}, u32[]{:S(2)}, u32[]{:S(2)}) %all-to-all-start.5) | async-done | bytes 65568 | tf_op jit(solution)/shard_map/all_to_all | solution.py:127
  216.6 21.1 %all_gather.39.stacked_ref = f32[128,1152]{1,0:T(8,128)} all-gather(f32[8,1152]{1,0:T(8,128)S(1)} %pad_maximum_fusion.5), channel_id=1, replica_groups=mesh['grp'=16,'atm'=16] {'grp'}, dimensions={0}, use_global_device_ids=true | all-gather | bytes 626688 | tf_op jit(solution)/shard_map/all_gather | solution.py:231
  237.7 9.2 %inverse_and_change.3 = (f32[128,128]{1,0:T(8,128)}, f32[16,8,128]{2,1,0:T(8,128)}) custom-call(f32[128,1152]{1,0:T(8,128)} %all_gather.39.stacked_ref, f32[128,128]{1,0:T(8,128)} %slice_subtract_fusion.mismatch_ref), custom_call_target="tpu_custom_call" | custom-call | tf_op jit(solution)/shard_map/inverse_and_change/pallas_call | solution.py:114
  246.9 3.8 %all-to-all-start.6 = ((f32[16,8,128]{2,1,0:T(8,128)}), f32[16,8,128]{2,1,0:T(8,128)S(1)}, u32[]{:S(2)}, u32[]{:S(2)}) async-start(f32[16,8,128]{2,1,0:T(8,128)} %get-tuple-element.27), calls=%async_computation.6 | async-start | bytes 131072 | tf_op jit(solution)/shard_map/all_to_all | solution.py:127
  250.7 1.7 convolution_multiply_fusion
  252.3 4.5 %all-to-all-done.6 = f32[16,8,128]{2,1,0:T(8,128)S(1)} async-done(((f32[16,8,128]{2,1,0:T(8,128)}), f32[16,8,128]{2,1,0:T(8,128)S(1)}, u32[]{:S(2)}, u32[]{:S(2)}) %all-to-all-start.6) | async-done | bytes 65568 | tf_op jit(solution)/shard_map/all_to_all | solution.py:127
  257.5 1.1 slice_bitcast_fusion
  258.6 6.4 %multiply_subtract_fusion = f32[1024,1024]{1,0:T(8,128)} fusion(f32[1024,1024]{1,0:T(8,128)} %param.15, f32[128,1024]{1,0:T(8,128)S(1)} %slice_bitcast_fusion, f32[128,1024]{1,0:T(8,128)S(1)} %slice_bitcast_fusion.1, f32[128,1024]{1,0:T(8,128)S(1)} %convolution_multiply_fusion, f32[128,1024]{1,0:T(8,128)S(1)} %copy-done.5), kind=kOutput, calls=%fused_computation.2 | convolution fusion | flops 1613234176 | bytes 10485760 | tf_op jit(solution)/shard_map/dot_general | solution.py:19
  (63 shorter events, 6.6 us)
Async XLA Ops:
  7.2 3.6 %copy-start = (f32[4,128]{1,0:T(4,128)S(1)}, f32[4,128]{1,0:T(4,128)}, u32[]{:S(2)}) copy-start(f32[4,128]{1,0:T(4,128)} %param.14) | copy-start | bytes 6148
  7.2 71.4 %all-gather.7.cloned.1.call-start = ((), (), s32[]{:S(2)}) async-start(), calls=%async_computation.7 | async-start | bytes 2297856 | tf_op jit(solution)/shard_map/all_gather | solution.py:173
  14.8 18.7 %all-to-all-start = ((f32[16,8,1152]{2,1,0:T(8,128)}), f32[16,8,1152]{2,1,0:T(8,128)S(1)}, u32[]{:S(2)}, u32[]{:S(2)}) async-start(f32[16,8,1152]{2,1,0:T(8,128)} %pad_maximum_fusion), calls=%async_computation | async-start | bytes 1179648 | tf_op jit(solution)/shard_map/all_to_all | solution.py:127
  58.5 8.9 %copy-start.10 = (f32[2,128]{1,0:T(2,128)S(1)}, f32[2,128]{1,0:T(2,128)}, u32[]{:S(2)}) copy-start(f32[2,128]{1,0:T(2,128)} %param.11) | copy-start | bytes 3076
  63.8 14.8 %all-to-all-start.1 = ((f32[16,8,1024]{2,1,0:T(8,128)}), f32[16,8,1024]{2,1,0:T(8,128)S(1)}, u32[]{:S(2)}, u32[]{:S(2)}) async-start(f32[16,8,1024]{2,1,0:T(8,128)} %convolution_bitcast_fusion), calls=%async_computation.1 | async-start | bytes 1048576 | tf_op jit(solution)/shard_map/all_to_all | solution.py:127
  67.3 105.1 %all-gather.9.cloned.1.call-start = ((), (), s32[]{:S(2)}) async-start(), calls=%async_computation.8 | async-start | bytes 1114112 | tf_op jit(solution)/shard_map/all_gather | solution.py:141
  81.3 9.2 %collective-permute-start = (f32[8,1024]{1,0:T(8,128)S(1)}, f32[8,1024]{1,0:T(8,128)S(1)}, u32[]{:S(2)}, u32[]{:S(2)}) collective-permute-start(f32[8,1024]{1,0:T(8,128)S(1)} %reduce_sum.65), channel_id=1, source_target_pairs={{0,0},{1,16},{2,32},{3,48},{4,64},{5,80},{6,96},{7,112},{8,128},{9... | collective-permute-start | bytes 98312 | tf_op jit(solution)/shard_map/ppermute | solution.py:136
  91.7 13.1 %all-to-all-start.2 = ((f32[16,8,128]{2,1,0:T(8,128)}), f32[16,8,128]{2,1,0:T(8,128)S(1)}, u32[]{:S(2)}, u32[]{:S(2)}) async-start(f32[16,8,128]{2,1,0:T(8,128)} %broadcast_in_dim.12), calls=%async_computation.2 | async-start | bytes 131072 | tf_op jit(solution)/shard_map/all_to_all | solution.py:127
  101.5 43.6 %copy-start.8 = (f32[128,128]{1,0:T(8,128)S(1)}, f32[128,128]{1,0:T(8,128)}, u32[]{:S(2)}) copy-start(f32[128,128]{1,0:T(8,128)} %param.12) | copy-start | bytes 196612
  101.5 43.6 %copy-start.9 = (f32[128]{0:T(128)S(1)}, f32[128]{0:T(128)}, u32[]{:S(2)}) copy-start(f32[128]{0:T(128)} %param.13) | copy-start | bytes 1540
  135.1 10.0 %all-to-all-start.3 = ((f32[16,8,128]{2,1,0:T(8,128)}), f32[16,8,128]{2,1,0:T(8,128)S(1)}, u32[]{:S(2)}, u32[]{:S(2)}) async-start(f32[16,8,128]{2,1,0:T(8,128)} %get-tuple-element.22), calls=%async_computation.3 | async-start | bytes 131072 | tf_op jit(solution)/shard_map/all_to_all | solution.py:127
  138.6 118.9 %all-gather.11.cloned.1.call-start = ((), (), s32[]{:S(2)}) async-start(), calls=%async_computation.9 | async-start | bytes 1114112 | tf_op jit(solution)/shard_map/all_gather | solution.py:141
  141.3 6.9 %copy-start.4 = (f32[64,4096]{1,0:T(8,128)S(1)}, f32[64,4096]{1,0:T(8,128)}, u32[]{:S(2)}) copy-start(f32[64,4096]{1,0:T(8,128)} %multiply_bitcast_fusion) | copy-start | bytes 3145732
  145.1 3.1 %copy-start.1 = (f32[4096,128]{1,0:T(8,128)S(1)}, f32[4096,128]{1,0:T(8,128)}, u32[]{:S(2)}) copy-start(f32[4096,128]{1,0:T(8,128)} %fusion.43) | copy-start | bytes 6291460
  146.9 1.3 copy-start.3
  148.2 1.7 copy-start.2
  149.9 22.0 %copy-start.6 = (f32[128,1024]{1,0:T(8,128)S(1)}, f32[128,1024]{1,0:T(8,128)}, u32[]{:S(2)}) copy-start(f32[128,1024]{1,0:T(8,128)} %get-tuple-element.39) | copy-start | bytes 1572868
  178.5 31.5 %copy-start.7 = (f32[256,1024]{1,0:T(8,128)S(1)}, f32[256,1024]{1,0:T(8,128)}, u32[]{:S(2)}) copy-start(f32[256,1024]{1,0:T(8,128)} %all-gather.9.cloned.1.call-done) | copy-start | bytes 3145732
  193.1 5.2 %collective-permute-start.1 = (f32[8,1024]{1,0:T(8,128)S(1)}, f32[8,1024]{1,0:T(8,128)S(1)}, u32[]{:S(2)}, u32[]{:S(2)}) collective-permute-start(f32[8,1024]{1,0:T(8,128)S(1)} %reduce_sum.68), channel_id=1, source_target_pairs={{0,0},{1,16},{2,32},{3,48},{4,64},{5,80},{6,96},{7,112},{8,128},{9... | collective-permute-start | bytes 98312 | tf_op jit(solution)/shard_map/ppermute | solution.py:136
  199.6 17.0 %all-to-all-start.5 = ((f32[16,8,128]{2,1,0:T(8,128)}), f32[16,8,128]{2,1,0:T(8,128)S(1)}, u32[]{:S(2)}, u32[]{:S(2)}) async-start(f32[16,8,128]{2,1,0:T(8,128)} %broadcast_in_dim.14), calls=%async_computation.5 | async-start | bytes 131072 | tf_op jit(solution)/shard_map/all_to_all | solution.py:127
  210.1 48.5 %copy-start.5 = (f32[128,1024]{1,0:T(8,128)S(1)}, f32[128,1024]{1,0:T(8,128)}, u32[]{:S(2)}) copy-start(f32[128,1024]{1,0:T(8,128)} %get-tuple-element.38) | copy-start | bytes 1572868
  246.9 10.0 %all-to-all-start.6 = ((f32[16,8,128]{2,1,0:T(8,128)}), f32[16,8,128]{2,1,0:T(8,128)S(1)}, u32[]{:S(2)}, u32[]{:S(2)}) async-start(f32[16,8,128]{2,1,0:T(8,128)} %get-tuple-element.27), calls=%async_computation.6 | async-start | bytes 131072 | tf_op jit(solution)/shard_map/all_to_all | solution.py:127
Sparse Core Ops, SparseCore 0:
  10.7 55.6 all-gather.6
  89.5 43.0 all-gather.8
  193.3 41.2 all-gather.10

commit v3 on v2

--- a/solution.py
+++ b/solution.py
@@ -1,3 +1,6 @@
+import functools
+import math
+
 import jax
 import jax.numpy as jnp
 from jax import lax
@@ -53,53 +56,55 @@
     return out
 
 
+def total(values):
+    values = list(values)
+    while len(values) > 1:
+        values = [values[i] + values[i + 1] if i + 1 < len(values) else values[i] for i in range(0, len(values), 2)]
+    return values[0]
+
+
 def sweep_inverse(tiles):
     n = tiles[0].shape[1]
     full = (SUB, n)
-    lane = lax.broadcasted_iota(jnp.int32, full, 1)
-    sub = lax.broadcasted_iota(jnp.int32, full, 0)
+    lane = lax.broadcasted_iota(jnp.int32, (1, n), 1)
+    sub = lax.broadcasted_iota(jnp.int32, (SUB, 1), 0)
     for t in range(n // SUB):
         k = t * SUB
         inside = (lane >= k) & (lane < k + SUB)
-        rows = [jnp.broadcast_to(tiles[t][u : u + 1, :], full) for u in range(SUB)]
+        rows = [tiles[t][u : u + 1, :] for u in range(SUB)]
         cols = [[jnp.broadcast_to(x[:, k + u : k + u + 1], full) for u in range(SUB)] for x in tiles]
-        piv = [[None] * SUB for _ in range(SUB)]
-        for u in range(SUB):
-            for v in range(u, SUB):
-                piv[u][v] = jnp.broadcast_to(cols[t][v][u : u + 1, :], full)
-                piv[v][u] = piv[u][v]
+        piv = [[cols[t][v][u : u + 1, :] for v in range(SUB)] for u in range(SUB)]
         inv = block_inverse(piv)
         rows = [jnp.where(inside, (lane == k + u).astype(jnp.float32), rows[u]) for u in range(SUB)]
-        w = [sum(inv[u][v] * rows[v] for v in range(SUB)) for u in range(SUB)]
+        w = [total(inv[u][v] * rows[v] for v in range(SUB)) for u in range(SUB)]
         new = []
         for i, x in enumerate(tiles):
             if i == t:
-                y = w[0]
+                y = jnp.broadcast_to(w[0], full)
                 for u in range(1, SUB):
                     y = jnp.where(sub == u, w[u], y)
             else:
-                y = jnp.where(inside, 0.0, x)
-                for u in range(SUB):
-                    y = y - cols[i][u] * w[u]
+                y = jnp.where(inside, 0.0, x) - total(cols[i][u] * w[u] for u in range(SUB))
             new.append(y)
         tiles = new
     return tiles
 
 
-def update_kernel(stacked_ref, mismatch_ref, inverse_ref, change_ref):
+def update_kernel(order, stacked_ref, mismatch_ref, inverse_ref, change_ref):
     n = mismatch_ref.shape[0]
     width = stacked_ref.shape[1] - n
-    curvature = stacked_ref[:, width:]
+    places = [order.index(t) * SUB for t in range(n // SUB)]
+    curvature = jnp.concatenate([stacked_ref[p : p + SUB, width:] for p in places], axis=0)
     row = lax.broadcasted_iota(jnp.int32, (n, n), 0)
     col = lax.broadcasted_iota(jnp.int32, (n, n), 1)
     innovation = 0.5 * (curvature + curvature.T) + jnp.where(row == col, forget_rate, 0.0)
     tiles = sweep_inverse([innovation[SUB * i : SUB * i + SUB] for i in range(n // SUB)])
-    total = jnp.zeros((SUB, n), jnp.float32)
-    for i, x in enumerate(tiles):
-        inverse_ref[SUB * i : SUB * i + SUB, :] = x
-        total = total + x * mismatch_ref[SUB * i : SUB * i + SUB, :]
-    coefficient = jnp.broadcast_to(jnp.sum(total, axis=0, keepdims=True), (SUB, n))
-    moved = jnp.dot(coefficient, stacked_ref[:, :width], precision=precise, preferred_element_type=jnp.float32)
+    for p, x in zip(places, tiles):
+        inverse_ref[p : p + SUB, :] = x
+    weighted = total(x * mismatch_ref[SUB * i : SUB * i + SUB, :] for i, x in enumerate(tiles))
+    coefficient = jnp.broadcast_to(jnp.sum(weighted, axis=0, keepdims=True), (SUB, n))
+    gains = jnp.concatenate([stacked_ref[p : p + SUB, :width] for p in places], axis=0)
+    moved = jnp.dot(coefficient, gains, precision=precise, preferred_element_type=jnp.float32)
     sub = lax.broadcasted_iota(jnp.int32, (SUB, FEATURES), 0)
     change = moved[:, :FEATURES]
     for r in range(1, width // FEATURES):
@@ -108,17 +113,18 @@
         change_ref[j] = change
 
 
-def solve_update(stacked, mismatch, copies):
+def solve_update(stacked, mismatch, copies, order):
     n = mismatch.shape[0]
     vmem = pl.BlockSpec(memory_space=pltpu.VMEM)
     return pl.pallas_call(
-        update_kernel,
+        functools.partial(update_kernel, order),
         out_shape=(
             jax.ShapeDtypeStruct((n, n), jnp.float32),
             jax.ShapeDtypeStruct((copies, SUB, FEATURES), jnp.float32),
         ),
         in_specs=[vmem, vmem],
         out_specs=(vmem, vmem),
+        compiler_params=pltpu.CompilerParams(vmem_limit_bytes=8 * 1024 * 1024),
         name="inverse_and_change",
     )(stacked, mismatch)
 
@@ -131,8 +137,13 @@
     return exchange(jnp.broadcast_to(x[None], (lax.axis_size(axis),) + x.shape), axis)
 
 
-def swap(x, rows, cols):
-    pairs = [(i * cols + j, j * cols + i) for i in range(rows) for j in range(cols)]
+def far_row(j, side):
+    return (j // side + side // 2) % side * side + (j % side + side // 2) % side
+
+
+def swap(x, order):
+    size = len(order)
+    pairs = [(i * size + order[a], a * size + i) for i in range(size) for a in range(size)]
     return lax.ppermute(x, ("grp", "atm"), pairs)
 
 
@@ -204,6 +215,7 @@
     col_index = lax.axis_index("atm")
     group_total = GROUP_LOCAL * rows
     width = covariance.shape[1]
+    order = [far_row(a, math.isqrt(rows)) for a in range(rows)]
     current = weights
     gathered = gather_atoms(atoms[1], kinds[1], member[1])
     row_gains, scaled = [], []
@@ -223,15 +235,17 @@
             own, *gathered = together(own, *gathered)
             later = later_terms(gathered, readout, col_index, width)
         row_gains.append(gather_rows(own))
-        other = swap(own, rows, cols)
+        other = swap(own, order)
         part = dot(other, jac, ((1,), (1,)), precise)
         part = spread(part, "atm").sum(axis=0)
         if step == 0:
             part, *later = together(part, *later)
         stacked = lax.all_gather(jnp.concatenate([other, part], axis=1), "grp", axis=0, tiled=True)
-        inverse, change = solve_update(stacked, mismatch, cols)
+        inverse, change = solve_update(stacked, mismatch, cols, order)
+        if step == STEPS - 1:
+            change, *row_gains = together(change, *row_gains)
         current = current + exchange(change, "atm").reshape(FEATURES, FEATURES)
-        scaled.append(dot(inverse, stacked[:, :width], ((1,), (0,)), precise))
+        scaled.append(dot(inverse, stacked[:, :width], ((0,), (0,)), precise))
     left = jnp.concatenate(row_gains, axis=0)
     right = jnp.concatenate([x / forget_rate ** (STEPS - i) for i, x in enumerate(scaled)], axis=0)
     covar = covariance / forget_rate**STEPS - dot(left, right, ((0,), (0,)), three)

time: 273 us -> 253 us (0.927)
  starting transfers between devices: 42.6 us -> 32.8 us
  blocking collectives: 100 us -> 96.7 us
  Pallas kernels: 18.3 us -> 15.2 us
    all_to_all x6, starting transfers between devices: 35.5 us -> 26.9 us  [exchange(): return lax.all_to_all(chunks, axis, 0, 0, tiled=True)]
    all_gather x2, blocking collectives: 42.3 us -> 39 us  [body(): lax.all_gather(jnp.concatenate([other, part], axis=1), 'grp', axis=0, til...]
    pallas_call x2, Pallas kernels: 18.3 us -> 15.2 us  [solve_update(): pl.pallas_call(functools.partial(update_kernel, order), out_shape=(jax.Sh...]
    ppermute x2, waiting for transfers between devices: 0.88 us -> 3.98 us  [swap(): return lax.ppermute(x, ('grp', 'atm'), pairs)]
    all_to_all x6, waiting for transfers between devices: 39.5 us -> 36.8 us  [exchange(): return lax.all_to_all(chunks, axis, 0, 0, tiled=True)]
  transfers between devices with their start and end apart: 11 -> 11, of which waited for: 7 -> 7; matrix products, arithmetic and copies ran while one was open for 13% -> 15% of each run, Pallas kernels for 7% -> 6%
where the time goes in v3:
time: 253 us; the launch traced here: 252 us
  blocking collectives  96.7 us (38%)
  waiting for transfers between devices  40.9 us (16%)
  matrix products  33.8 us (13%)
  starting transfers between devices  32.8 us (13%)
  Pallas kernels  15.2 us (6%)
  between operations  14.1 us (6%)
  local copies, waits for them, and re-layouts  12.3 us (5%)
  other arithmetic  6.53 us (3%)
    all_gather x2, blocking collectives, body(): stacked = lax.all_gather(chunk, 'grp', axis=0, tiled=True)  43.8 us
    all_gather x2, blocking collectives, body(): lax.all_gather(jnp.concatenate([other, part], axis=1), 'grp', axis=0, til...  39 us
    all_to_all x6, waiting for transfers between devices, exchange(): return lax.all_to_all(chunks, axis, 0, 0, tiled=True)  36.8 us
    all_to_all x6, starting transfers between devices, exchange(): return lax.all_to_all(chunks, axis, 0, 0, tiled=True)  26.9 us
    dot_general x12, matrix products, dot(): lax.dot_general(a, b, ((contract[0], contract[1]), ((), ())), precision=p...  26.3 us
    pallas_call x2, Pallas kernels, solve_update(): pl.pallas_call(functools.partial(update_kernel, order), out_shape=(jax.Sh...  15.2 us
    all_to_all x1, blocking collectives, exchange(): return lax.all_to_all(chunks, axis, 0, 0, tiled=True)  13.9 us
    ppermute x2, starting transfers between devices, swap(): return lax.ppermute(x, ('grp', 'atm'), pairs)  5.84 us
  transfers between devices with their start and end apart: 11, of which 7 were waited for; matrix products, arithmetic and copies ran while one was open for 15% of the time, Pallas kernels for 6%

profile of v3, /device:TPU:1, one launch (start us, length us, event | category | flops | bytes accessed | tf_op | source)
XLA Modules:
  0.0 252.3 jit_solution(14040042120741650516)
XLA Ops:
  7.2 0.8 slice_convert_fusion.1
  8.0 0.8 slice_convert_fusion
  8.7 1.0 slice_bitcast_fusion.2
  9.8 0.8 maximum_maximum_fusion
  11.0 1.2 fusion.9
  12.2 1.0 fusion.20
  14.0 0.9 pad_maximum_fusion
  14.8 7.6 %all-to-all-start = ((f32[16,8,1152]{2,1,0:T(8,128)}), f32[16,8,1152]{2,1,0:T(8,128)S(1)}, u32[]{:S(2)}, u32[]{:S(2)}) async-start(f32[16,8,1152]{2,1,0:T(8,128)} %pad_maximum_fusion), calls=%async_computation | async-start | bytes 1179648 | tf_op jit(solution)/shard_map/all_to_all | solution.py:133
  22.4 11.1 %all-to-all-done = f32[16,8,1152]{2,1,0:T(8,128)S(1)} async-done(((f32[16,8,1152]{2,1,0:T(8,128)}), f32[16,8,1152]{2,1,0:T(8,128)S(1)}, u32[]{:S(2)}, u32[]{:S(2)}) %all-to-all-start) | async-done | bytes 589856 | tf_op jit(solution)/shard_map/all_to_all | solution.py:133
  33.6 24.9 %all_gather.30 = f32[128,1152]{1,0:T(8,128)S(1)} all-gather(f32[8,1152]{1,0:T(8,128)S(1)} %reduce_sum.64), channel_id=1, replica_groups=mesh['grp'=16,'atm'=16] {'grp'}, dimensions={0}, use_global_device_ids=true | all-gather | bytes 626688 | tf_op jit(solution)/shard_map/all_gather | solution.py:227
  58.5 5.3 %convolution_bitcast_fusion = f32[16,8,1024]{2,1,0:T(8,128)} fusion(f32[1024,1024]{1,0:T(8,128)} %param.15, f32[128,1152]{1,0:T(8,128)S(1)} %all_gather.30), kind=kOutput, calls=%fused_computation.14 | convolution fusion | flops 805306368 | bytes 5242880 | tf_op jit(solution)/shard_map/dot_general | solution.py:22
  63.8 3.6 %all-to-all-start.1 = ((f32[16,8,1024]{2,1,0:T(8,128)}), f32[16,8,1024]{2,1,0:T(8,128)S(1)}, u32[]{:S(2)}, u32[]{:S(2)}) async-start(f32[16,8,1024]{2,1,0:T(8,128)} %convolution_bitcast_fusion), calls=%async_computation.1 | async-start | bytes 1048576 | tf_op jit(solution)/shard_map/all_to_all | solution.py:133
  67.5 11.0 %all-to-all-done.1 = f32[16,8,1024]{2,1,0:T(8,128)S(1)} async-done(((f32[16,8,1024]{2,1,0:T(8,128)}), f32[16,8,1024]{2,1,0:T(8,128)S(1)}, u32[]{:S(2)}, u32[]{:S(2)}) %all-to-all-start.1) | async-done | bytes 524320 | tf_op jit(solution)/shard_map/all_to_all | solution.py:133
  78.6 0.9 fusion.53
  79.5 1.7 slice.77
  81.3 2.5 %collective-permute-start = (f32[8,1024]{1,0:T(8,128)S(1)}, f32[8,1024]{1,0:T(8,128)S(1)}, u32[]{:S(2)}, u32[]{:S(2)}) collective-permute-start(f32[8,1024]{1,0:T(8,128)S(1)} %reduce_sum.65), channel_id=1, source_target_pairs={{10,0},{11,16},{8,32},{9,48},{14,64},{15,80},{12,96},{13,112},{2,1... | collective-permute-start | bytes 98312 | tf_op jit(solution)/shard_map/ppermute | solution.py:147
  83.8 0.6 pad_maximum_fusion.1
  84.5 1.9 dynamic-slice_bitcast_fusion
  86.4 2.2 copy.17
  88.7 1.1 multiply_bitcast_fusion
  90.2 0.7 broadcast_in_dim.12
  90.9 4.6 %all-to-all-start.2 = ((f32[16,8,128]{2,1,0:T(8,128)}), f32[16,8,128]{2,1,0:T(8,128)S(1)}, u32[]{:S(2)}, u32[]{:S(2)}) async-start(f32[16,8,128]{2,1,0:T(8,128)} %broadcast_in_dim.12), calls=%async_computation.2 | async-start | bytes 131072 | tf_op jit(solution)/shard_map/all_to_all | solution.py:133
  95.4 3.2 %fusion.43 = f32[4096,128]{1,0:T(8,128)} fusion(f32[4,128]{1,0:T(4,128)S(1)} %copy-done, f32[4096]{0:T(1024)S(1)} %bitcast.67, f32[4]{0:T(128)S(1)} %iota_convert_fusion.1), kind=kOutput, calls=%fused_computation.66 | convolution fusion | flops 25182208 | bytes 2115600 | tf_op jit(solution)/shard_map/dot_general | solution.py:158
  98.6 3.3 %all-to-all-done.2 = f32[16,8,128]{2,1,0:T(8,128)S(1)} async-done(((f32[16,8,128]{2,1,0:T(8,128)}), f32[16,8,128]{2,1,0:T(8,128)S(1)}, u32[]{:S(2)}, u32[]{:S(2)}) %all-to-all-start.2) | async-done | bytes 65568 | tf_op jit(solution)/shard_map/all_to_all | solution.py:133
  102.0 18.7 %all_gather.33.stacked_ref = f32[128,1152]{1,0:T(8,128)S(1)} all-gather(f32[8,1152]{1,0:T(8,128)S(1)} %pad_maximum_fusion.3), channel_id=1, replica_groups=mesh['grp'=16,'atm'=16] {'grp'}, dimensions={0}, use_global_device_ids=true | all-gather | bytes 626688 | tf_op jit(solution)/shard_map/all_gather | solution.py:243
  120.7 7.6 %inverse_and_change.2 = (f32[128,128]{1,0:T(8,128)S(1)}, f32[16,8,128]{2,1,0:T(8,128)}) custom-call(f32[128,1152]{1,0:T(8,128)S(1)} %all_gather.33.stacked_ref, f32[128,128]{1,0:T(8,128)S(1)} %slice_subtract_fusion.1.mismatch_ref), custom_call_target="tpu_custom_call" | custom-call | tf_op jit(solution)/shard_map/inverse_and_change/pallas_call | solution.py:119
  128.3 3.5 %all-to-all-start.3 = ((f32[16,8,128]{2,1,0:T(8,128)}), f32[16,8,128]{2,1,0:T(8,128)S(1)}, u32[]{:S(2)}, u32[]{:S(2)}) async-start(f32[16,8,128]{2,1,0:T(8,128)} %get-tuple-element.25), calls=%async_computation.3 | async-start | bytes 131072 | tf_op jit(solution)/shard_map/all_to_all | solution.py:133
  131.8 1.6 broadcast_multiply_fusion
  133.4 4.8 %all-to-all-done.3 = f32[16,8,128]{2,1,0:T(8,128)S(1)} async-done(((f32[16,8,128]{2,1,0:T(8,128)}), f32[16,8,128]{2,1,0:T(8,128)S(1)}, u32[]{:S(2)}, u32[]{:S(2)}) %all-to-all-start.3) | async-done | bytes 65568 | tf_op jit(solution)/shard_map/all_to_all | solution.py:133
  138.2 1.8 fusion
  140.1 1.3 copy-done.3
  141.4 1.6 fusion.3
  143.0 3.0 %fusion.10 = f32[8]{0:T(128)S(1)} fusion(f32[8,4096]{1,0:T(8,128)S(1)} %compare_convert_fusion, f32[4096,128]{1,0:T(8,128)} %copy-done.3, f32[4096,128]{1,0:T(8,128)S(1)} %copy-done.2), kind=kOutput, calls=%fused_computation.17 | convolution fusion | flops 50856952 | bytes 4325408 | tf_op jit(solution)/shard_map/dot_general | solution.py:22
  146.1 18.9 %all_gather.34 = f32[128,1152]{1,0:T(8,128)S(1)} all-gather(f32[8,1152]{1,0:T(8,128)S(1)} %pad_maximum_fusion.4), channel_id=1, replica_groups=mesh['grp'=16,'atm'=16] {'grp'}, dimensions={0}, use_global_device_ids=true | all-gather | bytes 626688 | tf_op jit(solution)/shard_map/all_gather | solution.py:227
  165.6 1.6 fusion.52
  167.3 4.4 %fusion.8 = f32[16,8,1024]{2,1,0:T(8,128)S(1)} fusion(f32[128,1024]{1,0:T(8,128)S(1)} %fusion.52, f32[1024,1024]{1,0:T(8,128)} %param.15, f32[128,1152]{1,0:T(8,128)S(1)} %all_gather.34), kind=kOutput, calls=%fused_computation.12 | convolution fusion | flops 805568512 | bytes 5767168 | tf_op jit(solution)/shard_map/dot_general | solution.py:22
  171.7 13.9 %all_to_all.35 = f32[16,8,1024]{2,1,0:T(8,128)S(1)} all-to-all(f32[16,8,1024]{2,1,0:T(8,128)S(1)} %fusion.8), channel_id=1, replica_groups=mesh['grp'=16,'atm'=16] {'atm'}, dimensions={0} | all-to-all | bytes 1048576 | tf_op jit(solution)/shard_map/all_to_all | solution.py:133
  186.3 3.3 %collective-permute-start.1 = (f32[8,1024]{1,0:T(8,128)S(1)}, f32[8,1024]{1,0:T(8,128)S(1)}, u32[]{:S(2)}, u32[]{:S(2)}) collective-permute-start(f32[8,1024]{1,0:T(8,128)S(1)} %reduce_sum.68), channel_id=1, source_target_pairs={{10,0},{11,16},{8,32},{9,48},{14,64},{15,80},{12,96},{13,112},{2,1... | collective-permute-start | bytes 98312 | tf_op jit(solution)/shard_map/ppermute | solution.py:147
  189.7 4.0 %collective-permute-done.1 = f32[8,1024]{1,0:T(8,128)S(1)} collective-permute-done((f32[8,1024]{1,0:T(8,128)S(1)}, f32[8,1024]{1,0:T(8,128)S(1)}, u32[]{:S(2)}, u32[]{:S(2)}) %collective-permute-start.1) | collective-permute-done | bytes 32800 | tf_op jit(solution)/shard_map/ppermute | solution.py:147
  194.2 0.7 broadcast_in_dim.14
  194.8 4.1 %all-to-all-start.5 = ((f32[16,8,128]{2,1,0:T(8,128)}), f32[16,8,128]{2,1,0:T(8,128)S(1)}, u32[]{:S(2)}, u32[]{:S(2)}) async-start(f32[16,8,128]{2,1,0:T(8,128)} %broadcast_in_dim.14), calls=%async_computation.5 | async-start | bytes 131072 | tf_op jit(solution)/shard_map/all_to_all | solution.py:133
  199.0 6.4 %all-to-all-done.5 = f32[16,8,128]{2,1,0:T(8,128)S(1)} async-done(((f32[16,8,128]{2,1,0:T(8,128)}), f32[16,8,128]{2,1,0:T(8,128)S(1)}, u32[]{:S(2)}, u32[]{:S(2)}) %all-to-all-start.5) | async-done | bytes 65568 | tf_op jit(solution)/shard_map/all_to_all | solution.py:133
  205.5 20.3 %all_gather.37.stacked_ref = f32[128,1152]{1,0:T(8,128)S(1)} all-gather(f32[8,1152]{1,0:T(8,128)S(1)} %pad_maximum_fusion.5), channel_id=1, replica_groups=mesh['grp'=16,'atm'=16] {'grp'}, dimensions={0}, use_global_device_ids=true | all-gather | bytes 626688 | tf_op jit(solution)/shard_map/all_gather | solution.py:243
  225.8 7.6 %inverse_and_change.3 = (f32[128,128]{1,0:T(8,128)S(1)}, f32[16,8,128]{2,1,0:T(8,128)}) custom-call(f32[128,1152]{1,0:T(8,128)S(1)} %all_gather.37.stacked_ref, f32[128,128]{1,0:T(8,128)S(1)} %slice_subtract_fusion.mismatch_ref), custom_call_target="tpu_custom_call" | custom-call | tf_op jit(solution)/shard_map/inverse_and_change/pallas_call | solution.py:119
  234.1 1.1 slice_bitcast_fusion
  235.2 3.5 %all-to-all-start.6 = ((f32[16,8,128]{2,1,0:T(8,128)}), f32[16,8,128]{2,1,0:T(8,128)S(1)}, u32[]{:S(2)}, u32[]{:S(2)}) async-start(f32[16,8,128]{2,1,0:T(8,128)} %get-tuple-element.33), calls=%async_computation.6 | async-start | bytes 131072 | tf_op jit(solution)/shard_map/all_to_all | solution.py:133
  238.7 6.4 %multiply_subtract_fusion = f32[1024,1024]{1,0:T(8,128)} fusion(f32[1024,1024]{1,0:T(8,128)} %param.15, f32[128,1024]{1,0:T(8,128)S(1)} %slice_bitcast_fusion, f32[128,1024]{1,0:T(8,128)S(1)} %slice_bitcast_fusion.1, f32[128,1024]{1,0:T(8,128)S(1)} %convolution_multiply_fusion, f32[128,1024]{1,0:T(8,128)S(1)} %copy-done.5), kind=kOutput, calls=%fused_computation.2 | convolution fusion | flops 1613234176 | bytes 10485760 | tf_op jit(solution)/shard_map/dot_general | solution.py:22
  245.1 0.6 bitcast_add_fusion
  (63 shorter events, 4.9 us)
Async XLA Ops:
  7.2 3.6 %copy-start = (f32[4,128]{1,0:T(4,128)S(1)}, f32[4,128]{1,0:T(4,128)}, u32[]{:S(2)}) copy-start(f32[4,128]{1,0:T(4,128)} %param.14) | copy-start | bytes 6148
  7.2 71.4 %all-gather.7.cloned.1.call-start = ((), (), s32[]{:S(2)}) async-start(), calls=%async_computation.7 | async-start | bytes 2297856 | tf_op jit(solution)/shard_map/all_gather | solution.py:184
  14.8 18.7 %all-to-all-start = ((f32[16,8,1152]{2,1,0:T(8,128)}), f32[16,8,1152]{2,1,0:T(8,128)S(1)}, u32[]{:S(2)}, u32[]{:S(2)}) async-start(f32[16,8,1152]{2,1,0:T(8,128)} %pad_maximum_fusion), calls=%async_computation | async-start | bytes 1179648 | tf_op jit(solution)/shard_map/all_to_all | solution.py:133
  58.5 8.9 %copy-start.10 = (f32[2,128]{1,0:T(2,128)S(1)}, f32[2,128]{1,0:T(2,128)}, u32[]{:S(2)}) copy-start(f32[2,128]{1,0:T(2,128)} %param.11) | copy-start | bytes 3076
  63.8 14.8 %all-to-all-start.1 = ((f32[16,8,1024]{2,1,0:T(8,128)}), f32[16,8,1024]{2,1,0:T(8,128)S(1)}, u32[]{:S(2)}, u32[]{:S(2)}) async-start(f32[16,8,1024]{2,1,0:T(8,128)} %convolution_bitcast_fusion), calls=%async_computation.1 | async-start | bytes 1048576 | tf_op jit(solution)/shard_map/all_to_all | solution.py:133
  67.3 98.3 %all-gather.9.cloned.1.call-start = ((), (), s32[]{:S(2)}) async-start(), calls=%async_computation.8 | async-start | bytes 1114112 | tf_op jit(solution)/shard_map/all_gather | solution.py:152
  81.3 8.4 %collective-permute-start = (f32[8,1024]{1,0:T(8,128)S(1)}, f32[8,1024]{1,0:T(8,128)S(1)}, u32[]{:S(2)}, u32[]{:S(2)}) collective-permute-start(f32[8,1024]{1,0:T(8,128)S(1)} %reduce_sum.65), channel_id=1, source_target_pairs={{10,0},{11,16},{8,32},{9,48},{14,64},{15,80},{12,96},{13,112},{2,1... | collective-permute-start | bytes 98312 | tf_op jit(solution)/shard_map/ppermute | solution.py:147
  90.9 11.1 %all-to-all-start.2 = ((f32[16,8,128]{2,1,0:T(8,128)}), f32[16,8,128]{2,1,0:T(8,128)S(1)}, u32[]{:S(2)}, u32[]{:S(2)}) async-start(f32[16,8,128]{2,1,0:T(8,128)} %broadcast_in_dim.12), calls=%async_computation.2 | async-start | bytes 131072 | tf_op jit(solution)/shard_map/all_to_all | solution.py:133
  98.6 39.6 %copy-start.8 = (f32[128,128]{1,0:T(8,128)S(1)}, f32[128,128]{1,0:T(8,128)}, u32[]{:S(2)}) copy-start(f32[128,128]{1,0:T(8,128)} %param.12) | copy-start | bytes 196612
  98.6 39.6 %copy-start.9 = (f32[128]{0:T(128)S(1)}, f32[128]{0:T(128)}, u32[]{:S(2)}) copy-start(f32[128]{0:T(128)} %param.13) | copy-start | bytes 1540
  128.3 10.0 %all-to-all-start.3 = ((f32[16,8,128]{2,1,0:T(8,128)}), f32[16,8,128]{2,1,0:T(8,128)S(1)}, u32[]{:S(2)}, u32[]{:S(2)}) async-start(f32[16,8,128]{2,1,0:T(8,128)} %get-tuple-element.25), calls=%async_computation.3 | async-start | bytes 131072 | tf_op jit(solution)/shard_map/all_to_all | solution.py:133
  131.8 102.3 %all-gather.11.cloned.1.call-start = ((), (), s32[]{:S(2)}) async-start(), calls=%async_computation.9 | async-start | bytes 1114112 | tf_op jit(solution)/shard_map/all_gather | solution.py:152
  133.4 7.9 %copy-start.4 = (f32[64,4096]{1,0:T(8,128)S(1)}, f32[64,4096]{1,0:T(8,128)}, u32[]{:S(2)}) copy-start(f32[64,4096]{1,0:T(8,128)} %multiply_bitcast_fusion) | copy-start | bytes 3145732
  138.2 3.1 %copy-start.1 = (f32[4096,128]{1,0:T(8,128)S(1)}, f32[4096,128]{1,0:T(8,128)}, u32[]{:S(2)}) copy-start(f32[4096,128]{1,0:T(8,128)} %fusion.43) | copy-start | bytes 6291460
  140.0 1.3 copy-start.3
  141.4 1.7 copy-start.2
  143.0 22.0 %copy-start.6 = (f32[128,1024]{1,0:T(8,128)S(1)}, f32[128,1024]{1,0:T(8,128)}, u32[]{:S(2)}) copy-start(f32[128,1024]{1,0:T(8,128)} %get-tuple-element.45) | copy-start | bytes 1572868
  171.7 27.3 %copy-start.7 = (f32[256,1024]{1,0:T(8,128)S(1)}, f32[256,1024]{1,0:T(8,128)}, u32[]{:S(2)}) copy-start(f32[256,1024]{1,0:T(8,128)} %all-gather.9.cloned.1.call-done) | copy-start | bytes 3145732
  186.3 7.4 %collective-permute-start.1 = (f32[8,1024]{1,0:T(8,128)S(1)}, f32[8,1024]{1,0:T(8,128)S(1)}, u32[]{:S(2)}, u32[]{:S(2)}) collective-permute-start(f32[8,1024]{1,0:T(8,128)S(1)} %reduce_sum.68), channel_id=1, source_target_pairs={{10,0},{11,16},{8,32},{9,48},{14,64},{15,80},{12,96},{13,112},{2,1... | collective-permute-start | bytes 98312 | tf_op jit(solution)/shard_map/ppermute | solution.py:147
  194.8 10.7 %all-to-all-start.5 = ((f32[16,8,128]{2,1,0:T(8,128)}), f32[16,8,128]{2,1,0:T(8,128)S(1)}, u32[]{:S(2)}, u32[]{:S(2)}) async-start(f32[16,8,128]{2,1,0:T(8,128)} %broadcast_in_dim.14), calls=%async_computation.5 | async-start | bytes 131072 | tf_op jit(solution)/shard_map/all_to_all | solution.py:133
  199.0 39.6 %copy-start.5 = (f32[128,1024]{1,0:T(8,128)S(1)}, f32[128,1024]{1,0:T(8,128)}, u32[]{:S(2)}) copy-start(f32[128,1024]{1,0:T(8,128)} %get-tuple-element.44) | copy-start | bytes 1572868
  235.2 10.0 %all-to-all-start.6 = ((f32[16,8,128]{2,1,0:T(8,128)}), f32[16,8,128]{2,1,0:T(8,128)S(1)}, u32[]{:S(2)}, u32[]{:S(2)}) async-start(f32[16,8,128]{2,1,0:T(8,128)} %get-tuple-element.33), calls=%async_computation.6 | async-start | bytes 131072 | tf_op jit(solution)/shard_map/all_to_all | solution.py:133
Sparse Core Ops, SparseCore 0:
  10.7 55.6 all-gather.6
  88.7 44.0 all-gather.8
  186.4 42.1 all-gather.10

commit v4 on v3

v4 whole, which is shorter than its diff:
```python
import functools
import math

import jax
import jax.numpy as jnp
from jax import lax
from jax.experimental import pallas as pl
from jax.experimental.pallas import tpu as pltpu
from jax.sharding import PartitionSpec as P

FEATURES = 128
GROUP_LOCAL = 8
STEPS = 2
SUB = 8

forget_rate = 0.98
precise = lax.Precision.HIGHEST
three = lax.Precision.HIGH
MIB = 1024 * 1024


def dot(a, b, contract, precision):
    return lax.dot_general(
        a, b, ((contract[0], contract[1]), ((), ())), precision=precision, preferred_element_type=jnp.float32
    )


def block_inverse(p):
    m = len(p)
    if m == 1:
        return [[1.0 / p[0][0]]]
    if m == 2:
        a, b, d = p[0][0], p[0][1], p[1][1]
        r = 1.0 / (a * d - b * b)
        return [[d * r, -b * r], [-b * r, a * r]]
    h = m // 2
    top = [[p[i][j] for j in range(h)] for i in range(h)]
    side = [[p[i][h + j] for j in range(h)] for i in range(h)]
    ti = block_inverse(top)
    ts = [[sum(ti[i][k] * side[k][j] for k in range(h)) for j in range(h)] for i in range(h)]
    schur = [[None] * h for _ in range(h)]
    for i in range(h):
        for j in range(i, h):
            schur[i][j] = p[h + i][h + j] - sum(side[k][i] * ts[k][j] for k in range(h))
            schur[j][i] = schur[i][j]
    si = block_inverse(schur)
    tss = [[sum(ts[i][k] * si[k][j] for k in range(h)) for j in range(h)] for i in range(h)]
    out = [[None] * m for _ in range(m)]
    for i in range(h):
        for j in range(h):
            out[i][h + j] = -tss[i][j]
            out[h + j][i] = -tss[i][j]
            out[h + i][h + j] = si[i][j]
            if j >= i:
                out[i][j] = ti[i][j] + sum(tss[i][k] * ts[j][k] for k in range(h))
                out[j][i] = out[i][j]
    return out


def total(values):
    values = list(values)
    while len(values) > 1:
        values = [values[i] + values[i + 1] if i + 1 < len(values) else values[i] for i in range(0, len(values), 2)]
    return values[0]


def sweep_inverse(tiles):
    n = tiles[0].shape[1]
    full = (SUB, n)
    lane = lax.broadcasted_iota(jnp.int32, (1, n), 1)
    sub = lax.broadcasted_iota(jnp.int32, (SUB, 1), 0)
    for t in range(n // SUB):
        k = t * SUB
        inside = (lane >= k) & (lane < k + SUB)
        rows = [tiles[t][u : u + 1, :] for u in range(SUB)]
        cols = [[jnp.broadcast_to(x[:, k + u : k + u + 1], full) for u in range(SUB)] for x in tiles]
        piv = [[cols[t][v][u : u + 1, :] for v in range(SUB)] for u in range(SUB)]
        inv = block_inverse(piv)
        rows = [jnp.where(inside, (lane == k + u).astype(jnp.float32), rows[u]) for u in range(SUB)]
        w = [total(inv[u][v] * rows[v] for v in range(SUB)) for u in range(SUB)]
        new = []
        for i, x in enumerate(tiles):
            if i == t:
                y = jnp.broadcast_to(w[0], full)
                for u in range(1, SUB):
                    y = jnp.where(sub == u, w[u], y)
            else:
                y = jnp.where(inside, 0.0, x) - total(cols[i][u] * w[u] for u in range(SUB))
            new.append(y)
        tiles = new
    return tiles


def split(x):
    high = x.astype(jnp.bfloat16)
    return high, (x - high.astype(jnp.float32)).astype(jnp.bfloat16)


def dot3(a, b, contract=((1,), (0,))):
    a_high, a_low = split(a)
    b_high, b_low = split(b)

    def one(x, y):
        return lax.dot_general(x, y, (contract, ((), ())), preferred_element_type=jnp.float32)

    return one(a_high, b_high) + (one(a_high, b_low) + one(a_low, b_high))


def exact(a, b, contract=((1,), (0,))):
    return lax.dot_general(a, b, (contract, ((), ())), precision=precise, preferred_element_type=jnp.float32)


def whole():
    return pl.BlockSpec(memory_space=pltpu.VMEM)


def scalar():
    return pl.BlockSpec(memory_space=pltpu.SMEM)


def params(mib):
    return pltpu.CompilerParams(vmem_limit_bytes=int(mib * MIB))


def f32(*shape):
    return jax.ShapeDtypeStruct(shape, jnp.float32)


def hot(values, count):
    return (lax.broadcasted_iota(jnp.int32, (count, values.shape[1]), 0) == values).astype(jnp.float32)


def vectors_of(kinds, readout):
    extra = SUB - readout.shape[0]
    table = jnp.concatenate([readout, jnp.zeros((extra, readout.shape[1]), jnp.float32)], axis=0)
    return exact(hot(kinds, SUB), table, ((0,), (0,)))


def layer(atoms, weights, bias, vectors):
    hidden = jnp.tanh(dot3(atoms, weights) + bias)
    return hidden * vectors, (1.0 - hidden * hidden) * vectors


def first_kernel(atoms_ref, kinds_ref, member_ref, weights_ref, bias_ref, readout_ref, out_ref, turned, masked):
    atoms = atoms_ref[...]
    vectors = vectors_of(kinds_ref[0:1, :], readout_ref[...])
    energy, slope = layer(atoms, weights_ref[...], bias_ref[...], vectors)
    group_hot = hot(member_ref[0:1, :], GROUP_LOCAL)
    turned[...] = atoms.T
    for i in range(FEATURES):
        masked[SUB * i : SUB * i + SUB, :] = turned[i : i + 1, :] * group_hot
    grads = dot3(masked[...], slope)
    energies = jnp.sum(dot3(group_hot, energy), axis=1, keepdims=True)
    energies = jnp.broadcast_to(energies, (GROUP_LOCAL, FEATURES))
    blocks, _, wide = out_ref.shape
    per = FEATURES // blocks
    for j in range(blocks):
        for f in range(per):
            i = j * per + f
            out_ref[j, :, f * FEATURES : (f + 1) * FEATURES] = grads[SUB * i : SUB * i + SUB]
        out_ref[j, :, wide - FEATURES :] = energies


def first_terms(atoms, kinds, member, weights, bias, readout, cols, width):
    local = atoms.shape[1]
    return pl.pallas_call(
        first_kernel,
        grid=(1,),
        out_shape=f32(cols, GROUP_LOCAL, width + FEATURES),
        in_specs=[pl.BlockSpec((None, local, FEATURES), lambda n: (0, 0, 0))] + [whole()] * 5,
        out_specs=whole(),
        scratch_shapes=[pltpu.VMEM((FEATURES, local), jnp.float32), pltpu.VMEM((SUB * FEATURES, local), jnp.float32)],
        compiler_params=params(63.9),
        name="first_terms",
    )(atoms, kinds, member, weights, bias, readout)


def prepare_kernel(col_ref, gathered_ref, readout_ref, vectors_ref, masked_ref, turned):
    local = vectors_ref.shape[0]
    lines = local // FEATURES
    count = (masked_ref.shape[0] - GROUP_LOCAL) // GROUP_LOCAL

    def row(start):
        parts = [gathered_ref[start + u : start + u + 1, :] for u in range(lines)]
        return jnp.concatenate(parts, axis=1).astype(jnp.int32)

    vectors_ref[...] = vectors_of(row(local), readout_ref[...])
    group_hot = hot(row(local + lines), GROUP_LOCAL)
    turned[...] = gathered_ref[:local, :].T
    part = turned[pl.ds(pl.multiple_of(col_ref[0] * count, SUB), count), :]
    for f in range(count):
        masked_ref[SUB * f : SUB * f + SUB, :] = part[f : f + 1, :] * group_hot
    masked_ref[SUB * count :, :] = group_hot


def prepare(gathered, readout, col_index, local, count):
    cols, tall, _ = gathered.shape
    lines = GROUP_LOCAL * (count + 1)
    return pl.pallas_call(
        prepare_kernel,
        grid=(cols,),
        out_shape=(f32(cols * local, FEATURES), f32(lines, cols * local)),
        in_specs=[scalar(), pl.BlockSpec((None, tall, FEATURES), lambda n: (n, 0, 0)), whole()],
        out_specs=(pl.BlockSpec((local, FEATURES), lambda n: (n, 0)), pl.BlockSpec((lines, local), lambda n: (0, n))),
        scratch_shapes=[pltpu.VMEM((FEATURES, local), jnp.float32)],
        compiler_params=params(63),
        name="prepare_terms",
    )(col_index, gathered, readout)


def later_kernel(gathered_ref, vectors_ref, masked_ref, weights_ref, change_ref, bias_ref, out_ref, acc):
    step = pl.program_id(0)
    blocks = gathered_ref.shape[0]
    local = vectors_ref.shape[0] // blocks
    atoms = gathered_ref[:, :local, :].reshape(blocks * local, FEATURES)
    weights = weights_ref[...] + change_ref[...].reshape(FEATURES, FEATURES)
    energy, slope = layer(atoms, weights, bias_ref[...], vectors_ref[...])
    split_row = acc.shape[0] - GROUP_LOCAL
    grads = dot3(masked_ref[:split_row, :], slope)
    energies = dot3(masked_ref[split_row:, :], energy)

    @pl.when(step == 0)
    def _():
        acc[:split_row, :] = grads
        acc[split_row:, :] = energies

    @pl.when(step > 0)
    def _():
        acc[:split_row, :] += grads
        acc[split_row:, :] += energies

    @pl.when(step == pl.num_programs(0) - 1)
    def _():
        total_energy = jnp.sum(acc[split_row:, :], axis=1, keepdims=True)
        total_energy = jnp.broadcast_to(total_energy, (GROUP_LOCAL, FEATURES))
        for copy in range(out_ref.shape[0]):
            for f in range(split_row // SUB):
                out_ref[copy, :, f * FEATURES : (f + 1) * FEATURES] = acc[SUB * f : SUB * f + SUB, :]
            out_ref[copy, :, split_row // SUB * FEATURES :] = total_energy


def later_terms(gathered, vectors, masked, weights, change, bias, copies):
    cols, tall, _ = gathered.shape
    parts = 4
    local = vectors.shape[0] // cols
    lines = masked.shape[0]
    width = (lines // GROUP_LOCAL - 1) * FEATURES
    each = cols // parts
    return pl.pallas_call(
        later_kernel,
        grid=(parts,),
        out_shape=f32(copies, GROUP_LOCAL, width + FEATURES),
        in_specs=[
            pl.BlockSpec((each, tall, FEATURES), lambda n: (n, 0, 0)),
            pl.BlockSpec((each * local, FEATURES), lambda n: (n, 0)),
            pl.BlockSpec((lines, each * local), lambda n: (0, n)),
            whole(),
            whole(),
            whole(),
        ],
        out_specs=whole(),
        scratch_shapes=[pltpu.VMEM((lines, FEATURES), jnp.float32)],
        compiler_params=params(63),
        name="later_terms",
    )(gathered, vectors, masked, weights, change, bias)


def sum_kernel(x_ref, out_ref):
    out = total(x_ref[i] for i in range(x_ref.shape[0]))
    for copy in range(out_ref.shape[0]):
        out_ref[copy] = out


def sum_copies(x, copies):
    return pl.pallas_call(
        sum_kernel,
        out_shape=f32(copies, *x.shape[1:]),
        in_specs=[whole()],
        out_specs=whole(),
        compiler_params=params(8),
        name="sum_of_chunks",
    )(x)


def terms_kernel(old, side_ref, jac_ref, cov_ref, *rest):
    width = cov_ref.shape[1]
    if old:
        scaled_ref, gains_ref = rest[:2]
        out_ref, moved = rest[-2:]
    else:
        out_ref = rest[-1]
    jac = jac_ref[:, :, :width].reshape(-1, width)
    terms = dot3(jac, cov_ref[...], ((1,), (1,)))
    if old:

        @pl.when(pl.program_id(0) == 0)
        def _():
            moved[...] = exact(jac, scaled_ref[...], ((1,), (1,)))

        terms = (terms - exact(moved[...], gains_ref[...])) * (1.0 / forget_rate)
    out_ref[...] = terms.reshape(out_ref.shape)


def gain_terms(side, jac, cov, old, into):
    blocks, sub, wide = jac.shape
    rows, width = cov.shape
    part = 256
    ins = [
        pl.BlockSpec((blocks, sub, wide), lambda n, s: (0, 0, 0)),
        pl.BlockSpec((part, width), lambda n, s: (n, 0)),
    ]
    args = [jac, cov]
    scratch = []
    if old:
        scaled, gains = old
        ins += [
            pl.BlockSpec(scaled.shape, lambda n, s: (0, 0)),
            pl.BlockSpec((gains.shape[0], part), lambda n, s: (0, n)),
        ]
        args += [scaled, gains]
        scratch = [pltpu.VMEM((blocks * sub, scaled.shape[0]), jnp.float32)]
    alias = {}
    if into is not None:
        ins.append(pl.BlockSpec(memory_space=pl.ANY))
        args.append(into)
        alias = {len(args): 0}
    return pl.pallas_call(
        functools.partial(terms_kernel, bool(old)),
        grid_spec=pltpu.PrefetchScalarGridSpec(
            num_scalar_prefetch=1,
            grid=(rows // part,),
            in_specs=ins,
            out_specs=pl.BlockSpec((blocks, sub, part), lambda n, s: (s[0], 0, n)),
            scratch_shapes=scratch,
        ),
        out_shape=f32(2 * blocks, sub, rows),
        input_output_aliases=alias,
        compiler_params=params(60.1),
        name="gain_terms",
    )(side, *args)


def part_kernel(side_ref, own_ref, other_ref, gains_ref, out_ref, jac):
    half = own_ref.shape[0]
    width = gains_ref.shape[1]
    side = side_ref[0]
    jac[pl.ds(side * half, half)] = own_ref[:, :, :width]
    jac[pl.ds((1 - side) * half, half)] = other_ref[:, :, :width]
    part = exact(gains_ref[...], jac[...].reshape(-1, width), ((1,), (1,)))
    for copy in range(out_ref.shape[0]):
        out_ref[copy] = part


def innovation_part(side, own, other, gains, copies):
    half, sub, _ = own.shape
    width = gains.shape[1]
    return pl.pallas_call(
        part_kernel,
        out_shape=f32(copies, sub, 2 * half * sub),
        in_specs=[scalar(), whole(), whole(), whole()],
        out_specs=whole(),
        scratch_shapes=[pltpu.VMEM((2 * half, sub, width), jnp.float32)],
        compiler_params=params(8),
        name="innovation_part",
    )(side, own, other, gains)


def pack_kernel(parts_ref, gains_ref, out_ref):
    width = gains_ref.shape[1]
    part = total(parts_ref[i] for i in range(parts_ref.shape[0]))
    for copy in range(out_ref.shape[0]):
        out_ref[copy, :, :width] = gains_ref[...]
        out_ref[copy, :, width:] = part


def pack(parts, gains, copies):
    sub, width = gains.shape
    return pl.pallas_call(
        pack_kernel,
        out_shape=f32(copies, sub, width + parts.shape[2]),
        in_specs=[whole(), whole()],
        out_specs=whole(),
        compiler_params=params(8),
        name="pack_gains",
    )(parts, gains)


def update_kernel(
    order, side_ref, own_ref, other_ref, e_own_ref, e_other_ref, targets_ref, inverse_ref, gains_ref, change_ref, both, energy
):
    n = targets_ref.shape[0]
    width = own_ref.shape[2] - n
    half = own_ref.shape[0]
    side = side_ref[0]
    mine, theirs = pl.ds(side * half, half), pl.ds((1 - side) * half, half)
    both[mine] = own_ref[...]
    both[theirs] = other_ref[...]
    energy[mine] = e_own_ref[...]
    energy[theirs] = e_other_ref[...]
    places = [order.index(t) for t in range(n // SUB)]
    curvature = jnp.concatenate([both[p, :, width:] for p in places], axis=0)
    row = lax.broadcasted_iota(jnp.int32, (n, n), 0)
    col = lax.broadcasted_iota(jnp.int32, (n, n), 1)
    innovation = 0.5 * (curvature + curvature.T) + jnp.where(row == col, forget_rate, 0.0)
    tiles = sweep_inverse([innovation[SUB * i : SUB * i + SUB] for i in range(n // SUB)])
    weighted = []
    for i, x in enumerate(tiles):
        inverse_ref[SUB * i : SUB * i + SUB, :] = x
        weighted.append(x * (targets_ref[SUB * i : SUB * i + SUB, :] - energy[i]))
    coefficient = jnp.broadcast_to(jnp.sum(total(weighted), axis=0, keepdims=True), (SUB, n))
    gains = jnp.concatenate([both[p, :, :width] for p in places], axis=0)
    gains_ref[...] = gains
    moved = exact(coefficient, gains)
    sub = lax.broadcasted_iota(jnp.int32, (SUB, FEATURES), 0)
    change = moved[:, :FEATURES]
    for r in range(1, width // FEATURES):
        change = jnp.where(sub == r, moved[:, r * FEATURES : (r + 1) * FEATURES], change)
    for j in range(change_ref.shape[0]):
        change_ref[j] = change


def solve_update(side, own, other, jac_own, jac_other, targets, copies, order):
    n = targets.shape[0]
    half, sub, wide = own.shape
    last = jac_own.shape[2] // FEATURES - 1
    energies = pl.BlockSpec((half, sub, FEATURES), lambda i: (0, 0, last))
    return pl.pallas_call(
        functools.partial(update_kernel, order),
        grid=(1,),
        out_shape=(f32(n, n), f32(n, wide - n), f32(copies, SUB, FEATURES)),
        in_specs=[scalar(), whole(), whole(), energies, energies, whole()],
        out_specs=(whole(), whole(), whole()),
        scratch_shapes=[pltpu.VMEM((2 * half, sub, wide), jnp.float32), pltpu.VMEM((2 * half, sub, FEATURES), jnp.float32)],
        compiler_params=params(8),
        name="inverse_and_change",
    )(side, own, other, jac_own, jac_other, targets)


def exchange(chunks, axis):
    return lax.all_to_all(chunks, axis, 0, 0, tiled=True)


def gather_pair(copies):
    count = copies.shape[0]
    lanes = [[core + 2 * z for z in range(count)] for core in range(2)]
    own = lax.all_to_all(copies, "grp", 0, 0, tiled=True, axis_index_groups=lanes)
    other = lax.ppermute(own, "grp", [(i, i ^ 1) for i in range(2 * count)])
    return own, other


def far_row(j, side):
    return (j // side + side // 2) % side * side + (j % side + side // 2) % side


def swap(x, chunk_of_row):
    size = len(chunk_of_row)
    pairs = [(i * size + chunk_of_row[a], a * size + i) for i in range(size) for a in range(size)]
    return lax.ppermute(x, ("grp", "atm"), pairs)


def gather_rows(own):
    twice = jnp.concatenate([own, own], axis=0)
    got = lax.all_gather(twice, "atm", axis=0, tiled=False)
    return got[:, : own.shape[0]].reshape(-1, own.shape[1])


def gather_kernel(atoms_ref, kinds_ref, member_ref, out_ref):
    local = atoms_ref.shape[0]
    lines = local // FEATURES
    out_ref[:local, :] = atoms_ref[...]
    out_ref[local:, :] = jnp.zeros((out_ref.shape[0] - local, FEATURES), jnp.float32)
    for which, ref in enumerate((kinds_ref, member_ref)):
        for u in range(lines):
            values = ref[1:2, u * FEATURES : (u + 1) * FEATURES].astype(jnp.float32)
            place = local + which * lines + u
            out_ref[place : place + 1, :] = values


def gather_atoms(atoms, kinds, member):
    local = atoms.shape[1]
    packed = pl.pallas_call(
        gather_kernel,
        grid=(1,),
        out_shape=f32(local + SUB, FEATURES),
        in_specs=[pl.BlockSpec((None, local, FEATURES), lambda n: (1, 0, 0)), whole(), whole()],
        out_specs=whole(),
        compiler_params=params(63.9),
        name="atoms_with_types",
    )(atoms, kinds, member)
    return lax.all_gather(packed, "atm", axis=0, tiled=False)


def together(*values):
    return lax.optimization_barrier(values)


def body(atoms, kinds, member, targets, weights, bias, readout, covariance):
    rows, cols = lax.axis_size("grp"), lax.axis_size("atm")
    chips = rows // 2
    col_index = lax.axis_index("atm").reshape(1)
    side = (lax.axis_index("grp") % 2).reshape(1)
    away = 1 - side
    local = atoms.shape[1]
    groups = GROUP_LOCAL * rows
    width = covariance.shape[1]
    bias = bias.reshape(1, FEATURES)
    ordered = targets.reshape(STEPS, chips, 2, GROUP_LOCAL).transpose(0, 2, 1, 3).reshape(STEPS, groups, 1)
    ordered = jnp.broadcast_to(ordered, (STEPS, groups, FEATURES))
    chunk_of_row = [far_row(a, math.isqrt(rows)) for a in range(rows)]
    order = [chunk_of_row[2 * z + core] for core in range(2) for z in range(chips)]
    current = weights
    row_gains, scaled = [], []
    for step in range(STEPS):
        if step == 0:
            chunks = first_terms(atoms, kinds, member, current, bias, readout, cols, width)
            chunks, later = together(chunks, atoms)
            gathered = gather_atoms(later, kinds, member)
            copies = sum_copies(exchange(chunks, "atm"), chips)
        else:
            copies = later_terms(gathered, vectors, masked, weights, change, bias, chips)
        jac_own, jac_other = gather_pair(copies)
        old = (scaled[0], row_gains[0]) if step else None
        terms = gain_terms(side, jac_own, covariance, old, None)
        terms = gain_terms(away, jac_other, covariance, old, terms)
        own = exchange(terms, "atm").sum(axis=0)
        if step == 0:
            own, gathered, ordered = together(own, gathered, ordered)
        row_gains.append(gather_rows(own))
        other = swap(own, chunk_of_row)
        if step == 0:
            vectors, masked = prepare(gathered, readout, col_index, local, width // FEATURES)
            other, vectors, masked = together(other, vectors, masked)
        part = exchange(innovation_part(side, jac_own, jac_other, other, cols), "atm")
        got_own, got_other = gather_pair(pack(part, other, chips))
        inverse, col_gains, change = solve_update(
            side, got_own, got_other, jac_own, jac_other, ordered[step], cols, order
        )
        if step == STEPS - 1:
            change, *row_gains = together(change, *row_gains)
        change = exchange(change, "atm")
        current = current + change.reshape(FEATURES, FEATURES)
        scaled.append(dot(inverse, col_gains, ((1,), (0,)), precise))
    left = jnp.concatenate(row_gains, axis=0)
    right = jnp.concatenate([x / forget_rate ** (STEPS - i) for i, x in enumerate(scaled)], axis=0)
    covar = covariance / forget_rate**STEPS - dot(left, right, ((0,), (0,)), three)
    return (covar, current)


def solution(mesh):
    return jax.shard_map(
        body,
        mesh=mesh,
        in_specs=(
            P(None, ("grp", "atm"), None),
            P(None, ("grp", "atm")),
            P(None, ("grp", "atm")),
            P(),
            P(),
            P(),
            P(),
            P("grp", "atm"),
        ),
        out_specs=(P("grp", "atm"), P()),
        check_vma=False,
    )
```

time: 253 us -> 268 us (1.059)
  Pallas kernels: 15.2 us -> 65.6 us
  blocking collectives: 96.7 us -> 124 us
  matrix products: 33.8 us -> 8.45 us
  waiting for transfers between devices: 40.9 us -> 19.8 us
  starting transfers between devices: 32.8 us -> 25.8 us
  local copies, waits for them, and re-layouts: 12.3 us -> 6.61 us
  other arithmetic: 6.53 us -> 1.99 us
    all_gather x4 -> x0, blocking collectives: 82.8 us -> none  [the longest x2 43.8 us: body(): stacked = lax.all_gather(chunk, 'grp', axis=0, tiled=True)]
    all_to_all x0 -> x4, blocking collectives: none -> 57.9 us  [gather_pair(): lax.all_to_all(copies, 'grp', 0, 0, tiled=True, axis_index_groups=lanes)]
    all_to_all x1 -> x5, blocking collectives: 13.9 us -> 65.9 us  [exchange(): return lax.all_to_all(chunks, axis, 0, 0, tiled=True)]
    pallas_call x2 -> x15, Pallas kernels: 15.2 us -> 65.6 us  [the longest x4 23.4 us: gain_terms(): pl.pallas_call(functools.partial(terms_kernel, bool(old)), grid_spec=pltp...]
    all_to_all x6 -> x2, waiting for transfers between devices: 36.8 us -> 11.6 us  [exchange(): return lax.all_to_all(chunks, axis, 0, 0, tiled=True)]
    all_to_all x6 -> x2, starting transfers between devices: 26.9 us -> 7.2 us  [exchange(): return lax.all_to_all(chunks, axis, 0, 0, tiled=True)]
    dot_general x12 -> x3, matrix products: 26.3 us -> 8.45 us  [dot(): lax.dot_general(a, b, ((contract[0], contract[1]), ((), ())), precision=p...]
    ppermute x0 -> x4, starting transfers between devices: none -> 16.1 us  [gather_pair(): other = lax.ppermute(own, 'grp', [(i, i ^ 1) for i in range(2 * count)])]
  transfers between devices with their start and end apart: 11 -> 11, of which waited for: 7 -> 5; matrix products, arithmetic and copies ran while one was open for 15% -> 4% of each run, Pallas kernels for 6% -> 21%
where the time goes in v4:
time: 268 us; the launch traced here: 266 us
  blocking collectives  124 us (46%)
  Pallas kernels  65.6 us (24%)
  starting transfers between devices  25.8 us (10%)
  waiting for transfers between devices  19.8 us (7%)
  between operations  13.9 us (5%)
  matrix products  8.45 us (3%)
  local copies, waits for them, and re-layouts  6.61 us (2%)
    all_to_all x5, blocking collectives, exchange(): return lax.all_to_all(chunks, axis, 0, 0, tiled=True)  65.9 us
    all_to_all x4, blocking collectives, gather_pair(): lax.all_to_all(copies, 'grp', 0, 0, tiled=True, axis_index_groups=lanes)  57.9 us
    pallas_call x4, Pallas kernels, gain_terms(): pl.pallas_call(functools.partial(terms_kernel, bool(old)), grid_spec=pltp...  23.4 us
    pallas_call x2, Pallas kernels, solve_update(): pl.pallas_call(functools.partial(update_kernel, order), grid=(1,), out_sh...  16.2 us
    ppermute x4, starting transfers between devices, gather_pair(): other = lax.ppermute(own, 'grp', [(i, i ^ 1) for i in range(2 * count)])  16.1 us
    pallas_call x1, Pallas kernels, prepare(): pl.pallas_call(prepare_kernel, grid=(cols,), out_shape=(f32(cols * local,...  11.7 us
    all_to_all x2, waiting for transfers between devices, exchange(): return lax.all_to_all(chunks, axis, 0, 0, tiled=True)  11.6 us
    dot_general x3, matrix products, dot(): lax.dot_general(a, b, ((contract[0], contract[1]), ((), ())), precision=p...  8.45 us
  transfers between devices with their start and end apart: 11, of which 5 were waited for; matrix products, arithmetic and copies ran while one was open for 4% of the time, Pallas kernels for 21%

profile of v4, /device:TPU:1, one launch (start us, length us, event | category | flops | bytes accessed | tf_op | source)
XLA Modules:
  0.0 266.0 jit_solution(5510491246392695325)
XLA Ops:
  7.2 2.9 %first_terms.1 = f32[16,8,1152]{2,1,0:T(8,128)} custom-call(f32[2,256,128]{2,1,0:T(8,128)} %atoms_ref.2, s32[2,256]{1,0:T(2,128)} %kinds_ref.3, s32[2,256]{1,0:T(2,128)} %member_ref.3, f32[128,128]{1,0:T(8,128)} %weights_ref.3, f32[1,128]{1,0:T(1,128)} %bitcast.32, f32[4,128]{1,0:T(4,128)} %readout_ref.3), custom_call_target="tpu_custom_call" | custom-call | tf_op jit(solution)/shard_map/first_terms/pallas_call | solution.py:166
  10.1 1.6 atoms_with_types.1
  11.7 18.9 %all_to_all.55.x_ref = f32[16,8,1152]{2,1,0:T(8,128)S(1)} all-to-all(f32[16,8,1152]{2,1,0:T(8,128)} %first_terms.1), channel_id=1, replica_groups=mesh['grp'=16,'atm'=16] {'atm'}, dimensions={0} | all-to-all | bytes 1179648 | tf_op jit(solution)/shard_map/all_to_all | solution.py:440
  30.6 17.7 %all_to_all.56.jac_ref.own_ref.e_own_ref = f32[8,8,1152]{2,1,0:T(8,128)} all-to-all(f32[8,8,1152]{2,1,0:T(8,128)S(1)} %sum_of_chunks.1), channel_id=1, replica_groups={{0,32,64,96,128,160,192,224},{16,48,80,112,144,176,208,240},{1,33,65,97..., dimensions={0} | all-to-all | bytes 589824 | tf_op jit(solution)/shard_map/all_to_all | solution.py:446
  48.2 4.0 %collective-permute-start = (f32[8,8,1152]{2,1,0:T(8,128)}, f32[8,8,1152]{2,1,0:T(8,128)S(1)}, u32[]{:S(2)}, u32[]{:S(2)}) collective-permute-start(f32[8,8,1152]{2,1,0:T(8,128)} %all_to_all.56.jac_ref.own_ref.e_own_ref), channel_id=1, source_target_pairs={{0,16},{16,0},{32,48},{48,32},{64,80},{80,64},{96,112},{112,96},{1... | collective-permute-start | bytes 884744 | tf_op jit(solution)/shard_map/ppermute | solution.py:447
  52.2 5.1 %gain_terms.4.rest_0_ = f32[16,8,1024]{2,1,0:T(8,128)} custom-call(s32[1]{0:T(128)} %bitcast.side_ref, f32[8,8,1152]{2,1,0:T(8,128)} %all_to_all.56.jac_ref.own_ref.e_own_ref, f32[1024,1024]{1,0:T(8,128)} %cov_ref.7), custom_call_target="tpu_custom_call" | custom-call | tf_op jit(solution)/shard_map/gain_terms/pallas_call | solution.py:327
  57.3 0.7 copy-done
  58.0 5.1 %gain_terms.5 = f32[16,8,1024]{2,1,0:T(8,128)} custom-call(s32[1]{0:T(128)S(6)} %sub.6.side_ref, f32[8,8,1152]{2,1,0:T(8,128)} %copy-done, f32[1024,1024]{1,0:T(8,128)} %cov_ref.7, f32[16,8,1024]{2,1,0:T(8,128)} %gain_terms.4.rest_0_), custom_call_target="tpu_custom_call", output_to_operand_aliasing={{}: (3, {})} | custom-call | tf_op jit(solution)/shard_map/gain_terms/pallas_call | solution.py:327
  63.1 3.7 %all-to-all-start.2 = ((f32[16,8,1024]{2,1,0:T(8,128)}), f32[16,8,1024]{2,1,0:T(8,128)S(1)}, u32[]{:S(2)}, u32[]{:S(2)}) async-start(f32[16,8,1024]{2,1,0:T(8,128)} %gain_terms.5), calls=%async_computation.2 | async-start | bytes 1048576 | tf_op jit(solution)/shard_map/all_to_all | solution.py:440
  66.9 0.1 reshape.32
  67.0 0.1 broadcast_in_dim.7
  67.1 11.5 %all-to-all-done.2 = f32[16,8,1024]{2,1,0:T(8,128)S(1)} async-done(((f32[16,8,1024]{2,1,0:T(8,128)}), f32[16,8,1024]{2,1,0:T(8,128)S(1)}, u32[]{:S(2)}, u32[]{:S(2)}) %all-to-all-start.2) | async-done | bytes 524320 | tf_op jit(solution)/shard_map/all_to_all | solution.py:440
  78.6 0.1 broadcast_in_dim.8
  78.7 0.6 pad_maximum_fusion
  79.5 0.9 collective-permute-start.1
  80.3 11.7 %prepare_terms.1 = (f32[4096,128]{1,0:T(8,128)}, f32[72,4096]{1,0:T(8,128)}) custom-call(s32[1]{0:T(128)} %bitcast.4.col_ref, f32[16,264,128]{2,1,0:T(8,128)} %bitcast.27, f32[4,128]{1,0:T(4,128)} %readout_ref.3), custom_call_target="tpu_custom_call" | custom-call | tf_op jit(solution)/shard_map/prepare_terms/pallas_call | solution.py:199
  92.0 1.5 innovation_part.2
  93.5 12.0 %all_to_all.57.parts_ref = f32[16,8,128]{2,1,0:T(8,128)S(1)} all-to-all(f32[16,8,128]{2,1,0:T(8,128)S(1)} %innovation_part.2), channel_id=1, replica_groups=mesh['grp'=16,'atm'=16] {'atm'}, dimensions={0} | all-to-all | bytes 131072 | tf_op jit(solution)/shard_map/all_to_all | solution.py:440
  105.6 13.7 %all_to_all.58.own_ref = f32[8,8,1152]{2,1,0:T(8,128)S(1)} all-to-all(f32[8,8,1152]{2,1,0:T(8,128)S(1)} %pack_gains.2), channel_id=1, replica_groups={{0,32,64,96,128,160,192,224},{16,48,80,112,144,176,208,240},{1,33,65,97..., dimensions={0} | all-to-all | bytes 589824 | tf_op jit(solution)/shard_map/all_to_all | solution.py:446
  119.3 4.1 %collective-permute-start.2 = (f32[8,8,1152]{2,1,0:T(8,128)S(1)}, f32[8,8,1152]{2,1,0:T(8,128)S(1)}, u32[]{:S(2)}, u32[]{:S(2)}) collective-permute-start(f32[8,8,1152]{2,1,0:T(8,128)S(1)} %all_to_all.58.own_ref), channel_id=1, source_target_pairs={{0,16},{16,0},{32,48},{48,32},{64,80},{80,64},{96,112},{112,96},{1... | collective-permute-start | bytes 884744 | tf_op jit(solution)/shard_map/ppermute | solution.py:447
  123.4 1.2 collective-permute-done.2.other_ref
  124.6 7.8 %inverse_and_change.2 = (f32[128,128]{1,0:T(8,128)S(1)}, f32[128,1024]{1,0:T(8,128)S(1)}, f32[16,8,128]{2,1,0:T(8,128)S(1)}) custom-call(s32[1]{0:T(128)} %bitcast.side_ref, f32[8,8,1152]{2,1,0:T(8,128)S(1)} %all_to_all.58.own_ref, f32[8,8,1152]{2,1,0:T(8,128)S(1)} %collective-permute-done.2.other_ref, f32[8,8,1152]{2,1,0:T(8,128)} %all_to_all.56.jac_ref.own_ref.e_own_ref, ...), custom_call_target="tpu_custom_call" | custom-call | tf_op jit(solution)/shard_map/inverse_and_change/pallas_call | solution.py:427
  132.4 9.7 %all_to_all.59.change_ref = f32[16,8,128]{2,1,0:T(8,128)} all-to-all(f32[16,8,128]{2,1,0:T(8,128)S(1)} %get-tuple-element.31), channel_id=1, replica_groups=mesh['grp'=16,'atm'=16] {'atm'}, dimensions={0} | all-to-all | bytes 131072 | tf_op jit(solution)/shard_map/all_to_all | solution.py:440
  142.1 6.7 %later_terms.1 = f32[8,8,1152]{2,1,0:T(8,128)} custom-call(f32[16,264,128]{2,1,0:T(8,128)} %bitcast.28, f32[4096,128]{1,0:T(8,128)} %get-tuple-element.27.vectors_ref, f32[72,4096]{1,0:T(8,128)} %get-tuple-element.28.masked_ref, f32[128,128]{1,0:T(8,128)} %weights_ref.3, f32[16,8,128]{2,1,0:T(8,128)} %all_to_all.59.change_ref, f32[1,128]{1,0:T(1,128)} %bitcast.33), custom_call_target="tpu_custom_call" | custom-call | tf_op jit(solution)/shard_map/later_terms/pallas_call | solution.py:249
  148.9 14.5 %all_to_all.60.jac_ref.own_ref.e_own_ref = f32[8,8,1152]{2,1,0:T(8,128)} all-to-all(f32[8,8,1152]{2,1,0:T(8,128)} %later_terms.1), channel_id=1, replica_groups={{0,32,64,96,128,160,192,224},{16,48,80,112,144,176,208,240},{1,33,65,97..., dimensions={0} | all-to-all | bytes 589824 | tf_op jit(solution)/shard_map/all_to_all | solution.py:446
  163.3 3.1 %collective-permute-start.3 = (f32[8,8,1152]{2,1,0:T(8,128)}, f32[8,8,1152]{2,1,0:T(8,128)S(1)}, u32[]{:S(2)}, u32[]{:S(2)}) collective-permute-start(f32[8,8,1152]{2,1,0:T(8,128)} %all_to_all.60.jac_ref.own_ref.e_own_ref), channel_id=1, source_target_pairs={{0,16},{16,0},{32,48},{48,32},{64,80},{80,64},{96,112},{112,96},{1... | collective-permute-start | bytes 884744 | tf_op jit(solution)/shard_map/ppermute | solution.py:447
  166.4 1.5 broadcast_multiply_fusion
  168.0 1.9 slice_bitcast_fusion.1.rest_1_
  169.9 6.6 %gain_terms.6.rest_2_ = f32[16,8,1024]{2,1,0:T(8,128)} custom-call(s32[1]{0:T(128)} %bitcast.side_ref, f32[8,8,1152]{2,1,0:T(8,128)} %all_to_all.60.jac_ref.own_ref.e_own_ref, f32[1024,1024]{1,0:T(8,128)} %cov_ref.7, f32[128,1024]{1,0:T(8,128)} %get-tuple-element.43.rest_0_, f32[128,1024]{1,0:T(8,128)} %slice_bitcast_fusion.1.rest_1_), custom_call_target="tpu_custom_call" | custom-call | tf_op jit(solution)/shard_map/gain_terms/pallas_call | solution.py:327
  176.5 0.7 copy-done.2
  177.2 6.6 %gain_terms.7 = f32[16,8,1024]{2,1,0:T(8,128)} custom-call(s32[1]{0:T(128)S(6)} %sub.6.side_ref, f32[8,8,1152]{2,1,0:T(8,128)} %copy-done.2, f32[1024,1024]{1,0:T(8,128)} %cov_ref.7, f32[128,1024]{1,0:T(8,128)} %get-tuple-element.43.rest_0_, f32[128,1024]{1,0:T(8,128)} %slice_bitcast_fusion.1.rest_1_, ...), custom_call_target="tpu_custom_call", output_to_operand_aliasing={{}: (5, {})} | custom-call | tf_op jit(solution)/shard_map/gain_terms/pallas_call | solution.py:327
  183.8 14.9 %all_to_all.61 = f32[16,8,1024]{2,1,0:T(8,128)S(1)} all-to-all(f32[16,8,1024]{2,1,0:T(8,128)} %gain_terms.7), channel_id=1, replica_groups=mesh['grp'=16,'atm'=16] {'atm'}, dimensions={0} | all-to-all | bytes 1048576 | tf_op jit(solution)/shard_map/all_to_all | solution.py:440
  198.7 0.6 pad_maximum_fusion.1
  199.4 1.5 collective-permute-start.4
  200.9 5.8 %collective-permute-done.4.gains_ref = f32[8,1024]{1,0:T(8,128)S(1)} collective-permute-done((f32[8,1024]{1,0:T(8,128)S(1)}, f32[8,1024]{1,0:T(8,128)S(1)}, u32[]{:S(2)}, u32[]{:S(2)}) %collective-permute-start.4) | collective-permute-done | bytes 32800 | tf_op jit(solution)/shard_map/ppermute | solution.py:458
  206.6 1.0 copy-done.3
  207.6 1.5 innovation_part.3
  209.1 10.4 %all_to_all.62.parts_ref = f32[16,8,128]{2,1,0:T(8,128)S(1)} all-to-all(f32[16,8,128]{2,1,0:T(8,128)S(1)} %innovation_part.3), channel_id=1, replica_groups=mesh['grp'=16,'atm'=16] {'atm'}, dimensions={0} | all-to-all | bytes 131072 | tf_op jit(solution)/shard_map/all_to_all | solution.py:440
  219.5 12.1 %all_to_all.63.own_ref = f32[8,8,1152]{2,1,0:T(8,128)S(1)} all-to-all(f32[8,8,1152]{2,1,0:T(8,128)S(1)} %pack_gains.3), channel_id=1, replica_groups={{0,32,64,96,128,160,192,224},{16,48,80,112,144,176,208,240},{1,33,65,97..., dimensions={0} | all-to-all | bytes 589824 | tf_op jit(solution)/shard_map/all_to_all | solution.py:446
  231.6 5.0 %collective-permute-start.5 = (f32[8,8,1152]{2,1,0:T(8,128)S(1)}, f32[8,8,1152]{2,1,0:T(8,128)S(1)}, u32[]{:S(2)}, u32[]{:S(2)}) collective-permute-start(f32[8,8,1152]{2,1,0:T(8,128)S(1)} %all_to_all.63.own_ref), channel_id=1, source_target_pairs={{0,16},{16,0},{32,48},{48,32},{64,80},{80,64},{96,112},{112,96},{1... | collective-permute-start | bytes 884744 | tf_op jit(solution)/shard_map/ppermute | solution.py:447
  236.6 1.2 collective-permute-done.5.other_ref
  237.8 1.0 copy-done.4
  238.7 8.4 %inverse_and_change.3 = (f32[128,128]{1,0:T(8,128)S(1)}, f32[128,1024]{1,0:T(8,128)S(1)}, f32[16,8,128]{2,1,0:T(8,128)}) custom-call(s32[1]{0:T(128)} %bitcast.side_ref, f32[8,8,1152]{2,1,0:T(8,128)S(1)} %all_to_all.63.own_ref, f32[8,8,1152]{2,1,0:T(8,128)S(1)} %collective-permute-done.5.other_ref, f32[8,8,1152]{2,1,0:T(8,128)} %all_to_all.60.jac_ref.own_ref.e_own_ref, ...), custom_call_target="tpu_custom_call" | custom-call | tf_op jit(solution)/shard_map/inverse_and_change/pallas_call | solution.py:427
  247.2 0.6 convolution_multiply_fusion
  247.8 1.1 slice_bitcast_fusion
  248.9 3.5 %all-to-all-start.10 = ((f32[16,8,128]{2,1,0:T(8,128)}), f32[16,8,128]{2,1,0:T(8,128)S(1)}, u32[]{:S(2)}, u32[]{:S(2)}) async-start(f32[16,8,128]{2,1,0:T(8,128)} %get-tuple-element.39), calls=%async_computation.10 | async-start | bytes 131072 | tf_op jit(solution)/shard_map/all_to_all | solution.py:440
  252.4 6.3 %multiply_subtract_fusion = f32[1024,1024]{1,0:T(8,128)} fusion(f32[1024,1024]{1,0:T(8,128)} %cov_ref.7, f32[128,1024]{1,0:T(8,128)S(1)} %slice_bitcast_fusion, f32[128,1024]{1,0:T(8,128)S(1)} %copy-done.5, f32[128,1024]{1,0:T(8,128)S(1)} %convolution_multiply_fusion, f32[128,1024]{1,0:T(8,128)S(1)} %copy-done.6), kind=kOutput, calls=%fused_computation | convolution fusion | flops 1613234176 | bytes 10485760 | tf_op jit(solution)/shard_map/dot_general | solution.py:23
  258.8 0.6 bitcast_add_fusion
  (36 shorter events, 0.5 us)
Async XLA Ops:
  7.2 71.5 %all-gather.7.cloned.1.call-start = ((), (), s32[]{:S(2)}) async-start(), calls=%async_computation.11 | async-start | bytes 2297856 | tf_op jit(solution)/shard_map/all_gather | solution.py:490
  48.2 9.1 %collective-permute-start = (f32[8,8,1152]{2,1,0:T(8,128)}, f32[8,8,1152]{2,1,0:T(8,128)S(1)}, u32[]{:S(2)}, u32[]{:S(2)}) collective-permute-start(f32[8,8,1152]{2,1,0:T(8,128)} %all_to_all.56.jac_ref.own_ref.e_own_ref), channel_id=1, source_target_pairs={{0,16},{16,0},{32,48},{48,32},{64,80},{80,64},{96,112},{112,96},{1... | collective-permute-start | bytes 884744 | tf_op jit(solution)/shard_map/ppermute | solution.py:447
  57.3 9.6 %copy-start.9 = (f32[2,128]{1,0:T(2,128)S(1)}, f32[2,128]{1,0:T(2,128)}, u32[]{:S(2)}) copy-start(f32[2,128]{1,0:T(2,128)} %param.11) | copy-start | bytes 3076
  57.3 0.7 copy-start
  63.1 28.9 %copy-start.1 = (f32[8,8,1152]{2,1,0:T(8,128)S(1)}, f32[8,8,1152]{2,1,0:T(8,128)}, u32[]{:S(2)}) copy-start(f32[8,8,1152]{2,1,0:T(8,128)} %copy-done) | copy-start | bytes 884740
  63.1 15.5 %all-to-all-start.2 = ((f32[16,8,1024]{2,1,0:T(8,128)}), f32[16,8,1024]{2,1,0:T(8,128)S(1)}, u32[]{:S(2)}, u32[]{:S(2)}) async-start(f32[16,8,1024]{2,1,0:T(8,128)} %gain_terms.5), calls=%async_computation.2 | async-start | bytes 1048576 | tf_op jit(solution)/shard_map/all_to_all | solution.py:440
  66.8 101.1 %all-gather.9.cloned.1.call-start = ((), (), s32[]{:S(2)}) async-start(), calls=%async_computation.12 | async-start | bytes 1114112 | tf_op jit(solution)/shard_map/all_gather | solution.py:463
  79.4 168.4 %all-gather.11.cloned.1.call-start = ((), (), s32[]{:S(2)}) async-start(), calls=%async_computation.13 | async-start | bytes 1114112 | tf_op jit(solution)/shard_map/all_gather | solution.py:463
  79.5 12.6 %collective-permute-start.1 = (f32[8,1024]{1,0:T(8,128)S(1)}, f32[8,1024]{1,0:T(8,128)S(1)}, u32[]{:S(2)}, u32[]{:S(2)}) collective-permute-start(f32[8,1024]{1,0:T(8,128)S(1)} %reduce_sum.18), channel_id=1, source_target_pairs={{10,0},{11,16},{8,32},{9,48},{14,64},{15,80},{12,96},{13,112},{2,1... | collective-permute-start | bytes 98312 | tf_op jit(solution)/shard_map/ppermute | solution.py:458
  119.3 5.3 %collective-permute-start.2 = (f32[8,8,1152]{2,1,0:T(8,128)S(1)}, f32[8,8,1152]{2,1,0:T(8,128)S(1)}, u32[]{:S(2)}, u32[]{:S(2)}) collective-permute-start(f32[8,8,1152]{2,1,0:T(8,128)S(1)} %all_to_all.58.own_ref), channel_id=1, source_target_pairs={{0,16},{16,0},{32,48},{48,32},{64,80},{80,64},{96,112},{112,96},{1... | collective-permute-start | bytes 884744 | tf_op jit(solution)/shard_map/ppermute | solution.py:447
  163.3 13.1 %collective-permute-start.3 = (f32[8,8,1152]{2,1,0:T(8,128)}, f32[8,8,1152]{2,1,0:T(8,128)S(1)}, u32[]{:S(2)}, u32[]{:S(2)}) collective-permute-start(f32[8,8,1152]{2,1,0:T(8,128)} %all_to_all.60.jac_ref.own_ref.e_own_ref), channel_id=1, source_target_pairs={{0,16},{16,0},{32,48},{48,32},{64,80},{80,64},{96,112},{112,96},{1... | collective-permute-start | bytes 884744 | tf_op jit(solution)/shard_map/ppermute | solution.py:447
  176.5 0.7 copy-start.2
  183.8 68.6 %copy-start.5 = (f32[128,1024]{1,0:T(8,128)S(1)}, f32[128,1024]{1,0:T(8,128)}, u32[]{:S(2)}) copy-start(f32[128,1024]{1,0:T(8,128)} %slice_bitcast_fusion.1.rest_1_) | copy-start | bytes 1572868
  183.8 68.6 %copy-start.6 = (f32[128,1024]{1,0:T(8,128)S(1)}, f32[128,1024]{1,0:T(8,128)}, u32[]{:S(2)}) copy-start(f32[128,1024]{1,0:T(8,128)} %get-tuple-element.42) | copy-start | bytes 1572868
  199.4 7.2 %collective-permute-start.4 = (f32[8,1024]{1,0:T(8,128)S(1)}, f32[8,1024]{1,0:T(8,128)S(1)}, u32[]{:S(2)}, u32[]{:S(2)}) collective-permute-start(f32[8,1024]{1,0:T(8,128)S(1)} %reduce_sum.19), channel_id=1, source_target_pairs={{10,0},{11,16},{8,32},{9,48},{14,64},{15,80},{12,96},{13,112},{2,1... | collective-permute-start | bytes 98312 | tf_op jit(solution)/shard_map/ppermute | solution.py:458
  206.6 1.0 copy-start.3
  231.6 6.2 %collective-permute-start.5 = (f32[8,8,1152]{2,1,0:T(8,128)S(1)}, f32[8,8,1152]{2,1,0:T(8,128)S(1)}, u32[]{:S(2)}, u32[]{:S(2)}) collective-permute-start(f32[8,8,1152]{2,1,0:T(8,128)S(1)} %all_to_all.63.own_ref), channel_id=1, source_target_pairs={{0,16},{16,0},{32,48},{48,32},{64,80},{80,64},{96,112},{112,96},{1... | collective-permute-start | bytes 884744 | tf_op jit(solution)/shard_map/ppermute | solution.py:447
  237.8 1.0 copy-start.4
  248.9 10.0 %all-to-all-start.10 = ((f32[16,8,128]{2,1,0:T(8,128)}), f32[16,8,128]{2,1,0:T(8,128)S(1)}, u32[]{:S(2)}, u32[]{:S(2)}) async-start(f32[16,8,128]{2,1,0:T(8,128)} %get-tuple-element.39), calls=%async_computation.10 | async-start | bytes 131072 | tf_op jit(solution)/shard_map/all_to_all | solution.py:440
  252.4 6.4 %copy-start.7 = (f32[128,128]{1,0:T(8,128)S(1)}, f32[128,128]{1,0:T(8,128)}, u32[]{:S(2)}) copy-start(f32[128,128]{1,0:T(8,128)} %weights_ref.3) | copy-start | bytes 196612
  252.4 6.4 %copy-start.8 = (f32[16,8,128]{2,1,0:T(8,128)S(1)}, f32[16,8,128]{2,1,0:T(8,128)}, u32[]{:S(2)}) copy-start(f32[16,8,128]{2,1,0:T(8,128)} %all_to_all.59.change_ref) | copy-start | bytes 196612
Sparse Core Ops, SparseCore 0:
  11.8 52.9 all-gather.6
  79.5 39.1 all-gather.8
  199.5 39.3 all-gather.10

commit v5 on v4

--- a/solution.py
+++ b/solution.py
@@ -131,9 +131,15 @@
 
 
 def vectors_of(kinds, readout):
-    extra = SUB - readout.shape[0]
+    extra = 2 * SUB - readout.shape[0]
     table = jnp.concatenate([readout, jnp.zeros((extra, readout.shape[1]), jnp.float32)], axis=0)
-    return exact(hot(kinds, SUB), table, ((0,), (0,)))
+    which = hot(kinds, 2 * SUB).astype(jnp.bfloat16)
+    out = 0.0
+    for _ in range(3):
+        part = table.astype(jnp.bfloat16)
+        table = table - part.astype(jnp.float32)
+        out = out + lax.dot_general(which, part, (((0,), (0,)), ((), ())), preferred_element_type=jnp.float32)
+    return out
 
 
 def layer(atoms, weights, bias, vectors):
@@ -176,33 +182,42 @@
 
 
 def prepare_kernel(col_ref, gathered_ref, readout_ref, vectors_ref, masked_ref, turned):
-    local = vectors_ref.shape[0]
+    blocks = gathered_ref.shape[0]
+    local = vectors_ref.shape[0] // blocks
     lines = local // FEATURES
     count = (masked_ref.shape[0] - GROUP_LOCAL) // GROUP_LOCAL
-
-    def row(start):
-        parts = [gathered_ref[start + u : start + u + 1, :] for u in range(lines)]
-        return jnp.concatenate(parts, axis=1).astype(jnp.int32)
-
-    vectors_ref[...] = vectors_of(row(local), readout_ref[...])
-    group_hot = hot(row(local + lines), GROUP_LOCAL)
-    turned[...] = gathered_ref[:local, :].T
-    part = turned[pl.ds(pl.multiple_of(col_ref[0] * count, SUB), count), :]
-    for f in range(count):
-        masked_ref[SUB * f : SUB * f + SUB, :] = part[f : f + 1, :] * group_hot
-    masked_ref[SUB * count :, :] = group_hot
+    first = pl.multiple_of(col_ref[0] * count, SUB)
+    for block in range(blocks):
+
+        def row(start):
+            parts = [gathered_ref[block, start + u : start + u + 1, :] for u in range(lines)]
+            return jnp.concatenate(parts, axis=1).astype(jnp.int32)
+
+        here = slice(block * local, (block + 1) * local)
+        vectors_ref[here, :] = vectors_of(row(local), readout_ref[...])
+        group_hot = hot(row(local + lines), GROUP_LOCAL)
+        turned[block] = gathered_ref[block, :local, :].T
+        part = turned[block, pl.ds(first, count), :]
+        for f in range(count):
+            masked_ref[SUB * f : SUB * f + SUB, here] = part[f : f + 1, :] * group_hot
+        masked_ref[SUB * count :, here] = group_hot
 
 
 def prepare(gathered, readout, col_index, local, count):
     cols, tall, _ = gathered.shape
     lines = GROUP_LOCAL * (count + 1)
+    parts = 4
+    each = cols // parts
     return pl.pallas_call(
         prepare_kernel,
-        grid=(cols,),
+        grid=(parts,),
         out_shape=(f32(cols * local, FEATURES), f32(lines, cols * local)),
-        in_specs=[scalar(), pl.BlockSpec((None, tall, FEATURES), lambda n: (n, 0, 0)), whole()],
-        out_specs=(pl.BlockSpec((local, FEATURES), lambda n: (n, 0)), pl.BlockSpec((lines, local), lambda n: (0, n))),
-        scratch_shapes=[pltpu.VMEM((FEATURES, local), jnp.float32)],
+        in_specs=[scalar(), pl.BlockSpec((each, tall, FEATURES), lambda n: (n, 0, 0)), whole()],
+        out_specs=(
+            pl.BlockSpec((each * local, FEATURES), lambda n: (n, 0)),
+            pl.BlockSpec((lines, each * local), lambda n: (0, n)),
+        ),
+        scratch_shapes=[pltpu.VMEM((each, FEATURES, local), jnp.float32)],
         compiler_params=params(63),
         name="prepare_terms",
     )(col_index, gathered, readout)
@@ -265,106 +280,6 @@
     )(gathered, vectors, masked, weights, change, bias)
 
 
-def sum_kernel(x_ref, out_ref):
-    out = total(x_ref[i] for i in range(x_ref.shape[0]))
-    for copy in range(out_ref.shape[0]):
-        out_ref[copy] = out
-
-
-def sum_copies(x, copies):
-    return pl.pallas_call(
-        sum_kernel,
-        out_shape=f32(copies, *x.shape[1:]),
-        in_specs=[whole()],
-        out_specs=whole(),
-        compiler_params=params(8),
-        name="sum_of_chunks",
-    )(x)
-
-
-def terms_kernel(old, side_ref, jac_ref, cov_ref, *rest):
-    width = cov_ref.shape[1]
-    if old:
-        scaled_ref, gains_ref = rest[:2]
-        out_ref, moved = rest[-2:]
-    else:
-        out_ref = rest[-1]
-    jac = jac_ref[:, :, :width].reshape(-1, width)
-    terms = dot3(jac, cov_ref[...], ((1,), (1,)))
-    if old:
-
-        @pl.when(pl.program_id(0) == 0)
-        def _():
-            moved[...] = exact(jac, scaled_ref[...], ((1,), (1,)))
-
-        terms = (terms - exact(moved[...], gains_ref[...])) * (1.0 / forget_rate)
-    out_ref[...] = terms.reshape(out_ref.shape)
-
-
-def gain_terms(side, jac, cov, old, into):
-    blocks, sub, wide = jac.shape
-    rows, width = cov.shape
-    part = 256
-    ins = [
-        pl.BlockSpec((blocks, sub, wide), lambda n, s: (0, 0, 0)),
-        pl.BlockSpec((part, width), lambda n, s: (n, 0)),
-    ]
-    args = [jac, cov]
-    scratch = []
-    if old:
-        scaled, gains = old
-        ins += [
-            pl.BlockSpec(scaled.shape, lambda n, s: (0, 0)),
-            pl.BlockSpec((gains.shape[0], part), lambda n, s: (0, n)),
-        ]
-        args += [scaled, gains]
-        scratch = [pltpu.VMEM((blocks * sub, scaled.shape[0]), jnp.float32)]
-    alias = {}
-    if into is not None:
-        ins.append(pl.BlockSpec(memory_space=pl.ANY))
-        args.append(into)
-        alias = {len(args): 0}
-    return pl.pallas_call(
-        functools.partial(terms_kernel, bool(old)),
-        grid_spec=pltpu.PrefetchScalarGridSpec(
-            num_scalar_prefetch=1,
-            grid=(rows // part,),
-            in_specs=ins,
-            out_specs=pl.BlockSpec((blocks, sub, part), lambda n, s: (s[0], 0, n)),
-            scratch_shapes=scratch,
-        ),
-        out_shape=f32(2 * blocks, sub, rows),
-        input_output_aliases=alias,
-        compiler_params=params(60.1),
-        name="gain_terms",
-    )(side, *args)
-
-
-def part_kernel(side_ref, own_ref, other_ref, gains_ref, out_ref, jac):
-    half = own_ref.shape[0]
-    width = gains_ref.shape[1]
-    side = side_ref[0]
-    jac[pl.ds(side * half, half)] = own_ref[:, :, :width]
-    jac[pl.ds((1 - side) * half, half)] = other_ref[:, :, :width]
-    part = exact(gains_ref[...], jac[...].reshape(-1, width), ((1,), (1,)))
-    for copy in range(out_ref.shape[0]):
-        out_ref[copy] = part
-
-
-def innovation_part(side, own, other, gains, copies):
-    half, sub, _ = own.shape
-    width = gains.shape[1]
-    return pl.pallas_call(
-        part_kernel,
-        out_shape=f32(copies, sub, 2 * half * sub),
-        in_specs=[scalar(), whole(), whole(), whole()],
-        out_specs=whole(),
-        scratch_shapes=[pltpu.VMEM((2 * half, sub, width), jnp.float32)],
-        compiler_params=params(8),
-        name="innovation_part",
-    )(side, own, other, gains)
-
-
 def pack_kernel(parts_ref, gains_ref, out_ref):
     width = gains_ref.shape[1]
     part = total(parts_ref[i] for i in range(parts_ref.shape[0]))
@@ -385,18 +300,13 @@
     )(parts, gains)
 
 
-def update_kernel(
-    order, side_ref, own_ref, other_ref, e_own_ref, e_other_ref, targets_ref, inverse_ref, gains_ref, change_ref, both, energy
-):
+def update_kernel(order, side_ref, own_ref, other_ref, energy_ref, targets_ref, inverse_ref, gains_ref, change_ref, both):
     n = targets_ref.shape[0]
     width = own_ref.shape[2] - n
     half = own_ref.shape[0]
     side = side_ref[0]
-    mine, theirs = pl.ds(side * half, half), pl.ds((1 - side) * half, half)
-    both[mine] = own_ref[...]
-    both[theirs] = other_ref[...]
-    energy[mine] = e_own_ref[...]
-    energy[theirs] = e_other_ref[...]
+    both[pl.ds(side * half, half)] = own_ref[...]
+    both[pl.ds((1 - side) * half, half)] = other_ref[...]
     places = [order.index(t) for t in range(n // SUB)]
     curvature = jnp.concatenate([both[p, :, width:] for p in places], axis=0)
     row = lax.broadcasted_iota(jnp.int32, (n, n), 0)
@@ -405,8 +315,9 @@
     tiles = sweep_inverse([innovation[SUB * i : SUB * i + SUB] for i in range(n // SUB)])
     weighted = []
     for i, x in enumerate(tiles):
-        inverse_ref[SUB * i : SUB * i + SUB, :] = x
-        weighted.append(x * (targets_ref[SUB * i : SUB * i + SUB, :] - energy[i]))
+        here = slice(SUB * i, SUB * i + SUB)
+        inverse_ref[here, :] = x
+        weighted.append(x * (targets_ref[here, :] - energy_ref[here, :]))
     coefficient = jnp.broadcast_to(jnp.sum(total(weighted), axis=0, keepdims=True), (SUB, n))
     gains = jnp.concatenate([both[p, :, :width] for p in places], axis=0)
     gains_ref[...] = gains
@@ -419,25 +330,28 @@
         change_ref[j] = change
 
 
-def solve_update(side, own, other, jac_own, jac_other, targets, copies, order):
+def solve_update(side, own, other, stacked, targets, copies, order):
     n = targets.shape[0]
     half, sub, wide = own.shape
-    last = jac_own.shape[2] // FEATURES - 1
-    energies = pl.BlockSpec((half, sub, FEATURES), lambda i: (0, 0, last))
+    last = stacked.shape[1] // FEATURES - 1
     return pl.pallas_call(
         functools.partial(update_kernel, order),
         grid=(1,),
         out_shape=(f32(n, n), f32(n, wide - n), f32(copies, SUB, FEATURES)),
-        in_specs=[scalar(), whole(), whole(), energies, energies, whole()],
+        in_specs=[scalar(), whole(), whole(), pl.BlockSpec((n, FEATURES), lambda i: (0, last)), whole()],
         out_specs=(whole(), whole(), whole()),
-        scratch_shapes=[pltpu.VMEM((2 * half, sub, wide), jnp.float32), pltpu.VMEM((2 * half, sub, FEATURES), jnp.float32)],
+        scratch_shapes=[pltpu.VMEM((2 * half, sub, wide), jnp.float32)],
         compiler_params=params(8),
         name="inverse_and_change",
-    )(side, own, other, jac_own, jac_other, targets)
+    )(side, own, other, stacked, targets)
 
 
 def exchange(chunks, axis):
     return lax.all_to_all(chunks, axis, 0, 0, tiled=True)
+
+
+def spread(x, axis):
+    return exchange(jnp.broadcast_to(x[None], (lax.axis_size(axis),) + x.shape), axis)
 
 
 def gather_pair(copies):
@@ -499,13 +413,11 @@
     chips = rows // 2
     col_index = lax.axis_index("atm").reshape(1)
     side = (lax.axis_index("grp") % 2).reshape(1)
-    away = 1 - side
     local = atoms.shape[1]
     groups = GROUP_LOCAL * rows
     width = covariance.shape[1]
     bias = bias.reshape(1, FEATURES)
-    ordered = targets.reshape(STEPS, chips, 2, GROUP_LOCAL).transpose(0, 2, 1, 3).reshape(STEPS, groups, 1)
-    ordered = jnp.broadcast_to(ordered, (STEPS, groups, FEATURES))
+    ordered = jnp.broadcast_to(targets[:, :, None], (STEPS, groups, FEATURES))
     chunk_of_row = [far_row(a, math.isqrt(rows)) for a in range(rows)]
     order = [chunk_of_row[2 * z + core] for core in range(2) for z in range(chips)]
     current = weights
@@ -515,14 +427,15 @@
             chunks = first_terms(atoms, kinds, member, current, bias, readout, cols, width)
             chunks, later = together(chunks, atoms)
             gathered = gather_atoms(later, kinds, member)
-            copies = sum_copies(exchange(chunks, "atm"), chips)
+            chunk = exchange(chunks, "atm").sum(axis=0)
         else:
-            copies = later_terms(gathered, vectors, masked, weights, change, bias, chips)
-        jac_own, jac_other = gather_pair(copies)
-        old = (scaled[0], row_gains[0]) if step else None
-        terms = gain_terms(side, jac_own, covariance, old, None)
-        terms = gain_terms(away, jac_other, covariance, old, terms)
-        own = exchange(terms, "atm").sum(axis=0)
+            chunk = later_terms(gathered, vectors, masked, weights, change, bias, 1)[0]
+        stacked = lax.all_gather(chunk, "grp", axis=0, tiled=True)
+        jac = stacked[:, :width]
+        terms = dot(jac, covariance, ((1,), (1,)), three)
+        for gains, part in zip(row_gains, scaled):
+            terms = (terms - dot(dot(jac, part, ((1,), (1,)), precise), gains, ((1,), (0,)), precise)) / forget_rate
+        own = exchange(terms.reshape(cols, groups // cols, width), "atm").sum(axis=0)
         if step == 0:
             own, gathered, ordered = together(own, gathered, ordered)
         row_gains.append(gather_rows(own))
@@ -530,10 +443,10 @@
         if step == 0:
             vectors, masked = prepare(gathered, readout, col_index, local, width // FEATURES)
             other, vectors, masked = together(other, vectors, masked)
-        part = exchange(innovation_part(side, jac_own, jac_other, other, cols), "atm")
+        part = spread(dot(other, jac, ((1,), (1,)), precise), "atm")
         got_own, got_other = gather_pair(pack(part, other, chips))
         inverse, col_gains, change = solve_update(
-            side, got_own, got_other, jac_own, jac_other, ordered[step], cols, order
+            side, got_own, got_other, stacked, ordered[step], cols, order
         )
         if step == STEPS - 1:
             change, *row_gains = together(change, *row_gains)

time: 268 us -> 245 us (0.914)
  Pallas kernels: 65.6 us -> 30.8 us
  blocking collectives: 124 us -> 137 us
  matrix products: 8.45 us -> 21.4 us
  waiting for transfers between devices: 19.8 us -> 11.2 us
  local copies, waits for them, and re-layouts: 6.61 us -> 2.93 us
    all_gather x0 -> x2, blocking collectives: none -> 41.2 us  [body(): stacked = lax.all_gather(chunk, 'grp', axis=0, tiled=True)]
    pallas_call x8 -> x1, Pallas kernels: 38.2 us -> 4.58 us  [prepare(): pl.pallas_call(prepare_kernel, grid=(parts,), out_shape=(f32(cols * local...]
    all_to_all x4 -> x2, blocking collectives: 57.9 us -> 28.4 us  [gather_pair(): lax.all_to_all(copies, 'grp', 0, 0, tiled=True, axis_index_groups=lanes)]
    dot_general x3 -> x9, matrix products: 8.45 us -> 21.4 us  [dot(): lax.dot_general(a, b, ((contract[0], contract[1]), ((), ())), precision=p...]
    ppermute x4 -> x2, starting transfers between devices: 16.1 us -> 9.4 us  [gather_pair(): other = lax.ppermute(own, 'grp', [(i, i ^ 1) for i in range(2 * count)])]
    all_to_all x2, waiting for transfers between devices: 11.6 us -> 5.11 us  [exchange(): return lax.all_to_all(chunks, axis, 0, 0, tiled=True)]
    ppermute x2, starting transfers between devices: 2.34 us -> 8.32 us  [swap(): return lax.ppermute(x, ('grp', 'atm'), pairs)]
    unnamed x20 -> x8, local copies, waits for them, and re-layouts: 3.37 us -> 0.65 us
  transfers between devices with their start and end apart: 11 -> 9, of which waited for: 5 -> 5; matrix products, arithmetic and copies ran while one was open for 4% -> 7% of each run, Pallas kernels for 21% -> 11%
where the time goes in v5:
time: 245 us; the launch traced here: 244 us
  blocking collectives  137 us (56%)
  Pallas kernels  30.8 us (13%)
  starting transfers between devices  24.8 us (10%)
  matrix products  21.4 us (9%)
  between operations  13.9 us (6%)
  waiting for transfers between devices  11.2 us (5%)
  local copies, waits for them, and re-layouts  2.93 us (1%)
    all_to_all x5, blocking collectives, exchange(): return lax.all_to_all(chunks, axis, 0, 0, tiled=True)  67 us
    all_gather x2, blocking collectives, body(): stacked = lax.all_gather(chunk, 'grp', axis=0, tiled=True)  41.2 us
    all_to_all x2, blocking collectives, gather_pair(): lax.all_to_all(copies, 'grp', 0, 0, tiled=True, axis_index_groups=lanes)  28.4 us
    dot_general x9, matrix products, dot(): lax.dot_general(a, b, ((contract[0], contract[1]), ((), ())), precision=p...  21.4 us
    pallas_call x2, Pallas kernels, solve_update(): pl.pallas_call(functools.partial(update_kernel, order), grid=(1,), out_sh...  15.3 us
    ppermute x2, starting transfers between devices, gather_pair(): other = lax.ppermute(own, 'grp', [(i, i ^ 1) for i in range(2 * count)])  9.4 us
    ppermute x2, starting transfers between devices, swap(): return lax.ppermute(x, ('grp', 'atm'), pairs)  8.32 us
    all_to_all x2, starting transfers between devices, exchange(): return lax.all_to_all(chunks, axis, 0, 0, tiled=True)  7 us
  transfers between devices with their start and end apart: 9, of which 5 were waited for; matrix products, arithmetic and copies ran while one was open for 7% of the time, Pallas kernels for 11%

profile of v5, /device:TPU:1, one launch (start us, length us, event | category | flops | bytes accessed | tf_op | source)
XLA Modules:
  0.0 243.7 jit_solution(11624775689115123925)
XLA Ops:
  7.2 0.0 all-gather.8.cloned.1.call-start
  7.2 2.7 %first_terms.1 = f32[16,8,1152]{2,1,0:T(8,128)} custom-call(f32[2,256,128]{2,1,0:T(8,128)} %atoms_ref.2, s32[2,256]{1,0:T(2,128)} %kinds_ref.3, s32[2,256]{1,0:T(2,128)} %member_ref.3, f32[128,128]{1,0:T(8,128)} %weights_ref.3, f32[1,128]{1,0:T(1,128)} %bitcast.45, f32[4,128]{1,0:T(4,128)} %readout_ref.3), custom_call_target="tpu_custom_call" | custom-call | tf_op jit(solution)/shard_map/first_terms/pallas_call | solution.py:172
  9.9 1.6 atoms_with_types.1
  11.5 0.0 all-gather.10.cloned.1.call-start
  11.6 18.9 %all_to_all.45 = f32[16,8,1152]{2,1,0:T(8,128)S(1)} all-to-all(f32[16,8,1152]{2,1,0:T(8,128)} %first_terms.1), channel_id=1, replica_groups=mesh['grp'=16,'atm'=16] {'atm'}, dimensions={0} | all-to-all | bytes 1179648 | tf_op jit(solution)/shard_map/all_to_all | solution.py:350
  30.5 23.4 %all_gather.24.energy_ref = f32[128,1152]{1,0:T(8,128)S(1)} all-gather(f32[8,1152]{1,0:T(8,128)S(1)} %reduce_sum.27), channel_id=1, replica_groups=mesh['grp'=16,'atm'=16] {'grp'}, dimensions={0}, use_global_device_ids=true | all-gather | bytes 626688 | tf_op jit(solution)/shard_map/all_gather | solution.py:433
  53.9 4.4 %convolution_bitcast_fusion = f32[16,8,1024]{2,1,0:T(8,128)S(1)} fusion(f32[1024,1024]{1,0:T(8,128)} %param.15, f32[128,1152]{1,0:T(8,128)S(1)} %all_gather.24.energy_ref), kind=kOutput, calls=%fused_computation.5 | convolution fusion | flops 805306368 | bytes 5242880 | tf_op jit(solution)/shard_map/dot_general | solution.py:23
  58.3 13.9 %all_to_all.46 = f32[16,8,1024]{2,1,0:T(8,128)S(1)} all-to-all(f32[16,8,1024]{2,1,0:T(8,128)S(1)} %convolution_bitcast_fusion), channel_id=1, replica_groups=mesh['grp'=16,'atm'=16] {'atm'}, dimensions={0} | all-to-all | bytes 1048576 | tf_op jit(solution)/shard_map/all_to_all | solution.py:350
  72.2 0.0 all-gather.8.cloned.1.call-done
  72.3 0.1 broadcast_in_dim.6
  72.4 0.6 pad_maximum_fusion
  73.0 5.4 %collective-permute-start = (f32[8,1024]{1,0:T(8,128)S(1)}, f32[8,1024]{1,0:T(8,128)S(1)}, u32[]{:S(2)}, u32[]{:S(2)}) collective-permute-start(f32[8,1024]{1,0:T(8,128)S(1)} %reduce_sum.28), channel_id=1, source_target_pairs={{10,0},{11,16},{8,32},{9,48},{14,64},{15,80},{12,96},{13,112},{2,1... | collective-permute-start | bytes 98312 | tf_op jit(solution)/shard_map/ppermute | solution.py:372
  78.5 4.6 %prepare_terms.1 = (f32[4096,128]{1,0:T(8,128)}, f32[72,4096]{1,0:T(8,128)}) custom-call(s32[1]{0:T(128)} %bitcast.4.col_ref, f32[16,264,128]{2,1,0:T(8,128)} %bitcast.40, f32[4,128]{1,0:T(4,128)} %readout_ref.3), custom_call_target="tpu_custom_call" | custom-call | tf_op jit(solution)/shard_map/prepare_terms/pallas_call | solution.py:211
  83.0 0.5 fusion.8
  83.6 9.9 %all_to_all.47.parts_ref = f32[16,8,128]{2,1,0:T(8,128)S(1)} all-to-all(f32[16,8,128]{2,1,0:T(8,128)S(1)} %broadcast_in_dim.7), channel_id=1, replica_groups=mesh['grp'=16,'atm'=16] {'atm'}, dimensions={0} | all-to-all | bytes 131072 | tf_op jit(solution)/shard_map/all_to_all | solution.py:350
  93.6 14.4 %all_to_all.48.own_ref = f32[8,8,1152]{2,1,0:T(8,128)S(1)} all-to-all(f32[8,8,1152]{2,1,0:T(8,128)S(1)} %pack_gains.2), channel_id=1, replica_groups={{0,32,64,96,128,160,192,224},{16,48,80,112,144,176,208,240},{1,33,65,97..., dimensions={0} | all-to-all | bytes 589824 | tf_op jit(solution)/shard_map/all_to_all | solution.py:360
  108.0 4.4 %collective-permute-start.1 = (f32[8,8,1152]{2,1,0:T(8,128)S(1)}, f32[8,8,1152]{2,1,0:T(8,128)S(1)}, u32[]{:S(2)}, u32[]{:S(2)}) collective-permute-start(f32[8,8,1152]{2,1,0:T(8,128)S(1)} %all_to_all.48.own_ref), channel_id=1, source_target_pairs={{0,16},{16,0},{32,48},{48,32},{64,80},{80,64},{96,112},{112,96},{1... | collective-permute-start | bytes 884744 | tf_op jit(solution)/shard_map/ppermute | solution.py:361
  112.4 1.2 collective-permute-done.1.other_ref
  113.6 7.7 %inverse_and_change.2 = (f32[128,128]{1,0:T(8,128)S(1)}, f32[128,1024]{1,0:T(8,128)S(1)}, f32[16,8,128]{2,1,0:T(8,128)}) custom-call(s32[1]{0:T(128)} %bitcast.side_ref, f32[8,8,1152]{2,1,0:T(8,128)S(1)} %all_to_all.48.own_ref, f32[8,8,1152]{2,1,0:T(8,128)S(1)} %collective-permute-done.1.other_ref, f32[128,1152]{1,0:T(8,128)S(1)} %all_gather.24.energy_ref, ...), custom_call_target="tpu_custom_call" | custom-call | tf_op jit(solution)/shard_map/inverse_and_change/pallas_call | solution.py:337
  121.3 3.5 %all-to-all-start.4 = ((f32[16,8,128]{2,1,0:T(8,128)}), f32[16,8,128]{2,1,0:T(8,128)S(1)}, u32[]{:S(2)}, u32[]{:S(2)}) async-start(f32[16,8,128]{2,1,0:T(8,128)} %get-tuple-element.31), calls=%async_computation.4 | async-start | bytes 131072 | tf_op jit(solution)/shard_map/all_to_all | solution.py:350
  124.8 0.0 all-gather.12.cloned.1.call-start
  124.9 1.4 broadcast_multiply_fusion
  126.3 5.0 %all-to-all-done.4.change_ref = f32[16,8,128]{2,1,0:T(8,128)S(1)} async-done(((f32[16,8,128]{2,1,0:T(8,128)}), f32[16,8,128]{2,1,0:T(8,128)S(1)}, u32[]{:S(2)}, u32[]{:S(2)}) %all-to-all-start.4) | async-done | bytes 65568 | tf_op jit(solution)/shard_map/all_to_all | solution.py:350
  131.3 0.6 copy-done.1
  131.9 6.6 %later_terms.1 = f32[1,8,1152]{2,1,0:T(8,128)} custom-call(f32[16,264,128]{2,1,0:T(8,128)} %bitcast.41, f32[4096,128]{1,0:T(8,128)} %get-tuple-element.27.vectors_ref, f32[72,4096]{1,0:T(8,128)} %get-tuple-element.28.masked_ref, f32[128,128]{1,0:T(8,128)} %weights_ref.3, f32[16,8,128]{2,1,0:T(8,128)} %copy-done.1, f32[1,128]{1,0:T(1,128)} %bitcast.46), custom_call_target="tpu_custom_call" | custom-call | tf_op jit(solution)/shard_map/later_terms/pallas_call | solution.py:264
  138.5 17.9 %all-gather.1 = f32[1,128,1152]{2,1,0:T(8,128)S(1)} all-gather(f32[1,8,1152]{2,1,0:T(8,128)} %later_terms.1), channel_id=3, replica_groups=mesh['grp'=16,'atm'=16] {'grp'}, dimensions={1}, use_global_device_ids=true | all-gather | bytes 626688 | tf_op jit(solution)/shard_map/all_gather | solution.py:433
  156.4 1.6 fusion.13
  158.0 0.0 all-gather.10.cloned.1.call-done
  158.0 1.6 fusion.17
  159.6 4.4 %fusion.1 = f32[16,8,1024]{2,1,0:T(8,128)S(1)} fusion(f32[128,1024]{1,0:T(8,128)S(1)} %fusion.17, f32[1024,1024]{1,0:T(8,128)} %param.15, f32[128,1152]{1,0:T(8,128)S(1)} %bitcast.37), kind=kOutput, calls=%fused_computation.3 | convolution fusion | flops 805568512 | bytes 5767168 | tf_op jit(solution)/shard_map/dot_general | solution.py:23
  164.0 13.8 %all_to_all.49 = f32[16,8,1024]{2,1,0:T(8,128)S(1)} all-to-all(f32[16,8,1024]{2,1,0:T(8,128)S(1)} %fusion.1), channel_id=1, replica_groups=mesh['grp'=16,'atm'=16] {'atm'}, dimensions={0} | all-to-all | bytes 1048576 | tf_op jit(solution)/shard_map/all_to_all | solution.py:350
  177.9 0.6 pad_maximum_fusion.1
  178.5 2.9 %collective-permute-start.2 = (f32[8,1024]{1,0:T(8,128)S(1)}, f32[8,1024]{1,0:T(8,128)S(1)}, u32[]{:S(2)}, u32[]{:S(2)}) collective-permute-start(f32[8,1024]{1,0:T(8,128)S(1)} %reduce_sum.29), channel_id=1, source_target_pairs={{10,0},{11,16},{8,32},{9,48},{14,64},{15,80},{12,96},{13,112},{2,1... | collective-permute-start | bytes 98312 | tf_op jit(solution)/shard_map/ppermute | solution.py:372
  181.4 4.7 %collective-permute-done.2.gains_ref = f32[8,1024]{1,0:T(8,128)S(1)} collective-permute-done((f32[8,1024]{1,0:T(8,128)S(1)}, f32[8,1024]{1,0:T(8,128)S(1)}, u32[]{:S(2)}, u32[]{:S(2)}) %collective-permute-start.2) | collective-permute-done | bytes 32800 | tf_op jit(solution)/shard_map/ppermute | solution.py:372
  186.1 0.5 fusion.11
  186.6 10.5 %all_to_all.50.parts_ref = f32[16,8,128]{2,1,0:T(8,128)S(1)} all-to-all(f32[16,8,128]{2,1,0:T(8,128)S(1)} %broadcast_in_dim.8), channel_id=1, replica_groups=mesh['grp'=16,'atm'=16] {'atm'}, dimensions={0} | all-to-all | bytes 131072 | tf_op jit(solution)/shard_map/all_to_all | solution.py:350
  197.1 13.9 %all_to_all.51.own_ref = f32[8,8,1152]{2,1,0:T(8,128)S(1)} all-to-all(f32[8,8,1152]{2,1,0:T(8,128)S(1)} %pack_gains.3), channel_id=1, replica_groups={{0,32,64,96,128,160,192,224},{16,48,80,112,144,176,208,240},{1,33,65,97..., dimensions={0} | all-to-all | bytes 589824 | tf_op jit(solution)/shard_map/all_to_all | solution.py:360
  211.1 5.0 %collective-permute-start.3 = (f32[8,8,1152]{2,1,0:T(8,128)S(1)}, f32[8,8,1152]{2,1,0:T(8,128)S(1)}, u32[]{:S(2)}, u32[]{:S(2)}) collective-permute-start(f32[8,8,1152]{2,1,0:T(8,128)S(1)} %all_to_all.51.own_ref), channel_id=1, source_target_pairs={{0,16},{16,0},{32,48},{48,32},{64,80},{80,64},{96,112},{112,96},{1... | collective-permute-start | bytes 884744 | tf_op jit(solution)/shard_map/ppermute | solution.py:361
  216.0 1.1 slice_bitcast_fusion.1
  217.1 0.1 collective-permute-done.3.other_ref
  217.2 7.7 %inverse_and_change.3 = (f32[128,128]{1,0:T(8,128)S(1)}, f32[128,1024]{1,0:T(8,128)S(1)}, f32[16,8,128]{2,1,0:T(8,128)}) custom-call(s32[1]{0:T(128)} %bitcast.side_ref, f32[8,8,1152]{2,1,0:T(8,128)S(1)} %all_to_all.51.own_ref, f32[8,8,1152]{2,1,0:T(8,128)S(1)} %collective-permute-done.3.other_ref, f32[128,1152]{1,0:T(8,128)S(1)} %bitcast.39, ...), custom_call_target="tpu_custom_call" | custom-call | tf_op jit(solution)/shard_map/inverse_and_change/pallas_call | solution.py:337
  224.9 0.6 convolution_multiply_fusion
  225.5 0.0 all-gather.12.cloned.1.call-done
  225.5 1.1 slice_bitcast_fusion
  226.6 3.5 %all-to-all-start.8 = ((f32[16,8,128]{2,1,0:T(8,128)}), f32[16,8,128]{2,1,0:T(8,128)S(1)}, u32[]{:S(2)}, u32[]{:S(2)}) async-start(f32[16,8,128]{2,1,0:T(8,128)} %get-tuple-element.39), calls=%async_computation.8 | async-start | bytes 131072 | tf_op jit(solution)/shard_map/all_to_all | solution.py:350
  230.1 6.3 %multiply_subtract_fusion = f32[1024,1024]{1,0:T(8,128)} fusion(f32[1024,1024]{1,0:T(8,128)} %param.15, f32[128,1024]{1,0:T(8,128)S(1)} %slice_bitcast_fusion, f32[128,1024]{1,0:T(8,128)S(1)} %slice_bitcast_fusion.1, f32[128,1024]{1,0:T(8,128)S(1)} %convolution_multiply_fusion, f32[128,1024]{1,0:T(8,128)S(1)} %get-tuple-element.42), kind=kOutput, calls=%fused_computation | convolution fusion | flops 1613234176 | bytes 10485760 | tf_op jit(solution)/shard_map/dot_general | solution.py:23
  236.4 0.1 all-to-all-done.8
  236.6 0.6 bitcast_add_fusion
  (19 shorter events, 0.3 us)
Async XLA Ops:
  7.2 65.1 %all-gather.8.cloned.1.call-start = ((), (), s32[]{:S(2)}) async-start(), calls=%async_computation.9 | async-start | bytes 2297856 | tf_op jit(solution)/shard_map/all_gather | solution.py:404
  11.5 146.5 %all-gather.10.cloned.1.call-start = ((), (), s32[]{:S(2)}) async-start(), calls=%async_computation.10 | async-start | bytes 1114112 | tf_op jit(solution)/shard_map/all_gather | solution.py:377
  30.4 41.8 %copy-start.3 = (f32[2,128]{1,0:T(2,128)S(1)}, f32[2,128]{1,0:T(2,128)}, u32[]{:S(2)}) copy-start(f32[2,128]{1,0:T(2,128)} %param.11) | copy-start | bytes 3076
  73.0 10.0 %collective-permute-start = (f32[8,1024]{1,0:T(8,128)S(1)}, f32[8,1024]{1,0:T(8,128)S(1)}, u32[]{:S(2)}, u32[]{:S(2)}) collective-permute-start(f32[8,1024]{1,0:T(8,128)S(1)} %reduce_sum.28), channel_id=1, source_target_pairs={{10,0},{11,16},{8,32},{9,48},{14,64},{15,80},{12,96},{13,112},{2,1... | collective-permute-start | bytes 98312 | tf_op jit(solution)/shard_map/ppermute | solution.py:372
  108.0 5.6 %collective-permute-start.1 = (f32[8,8,1152]{2,1,0:T(8,128)S(1)}, f32[8,8,1152]{2,1,0:T(8,128)S(1)}, u32[]{:S(2)}, u32[]{:S(2)}) collective-permute-start(f32[8,8,1152]{2,1,0:T(8,128)S(1)} %all_to_all.48.own_ref), channel_id=1, source_target_pairs={{0,16},{16,0},{32,48},{48,32},{64,80},{80,64},{96,112},{112,96},{1... | collective-permute-start | bytes 884744 | tf_op jit(solution)/shard_map/ppermute | solution.py:361
  121.3 10.0 %all-to-all-start.4 = ((f32[16,8,128]{2,1,0:T(8,128)}), f32[16,8,128]{2,1,0:T(8,128)S(1)}, u32[]{:S(2)}, u32[]{:S(2)}) async-start(f32[16,8,128]{2,1,0:T(8,128)} %get-tuple-element.31), calls=%async_computation.4 | async-start | bytes 131072 | tf_op jit(solution)/shard_map/all_to_all | solution.py:350
  124.8 100.7 %all-gather.12.cloned.1.call-start = ((), (), s32[]{:S(2)}) async-start(), calls=%async_computation.11 | async-start | bytes 1114112 | tf_op jit(solution)/shard_map/all_gather | solution.py:377
  131.3 0.6 copy-start.1
  178.5 7.6 %collective-permute-start.2 = (f32[8,1024]{1,0:T(8,128)S(1)}, f32[8,1024]{1,0:T(8,128)S(1)}, u32[]{:S(2)}, u32[]{:S(2)}) collective-permute-start(f32[8,1024]{1,0:T(8,128)S(1)} %reduce_sum.29), channel_id=1, source_target_pairs={{10,0},{11,16},{8,32},{9,48},{14,64},{15,80},{12,96},{13,112},{2,1... | collective-permute-start | bytes 98312 | tf_op jit(solution)/shard_map/ppermute | solution.py:372
  211.1 6.2 %collective-permute-start.3 = (f32[8,8,1152]{2,1,0:T(8,128)S(1)}, f32[8,8,1152]{2,1,0:T(8,128)S(1)}, u32[]{:S(2)}, u32[]{:S(2)}) collective-permute-start(f32[8,8,1152]{2,1,0:T(8,128)S(1)} %all_to_all.51.own_ref), channel_id=1, source_target_pairs={{0,16},{16,0},{32,48},{48,32},{64,80},{80,64},{96,112},{112,96},{1... | collective-permute-start | bytes 884744 | tf_op jit(solution)/shard_map/ppermute | solution.py:361
  226.6 10.0 %all-to-all-start.8 = ((f32[16,8,128]{2,1,0:T(8,128)}), f32[16,8,128]{2,1,0:T(8,128)S(1)}, u32[]{:S(2)}, u32[]{:S(2)}) async-start(f32[16,8,128]{2,1,0:T(8,128)} %get-tuple-element.39), calls=%async_computation.8 | async-start | bytes 131072 | tf_op jit(solution)/shard_map/all_to_all | solution.py:350
  230.1 6.5 %copy-start = (f32[128,128]{1,0:T(8,128)S(1)}, f32[128,128]{1,0:T(8,128)}, u32[]{:S(2)}) copy-start(f32[128,128]{1,0:T(8,128)} %weights_ref.3) | copy-start | bytes 196612
  230.1 6.4 %copy-start.2 = (f32[16,8,128]{2,1,0:T(8,128)S(1)}, f32[16,8,128]{2,1,0:T(8,128)}, u32[]{:S(2)}) copy-start(f32[16,8,128]{2,1,0:T(8,128)} %copy-done.1) | copy-start | bytes 196612
Sparse Core Ops, SparseCore 0:
  11.6 52.9 all-gather.7
  73.1 45.4 all-gather.9
  178.7 41.6 all-gather.11

commit v6 on v5

--- a/solution.py
+++ b/solution.py
@@ -147,7 +147,18 @@
     return hidden * vectors, (1.0 - hidden * hidden) * vectors
 
 
-def first_kernel(atoms_ref, kinds_ref, member_ref, weights_ref, bias_ref, readout_ref, out_ref, turned, masked):
+def first_kernel(
+    atoms_ref, next_ref, kinds_ref, member_ref, weights_ref, bias_ref, readout_ref, out_ref, packed_ref, turned, masked
+):
+    local = next_ref.shape[0]
+    lines = local // FEATURES
+    packed_ref[:local, :] = next_ref[...]
+    packed_ref[local:, :] = jnp.zeros((packed_ref.shape[0] - local, FEATURES), jnp.float32)
+    for which, ref in enumerate((kinds_ref, member_ref)):
+        for u in range(lines):
+            values = ref[1:2, u * FEATURES : (u + 1) * FEATURES].astype(jnp.float32)
+            place = local + which * lines + u
+            packed_ref[place : place + 1, :] = values
     atoms = atoms_ref[...]
     vectors = vectors_of(kinds_ref[0:1, :], readout_ref[...])
     energy, slope = layer(atoms, weights_ref[...], bias_ref[...], vectors)
@@ -172,20 +183,25 @@
     return pl.pallas_call(
         first_kernel,
         grid=(1,),
-        out_shape=f32(cols, GROUP_LOCAL, width + FEATURES),
-        in_specs=[pl.BlockSpec((None, local, FEATURES), lambda n: (0, 0, 0))] + [whole()] * 5,
-        out_specs=whole(),
+        out_shape=(f32(cols, GROUP_LOCAL, width + FEATURES), f32(local + SUB, FEATURES)),
+        in_specs=[
+            pl.BlockSpec((None, local, FEATURES), lambda n: (0, 0, 0)),
+            pl.BlockSpec((None, local, FEATURES), lambda n: (1, 0, 0)),
+        ]
+        + [whole()] * 5,
+        out_specs=(whole(), whole()),
         scratch_shapes=[pltpu.VMEM((FEATURES, local), jnp.float32), pltpu.VMEM((SUB * FEATURES, local), jnp.float32)],
         compiler_params=params(63.9),
         name="first_terms",
-    )(atoms, kinds, member, weights, bias, readout)
-
-
-def prepare_kernel(col_ref, gathered_ref, readout_ref, vectors_ref, masked_ref, turned):
+    )(atoms, atoms, kinds, member, weights, bias, readout)
+
+
+def prepare_kernel(col_ref, gathered_ref, readout_ref, atoms_ref, vectors_ref, masked_ref, turned):
     blocks = gathered_ref.shape[0]
     local = vectors_ref.shape[0] // blocks
     lines = local // FEATURES
-    count = (masked_ref.shape[0] - GROUP_LOCAL) // GROUP_LOCAL
+    high_rows = (masked_ref.shape[0] - 2 * SUB) // 2
+    count = high_rows // GROUP_LOCAL
     first = pl.multiple_of(col_ref[0] * count, SUB)
     for block in range(blocks):
 
@@ -196,24 +212,35 @@
         here = slice(block * local, (block + 1) * local)
         vectors_ref[here, :] = vectors_of(row(local), readout_ref[...])
         group_hot = hot(row(local + lines), GROUP_LOCAL)
-        turned[block] = gathered_ref[block, :local, :].T
+        atoms = gathered_ref[block, :local, :]
+        high, low = split(atoms)
+        atoms_ref[here, :FEATURES] = high
+        atoms_ref[here, FEATURES:] = low
+        turned[block] = atoms.T
         part = turned[block, pl.ds(first, count), :]
-        for f in range(count):
-            masked_ref[SUB * f : SUB * f + SUB, here] = part[f : f + 1, :] * group_hot
-        masked_ref[SUB * count :, here] = group_hot
+        high, low = split(jnp.concatenate([part[f : f + 1, :] * group_hot for f in range(count)], axis=0))
+        masked_ref[:high_rows, here] = high
+        masked_ref[high_rows : 2 * high_rows, here] = low
+        pair = jnp.concatenate([group_hot, jnp.zeros_like(group_hot)], axis=0)
+        masked_ref[2 * high_rows :, here] = pair.astype(jnp.bfloat16)
+
+
+def bf16(*shape):
+    return jax.ShapeDtypeStruct(shape, jnp.bfloat16)
 
 
 def prepare(gathered, readout, col_index, local, count):
     cols, tall, _ = gathered.shape
-    lines = GROUP_LOCAL * (count + 1)
+    lines = 2 * GROUP_LOCAL * (count + 1)
     parts = 4
     each = cols // parts
     return pl.pallas_call(
         prepare_kernel,
         grid=(parts,),
-        out_shape=(f32(cols * local, FEATURES), f32(lines, cols * local)),
+        out_shape=(bf16(cols * local, 2 * FEATURES), f32(cols * local, FEATURES), bf16(lines, cols * local)),
         in_specs=[scalar(), pl.BlockSpec((each, tall, FEATURES), lambda n: (n, 0, 0)), whole()],
         out_specs=(
+            pl.BlockSpec((each * local, 2 * FEATURES), lambda n: (n, 0)),
             pl.BlockSpec((each * local, FEATURES), lambda n: (n, 0)),
             pl.BlockSpec((lines, each * local), lambda n: (0, n)),
         ),
@@ -223,61 +250,104 @@
     )(col_index, gathered, readout)
 
 
-def later_kernel(gathered_ref, vectors_ref, masked_ref, weights_ref, change_ref, bias_ref, out_ref, acc):
+def later_kernel(atoms_ref, vectors_ref, masked_ref, weights_ref, bias_ref, out_ref, acc):
     step = pl.program_id(0)
-    blocks = gathered_ref.shape[0]
-    local = vectors_ref.shape[0] // blocks
-    atoms = gathered_ref[:, :local, :].reshape(blocks * local, FEATURES)
-    weights = weights_ref[...] + change_ref[...].reshape(FEATURES, FEATURES)
-    energy, slope = layer(atoms, weights, bias_ref[...], vectors_ref[...])
-    split_row = acc.shape[0] - GROUP_LOCAL
-    grads = dot3(masked_ref[:split_row, :], slope)
-    energies = dot3(masked_ref[split_row:, :], energy)
+    rows = masked_ref.shape[0] - 2 * SUB
+    w_high, w_low = split(weights_ref[...])
+    table = jnp.concatenate(
+        [jnp.concatenate([w_high, w_low], axis=1), jnp.concatenate([w_high, jnp.zeros_like(w_low)], axis=1)], axis=0
+    )
+    preact = jnp.dot(atoms_ref[...], table, preferred_element_type=jnp.float32)
+    hidden = jnp.tanh(preact[:, :FEATURES] + preact[:, FEATURES:] + bias_ref[...])
+    vectors = vectors_ref[...]
+    slope = jnp.concatenate(split((1.0 - hidden * hidden) * vectors), axis=1)
+    energy = jnp.concatenate(split(hidden * vectors), axis=1)
+    grads = jnp.dot(masked_ref[:rows, :], slope, preferred_element_type=jnp.float32)
+    energies = jnp.dot(masked_ref[rows:, :], energy, preferred_element_type=jnp.float32)
 
     @pl.when(step == 0)
     def _():
-        acc[:split_row, :] = grads
-        acc[split_row:, :] = energies
+        acc[:rows, :] = grads
+        acc[rows:, :] = energies
 
     @pl.when(step > 0)
     def _():
-        acc[:split_row, :] += grads
-        acc[split_row:, :] += energies
+        acc[:rows, :] += grads
+        acc[rows:, :] += energies
 
     @pl.when(step == pl.num_programs(0) - 1)
     def _():
-        total_energy = jnp.sum(acc[split_row:, :], axis=1, keepdims=True)
-        total_energy = jnp.broadcast_to(total_energy, (GROUP_LOCAL, FEATURES))
-        for copy in range(out_ref.shape[0]):
-            for f in range(split_row // SUB):
-                out_ref[copy, :, f * FEATURES : (f + 1) * FEATURES] = acc[SUB * f : SUB * f + SUB, :]
-            out_ref[copy, :, split_row // SUB * FEATURES :] = total_energy
-
-
-def later_terms(gathered, vectors, masked, weights, change, bias, copies):
-    cols, tall, _ = gathered.shape
+        both = acc[:, :FEATURES] + acc[:, FEATURES:]
+        high_rows = rows // 2
+        grads = both[:high_rows] + both[high_rows:rows]
+        for f in range(high_rows // SUB):
+            out_ref[:, f * FEATURES : (f + 1) * FEATURES] = grads[SUB * f : SUB * f + SUB]
+        total_energy = jnp.sum(both[rows : rows + SUB], axis=1, keepdims=True)
+        out_ref[:, high_rows // SUB * FEATURES :] = jnp.broadcast_to(total_energy, (GROUP_LOCAL, FEATURES))
+
+
+def later_terms(terms, weights, bias):
+    atoms, vectors, masked = terms
     parts = 4
-    local = vectors.shape[0] // cols
-    lines = masked.shape[0]
-    width = (lines // GROUP_LOCAL - 1) * FEATURES
-    each = cols // parts
+    lines, count = masked.shape
+    width = (lines // (2 * GROUP_LOCAL) - 1) * FEATURES
+    each = count // parts
     return pl.pallas_call(
         later_kernel,
         grid=(parts,),
-        out_shape=f32(copies, GROUP_LOCAL, width + FEATURES),
+        out_shape=f32(GROUP_LOCAL, width + FEATURES),
         in_specs=[
-            pl.BlockSpec((each, tall, FEATURES), lambda n: (n, 0, 0)),
-            pl.BlockSpec((each * local, FEATURES), lambda n: (n, 0)),
-            pl.BlockSpec((lines, each * local), lambda n: (0, n)),
-            whole(),
+            pl.BlockSpec((each, 2 * FEATURES), lambda n: (n, 0)),
+            pl.BlockSpec((each, FEATURES), lambda n: (n, 0)),
+            pl.BlockSpec((lines, each), lambda n: (0, n)),
             whole(),
             whole(),
         ],
         out_specs=whole(),
-        scratch_shapes=[pltpu.VMEM((lines, FEATURES), jnp.float32)],
+        scratch_shapes=[pltpu.VMEM((lines, 2 * FEATURES), jnp.float32)],
         compiler_params=params(63),
         name="later_terms",
-    )(gathered, vectors, masked, weights, change, bias)
+    )(atoms, vectors, masked, weights, bias)
+
+
+def downdate_kernel(cov_ref, first_ref, second_ref, scaled_ref, inverse_ref, gains_ref, out_ref, high, low):
+    groups = scaled_ref.shape[0]
+
+    @pl.when(pl.program_id(0) == 0)
+    def _():
+        fresh = dot3(inverse_ref[...], gains_ref[...]) * (1.0 / forget_rate)
+        for place, value in ((0, scaled_ref[...] * (1.0 / forget_rate**2)), (groups, fresh)):
+            value_high, value_low = split(value)
+            high[place : place + groups, :] = value_high
+            low[place : place + groups, :] = value_low
+
+    def rows(ref):
+        return ref[:, :GROUP_LOCAL, :].reshape(groups, ref.shape[2])
+
+    left_high, left_low = split(jnp.concatenate([rows(first_ref), rows(second_ref)], axis=0).T)
+
+    def one(x, y):
+        return jnp.dot(x, y[...], preferred_element_type=jnp.float32)
+
+    change = one(left_high, high) + (one(left_high, low) + one(left_low, high))
+    out_ref[...] = cov_ref[...] * (1.0 / forget_rate**2) - change
+
+
+def downdate(cov, first, second, scaled, inverse, gains):
+    rows, width = cov.shape
+    part = 256
+    cols, tall, _ = first.shape
+    block = pl.BlockSpec((cols, tall, part), lambda n: (0, 0, n))
+    return pl.pallas_call(
+        downdate_kernel,
+        grid=(rows // part,),
+        out_shape=f32(rows, width),
+        in_specs=[pl.BlockSpec((part, width), lambda n: (n, 0)), block, block, whole(), whole(), whole()],
+        out_specs=pl.BlockSpec((part, width), lambda n: (n, 0)),
+        scratch_shapes=[pltpu.VMEM((2 * scaled.shape[0], width), jnp.bfloat16)] * 2,
+        compiler_params=params(60.1),
+        name="downdate",
+    )(cov, first, second, scaled, inverse, gains)
 
 
 def pack_kernel(parts_ref, gains_ref, out_ref):
@@ -374,34 +444,7 @@
 
 def gather_rows(own):
     twice = jnp.concatenate([own, own], axis=0)
-    got = lax.all_gather(twice, "atm", axis=0, tiled=False)
-    return got[:, : own.shape[0]].reshape(-1, own.shape[1])
-
-
-def gather_kernel(atoms_ref, kinds_ref, member_ref, out_ref):
-    local = atoms_ref.shape[0]
-    lines = local // FEATURES
-    out_ref[:local, :] = atoms_ref[...]
-    out_ref[local:, :] = jnp.zeros((out_ref.shape[0] - local, FEATURES), jnp.float32)
-    for which, ref in enumerate((kinds_ref, member_ref)):
-        for u in range(lines):
-            values = ref[1:2, u * FEATURES : (u + 1) * FEATURES].astype(jnp.float32)
-            place = local + which * lines + u
-            out_ref[place : place + 1, :] = values
-
-
-def gather_atoms(atoms, kinds, member):
-    local = atoms.shape[1]
-    packed = pl.pallas_call(
-        gather_kernel,
-        grid=(1,),
-        out_shape=f32(local + SUB, FEATURES),
-        in_specs=[pl.BlockSpec((None, local, FEATURES), lambda n: (1, 0, 0)), whole(), whole()],
-        out_specs=whole(),
-        compiler_params=params(63.9),
-        name="atoms_with_types",
-    )(atoms, kinds, member)
-    return lax.all_gather(packed, "atm", axis=0, tiled=False)
+    return lax.all_gather(twice, "atm", axis=0, tiled=False)
 
 
 def together(*values):
@@ -421,28 +464,29 @@
     chunk_of_row = [far_row(a, math.isqrt(rows)) for a in range(rows)]
     order = [chunk_of_row[2 * z + core] for core in range(2) for z in range(chips)]
     current = weights
-    row_gains, scaled = [], []
+    row_gains = []
     for step in range(STEPS):
         if step == 0:
-            chunks = first_terms(atoms, kinds, member, current, bias, readout, cols, width)
-            chunks, later = together(chunks, atoms)
-            gathered = gather_atoms(later, kinds, member)
+            chunks, packed = first_terms(atoms, kinds, member, current, bias, readout, cols, width)
+            gathered = lax.all_gather(packed, "atm", axis=0, tiled=False)
             chunk = exchange(chunks, "atm").sum(axis=0)
         else:
-            chunk = later_terms(gathered, vectors, masked, weights, change, bias, 1)[0]
+            chunk = later_terms(later, current, bias)
         stacked = lax.all_gather(chunk, "grp", axis=0, tiled=True)
         jac = stacked[:, :width]
         terms = dot(jac, covariance, ((1,), (1,)), three)
-        for gains, part in zip(row_gains, scaled):
-            terms = (terms - dot(dot(jac, part, ((1,), (1,)), precise), gains, ((1,), (0,)), precise)) / forget_rate
+        if step:
+            moved = dot(jac, scaled, ((1,), (1,)), three)
+            gains = row_gains[0][:, :GROUP_LOCAL].reshape(groups, width)
+            terms = (terms - dot(moved, gains, ((1,), (0,)), three)) / forget_rate
         own = exchange(terms.reshape(cols, groups // cols, width), "atm").sum(axis=0)
         if step == 0:
             own, gathered, ordered = together(own, gathered, ordered)
         row_gains.append(gather_rows(own))
         other = swap(own, chunk_of_row)
         if step == 0:
-            vectors, masked = prepare(gathered, readout, col_index, local, width // FEATURES)
-            other, vectors, masked = together(other, vectors, masked)
+            later = prepare(gathered, readout, col_index, local, width // FEATURES)
+            other, *later = together(other, *later)
         part = spread(dot(other, jac, ((1,), (1,)), precise), "atm")
         got_own, got_other = gather_pair(pack(part, other, chips))
         inverse, col_gains, change = solve_update(
@@ -452,10 +496,9 @@
             change, *row_gains = together(change, *row_gains)
         change = exchange(change, "atm")
         current = current + change.reshape(FEATURES, FEATURES)
-        scaled.append(dot(inverse, col_gains, ((1,), (0,)), precise))
-    left = jnp.concatenate(row_gains, axis=0)
-    right = jnp.concatenate([x / forget_rate ** (STEPS - i) for i, x in enumerate(scaled)], axis=0)
-    covar = covariance / forget_rate**STEPS - dot(left, right, ((0,), (0,)), three)
+        if step == 0:
+            scaled = dot(inverse, col_gains, ((1,), (0,)), precise)
+    covar = downdate(covariance, *row_gains, scaled, inverse, col_gains)
     return (covar, current)
 
 

time: 245 us -> 241 us (0.984)
  blocking collectives: 137 us -> 122 us
  waiting for transfers between devices: 11.2 us -> 24.2 us
  matrix products: 21.4 us -> 13 us
  Pallas kernels: 30.8 us -> 36 us
    all_to_all x5 -> x4, blocking collectives: 67 us -> 53.3 us  [exchange(): return lax.all_to_all(chunks, axis, 0, 0, tiled=True)]
    all_to_all x2 -> x3, waiting for transfers between devices: 5.11 us -> 17 us  [exchange(): return lax.all_to_all(chunks, axis, 0, 0, tiled=True)]
    dot_general x9 -> x7, matrix products: 21.4 us -> 13 us  [dot(): lax.dot_general(a, b, ((contract[0], contract[1]), ((), ())), precision=p...]
    pallas_call x4, Pallas kernels: 15.5 us -> 20.6 us  [the longest x1 7.39 us: downdate(): pl.pallas_call(downdate_kernel, grid=(rows // part,), out_shape=f32(rows,...]
    all_to_all x2 -> x3, starting transfers between devices: 7 us -> 10.7 us  [exchange(): return lax.all_to_all(chunks, axis, 0, 0, tiled=True)]
  transfers between devices with their start and end apart: 9 -> 10, of which waited for: 5 -> 5; matrix products, arithmetic and copies ran while one was open for 7% -> 4% of each run, Pallas kernels for 11% -> 14%
where the time goes in v6:
time: 241 us; the launch traced here: 240 us
  blocking collectives  122 us (51%)
  Pallas kernels  36 us (15%)
  starting transfers between devices  27.1 us (11%)
  waiting for transfers between devices  24.2 us (10%)
  between operations  13.9 us (6%)
  matrix products  13 us (5%)
  other arithmetic  2.64 us (1%)
    all_to_all x4, blocking collectives, exchange(): return lax.all_to_all(chunks, axis, 0, 0, tiled=True)  53.3 us
    all_gather x2, blocking collectives, body(): stacked = lax.all_gather(chunk, 'grp', axis=0, tiled=True)  41.3 us
    all_to_all x2, blocking collectives, gather_pair(): lax.all_to_all(copies, 'grp', 0, 0, tiled=True, axis_index_groups=lanes)  27.4 us
    all_to_all x3, waiting for transfers between devices, exchange(): return lax.all_to_all(chunks, axis, 0, 0, tiled=True)  17 us
    pallas_call x2, Pallas kernels, solve_update(): pl.pallas_call(functools.partial(update_kernel, order), grid=(1,), out_sh...  15.3 us
    dot_general x7, matrix products, dot(): lax.dot_general(a, b, ((contract[0], contract[1]), ((), ())), precision=p...  13 us
    all_to_all x3, starting transfers between devices, exchange(): return lax.all_to_all(chunks, axis, 0, 0, tiled=True)  10.7 us
    ppermute x2, starting transfers between devices, gather_pair(): other = lax.ppermute(own, 'grp', [(i, i ^ 1) for i in range(2 * count)])  9.33 us
  transfers between devices with their start and end apart: 10, of which 5 were waited for; matrix products, arithmetic and copies ran while one was open for 4% of the time, Pallas kernels for 14%

profile of v6, /device:TPU:1, one launch (start us, length us, event | category | flops | bytes accessed | tf_op | source)
XLA Modules:
  0.0 240.5 jit_solution(6874606750602191565)
XLA Ops:
  7.2 0.0 all-gather.7.cloned.1.call-start
  7.2 2.8 %first_terms.1 = (f32[16,8,1152]{2,1,0:T(8,128)}, f32[264,128]{1,0:T(8,128)}) custom-call(f32[2,256,128]{2,1,0:T(8,128)} %next_ref.1, f32[2,256,128]{2,1,0:T(8,128)} %next_ref.1, s32[2,256]{1,0:T(2,128)} %kinds_ref.1, s32[2,256]{1,0:T(2,128)} %member_ref.1, f32[128,128]{1,0:T(8,128)} %weights_ref.1, f32[1,128]{1,0:T(1,128)} %bitcast.33, f32[4,128]{1,0:T(4,128)} %readout_ref.3), custom_call_target="tpu_custom_call" | custom-call | tf_op jit(solution)/shard_map/first_terms/pallas_call | solution.py:183
  10.0 0.0 all-gather.7.cloned.1.call-update
  10.0 18.9 %all_to_all.45 = f32[16,8,1152]{2,1,0:T(8,128)S(1)} all-to-all(f32[16,8,1152]{2,1,0:T(8,128)} %get-tuple-element.23), channel_id=1, replica_groups=mesh['grp'=16,'atm'=16] {'atm'}, dimensions={0} | all-to-all | bytes 1179648 | tf_op jit(solution)/shard_map/all_to_all | solution.py:420
  28.9 23.4 %all_gather.24.energy_ref = f32[128,1152]{1,0:T(8,128)S(1)} all-gather(f32[8,1152]{1,0:T(8,128)S(1)} %reduce_sum.27), channel_id=1, replica_groups=mesh['grp'=16,'atm'=16] {'grp'}, dimensions={0}, use_global_device_ids=true | all-gather | bytes 626688 | tf_op jit(solution)/shard_map/all_gather | solution.py:475
  52.3 5.2 %convolution_bitcast_fusion = f32[16,8,1024]{2,1,0:T(8,128)} fusion(f32[1024,1024]{1,0:T(8,128)} %cov_ref.1, f32[128,1152]{1,0:T(8,128)S(1)} %all_gather.24.energy_ref), kind=kOutput, calls=%fused_computation.3 | convolution fusion | flops 805306368 | bytes 5242880 | tf_op jit(solution)/shard_map/dot_general | solution.py:23
  57.5 3.7 %all-to-all-start.1 = ((f32[16,8,1024]{2,1,0:T(8,128)}), f32[16,8,1024]{2,1,0:T(8,128)S(1)}, u32[]{:S(2)}, u32[]{:S(2)}) async-start(f32[16,8,1024]{2,1,0:T(8,128)} %convolution_bitcast_fusion), calls=%async_computation.1 | async-start | bytes 1048576 | tf_op jit(solution)/shard_map/all_to_all | solution.py:420
  61.2 0.0 all-gather.9.cloned.1.call-start
  61.3 11.1 %all-to-all-done.1 = f32[16,8,1024]{2,1,0:T(8,128)S(1)} async-done(((f32[16,8,1024]{2,1,0:T(8,128)}), f32[16,8,1024]{2,1,0:T(8,128)S(1)}, u32[]{:S(2)}, u32[]{:S(2)}) %all-to-all-start.1) | async-done | bytes 524320 | tf_op jit(solution)/shard_map/all_to_all | solution.py:420
  72.4 0.0 all-gather.7.cloned.1.call-done
  72.5 0.1 broadcast_in_dim.6
  72.6 4.4 %collective-permute-start = (f32[8,1024]{1,0:T(8,128)S(1)}, f32[8,1024]{1,0:T(8,128)S(1)}, u32[]{:S(2)}, u32[]{:S(2)}) collective-permute-start(f32[8,1024]{1,0:T(8,128)S(1)} %reduce_sum.28), channel_id=1, source_target_pairs={{10,0},{11,16},{8,32},{9,48},{14,64},{15,80},{12,96},{13,112},{2,1... | collective-permute-start | bytes 98312 | tf_op jit(solution)/shard_map/ppermute | solution.py:442
  77.0 0.6 pad_maximum_fusion
  77.6 0.0 all-gather.9.cloned.1.call-update
  77.6 4.9 %prepare_terms.1 = (bf16[4096,256]{1,0:T(8,128)(2,1)}, f32[4096,128]{1,0:T(8,128)}, bf16[144,4096]{1,0:T(8,128)(2,1)}) custom-call(s32[1]{0:T(128)} %bitcast.4.col_ref, f32[16,264,128]{2,1,0:T(8,128)} %bitcast.31, f32[4,128]{1,0:T(4,128)} %readout_ref.3), custom_call_target="tpu_custom_call" | custom-call | tf_op jit(solution)/shard_map/prepare_terms/pallas_call | solution.py:237
  82.5 0.5 fusion.3
  83.0 10.2 %all_to_all.46.parts_ref = f32[16,8,128]{2,1,0:T(8,128)S(1)} all-to-all(f32[16,8,128]{2,1,0:T(8,128)S(1)} %broadcast_in_dim.7), channel_id=1, replica_groups=mesh['grp'=16,'atm'=16] {'atm'}, dimensions={0} | all-to-all | bytes 131072 | tf_op jit(solution)/shard_map/all_to_all | solution.py:420
  93.3 13.5 %all_to_all.47.own_ref = f32[8,8,1152]{2,1,0:T(8,128)S(1)} all-to-all(f32[8,8,1152]{2,1,0:T(8,128)S(1)} %pack_gains.2), channel_id=1, replica_groups={{0,32,64,96,128,160,192,224},{16,48,80,112,144,176,208,240},{1,33,65,97..., dimensions={0} | all-to-all | bytes 589824 | tf_op jit(solution)/shard_map/all_to_all | solution.py:430
  106.8 4.3 %collective-permute-start.1 = (f32[8,8,1152]{2,1,0:T(8,128)S(1)}, f32[8,8,1152]{2,1,0:T(8,128)S(1)}, u32[]{:S(2)}, u32[]{:S(2)}) collective-permute-start(f32[8,8,1152]{2,1,0:T(8,128)S(1)} %all_to_all.47.own_ref), channel_id=1, source_target_pairs={{0,16},{16,0},{32,48},{48,32},{64,80},{80,64},{96,112},{112,96},{1... | collective-permute-start | bytes 884744 | tf_op jit(solution)/shard_map/ppermute | solution.py:431
  111.2 1.2 collective-permute-done.1.other_ref
  112.4 7.7 %inverse_and_change.2 = (f32[128,128]{1,0:T(8,128)S(1)}, f32[128,1024]{1,0:T(8,128)S(1)}, f32[16,8,128]{2,1,0:T(8,128)}) custom-call(s32[1]{0:T(128)} %bitcast.side_ref, f32[8,8,1152]{2,1,0:T(8,128)S(1)} %all_to_all.47.own_ref, f32[8,8,1152]{2,1,0:T(8,128)S(1)} %collective-permute-done.1.other_ref, f32[128,1152]{1,0:T(8,128)S(1)} %all_gather.24.energy_ref, ...), custom_call_target="tpu_custom_call" | custom-call | tf_op jit(solution)/shard_map/inverse_and_change/pallas_call | solution.py:407
  120.0 3.5 %all-to-all-start.4 = ((f32[16,8,128]{2,1,0:T(8,128)}), f32[16,8,128]{2,1,0:T(8,128)S(1)}, u32[]{:S(2)}, u32[]{:S(2)}) async-start(f32[16,8,128]{2,1,0:T(8,128)} %get-tuple-element.35), calls=%async_computation.4 | async-start | bytes 131072 | tf_op jit(solution)/shard_map/all_to_all | solution.py:420
  123.5 0.0 all-gather.11.cloned.1.call-start
  123.6 0.6 fusion.11.scaled_ref
  124.2 5.8 %all-to-all-done.4 = f32[16,8,128]{2,1,0:T(8,128)S(1)} async-done(((f32[16,8,128]{2,1,0:T(8,128)}), f32[16,8,128]{2,1,0:T(8,128)S(1)}, u32[]{:S(2)}, u32[]{:S(2)}) %all-to-all-start.4) | async-done | bytes 65568 | tf_op jit(solution)/shard_map/all_to_all | solution.py:420
  130.0 0.6 bitcast_add_fusion.1.weights_ref
  130.6 5.6 %later_terms.1 = f32[8,1152]{1,0:T(8,128)} custom-call(bf16[4096,256]{1,0:T(8,128)(2,1)} %get-tuple-element.30.atoms_ref, f32[4096,128]{1,0:T(8,128)} %get-tuple-element.31.vectors_ref, bf16[144,4096]{1,0:T(8,128)(2,1)} %get-tuple-element.32.masked_ref, f32[128,128]{1,0:T(8,128)} %bitcast_add_fusion.1.weights_ref, f32[1,128]{1,0:T(1,128)} %bitcast.34), custom_call_target="tpu_custom_call" | custom-call | tf_op jit(solution)/shard_map/later_terms/pallas_call | solution.py:295
  136.2 17.9 %all_gather.27.energy_ref = f32[128,1152]{1,0:T(8,128)S(1)} all-gather(f32[8,1152]{1,0:T(8,128)} %later_terms.1), channel_id=1, replica_groups=mesh['grp'=16,'atm'=16] {'grp'}, dimensions={0}, use_global_device_ids=true | all-gather | bytes 626688 | tf_op jit(solution)/shard_map/all_gather | solution.py:475
  154.1 0.4 fusion.8
  154.5 0.0 all-gather.9.cloned.1.call-done
  154.5 1.4 fusion.2
  156.0 4.4 %fusion.1 = f32[16,8,1024]{2,1,0:T(8,128)S(1)} fusion(f32[128,1024]{1,0:T(8,128)S(1)} %fusion.2, f32[1024,1024]{1,0:T(8,128)} %cov_ref.1, f32[128,1152]{1,0:T(8,128)S(1)} %all_gather.27.energy_ref), kind=kOutput, calls=%fused_computation.2 | convolution fusion | flops 805568512 | bytes 5767168 | tf_op jit(solution)/shard_map/dot_general | solution.py:23
  160.4 13.8 %all_to_all.48 = f32[16,8,1024]{2,1,0:T(8,128)S(1)} all-to-all(f32[16,8,1024]{2,1,0:T(8,128)S(1)} %fusion.1), channel_id=1, replica_groups=mesh['grp'=16,'atm'=16] {'atm'}, dimensions={0} | all-to-all | bytes 1048576 | tf_op jit(solution)/shard_map/all_to_all | solution.py:420
  174.2 0.6 pad_maximum_fusion.1
  174.9 0.0 all-gather.11.cloned.1.call-update
  174.9 2.6 %collective-permute-start.2 = (f32[8,1024]{1,0:T(8,128)S(1)}, f32[8,1024]{1,0:T(8,128)S(1)}, u32[]{:S(2)}, u32[]{:S(2)}) collective-permute-start(f32[8,1024]{1,0:T(8,128)S(1)} %reduce_sum.29), channel_id=1, source_target_pairs={{10,0},{11,16},{8,32},{9,48},{14,64},{15,80},{12,96},{13,112},{2,1... | collective-permute-start | bytes 98312 | tf_op jit(solution)/shard_map/ppermute | solution.py:442
  177.5 4.8 %collective-permute-done.2.gains_ref = f32[8,1024]{1,0:T(8,128)S(1)} collective-permute-done((f32[8,1024]{1,0:T(8,128)S(1)}, f32[8,1024]{1,0:T(8,128)S(1)}, u32[]{:S(2)}, u32[]{:S(2)}) %collective-permute-start.2) | collective-permute-done | bytes 32800 | tf_op jit(solution)/shard_map/ppermute | solution.py:442
  182.2 0.5 fusion.6
  182.8 10.5 %all_to_all.49.parts_ref = f32[16,8,128]{2,1,0:T(8,128)S(1)} all-to-all(f32[16,8,128]{2,1,0:T(8,128)S(1)} %broadcast_in_dim.8), channel_id=1, replica_groups=mesh['grp'=16,'atm'=16] {'atm'}, dimensions={0} | all-to-all | bytes 131072 | tf_op jit(solution)/shard_map/all_to_all | solution.py:420
  193.2 13.8 %all_to_all.50.own_ref = f32[8,8,1152]{2,1,0:T(8,128)S(1)} all-to-all(f32[8,8,1152]{2,1,0:T(8,128)S(1)} %pack_gains.3), channel_id=1, replica_groups={{0,32,64,96,128,160,192,224},{16,48,80,112,144,176,208,240},{1,33,65,97..., dimensions={0} | all-to-all | bytes 589824 | tf_op jit(solution)/shard_map/all_to_all | solution.py:430
  207.1 5.0 %collective-permute-start.3 = (f32[8,8,1152]{2,1,0:T(8,128)S(1)}, f32[8,8,1152]{2,1,0:T(8,128)S(1)}, u32[]{:S(2)}, u32[]{:S(2)}) collective-permute-start(f32[8,8,1152]{2,1,0:T(8,128)S(1)} %all_to_all.50.own_ref), channel_id=1, source_target_pairs={{0,16},{16,0},{32,48},{48,32},{64,80},{80,64},{96,112},{112,96},{1... | collective-permute-start | bytes 884744 | tf_op jit(solution)/shard_map/ppermute | solution.py:431
  212.1 1.2 collective-permute-done.3.other_ref
  213.3 7.7 %inverse_and_change.3 = (f32[128,128]{1,0:T(8,128)S(1)}, f32[128,1024]{1,0:T(8,128)S(1)}, f32[16,8,128]{2,1,0:T(8,128)}) custom-call(s32[1]{0:T(128)} %bitcast.side_ref, f32[8,8,1152]{2,1,0:T(8,128)S(1)} %all_to_all.50.own_ref, f32[8,8,1152]{2,1,0:T(8,128)S(1)} %collective-permute-done.3.other_ref, f32[128,1152]{1,0:T(8,128)S(1)} %all_gather.27.energy_ref, ...), custom_call_target="tpu_custom_call" | custom-call | tf_op jit(solution)/shard_map/inverse_and_change/pallas_call | solution.py:407
  221.0 0.8 copy-done
  221.8 0.6 copy-done.1
  222.4 3.5 %all-to-all-start.8 = ((f32[16,8,128]{2,1,0:T(8,128)}), f32[16,8,128]{2,1,0:T(8,128)S(1)}, u32[]{:S(2)}, u32[]{:S(2)}) async-start(f32[16,8,128]{2,1,0:T(8,128)} %get-tuple-element.43), calls=%async_computation.8 | async-start | bytes 131072 | tf_op jit(solution)/shard_map/all_to_all | solution.py:420
  225.9 7.4 %downdate.1 = f32[1024,1024]{1,0:T(8,128)} custom-call(f32[1024,1024]{1,0:T(8,128)} %cov_ref.1, f32[16,16,1024]{2,1,0:T(8,128)} %bitcast.30, f32[16,16,1024]{2,1,0:T(8,128)} %bitcast.32, f32[128,1024]{1,0:T(8,128)} %copy-done.2, f32[128,128]{1,0:T(8,128)} %copy-done.1, f32[128,1024]{1,0:T(8,128)} %copy-done), custom_call_target="tpu_custom_call" | custom-call | tf_op jit(solution)/shard_map/downdate/pallas_call | solution.py:341
  233.3 0.6 bitcast_add_fusion
  (21 shorter events, 0.2 us)
Async XLA Ops:
  7.2 65.3 %all-gather.7.cloned.1.call-start = ((), (), s32[]{:S(2)}) async-start(), calls=%async_computation.9 | async-start | bytes 2297856 | tf_op jit(solution)/shard_map/all_gather | solution.py:471
  28.9 43.6 %copy-start.5 = (f32[2,128]{1,0:T(2,128)S(1)}, f32[2,128]{1,0:T(2,128)}, u32[]{:S(2)}) copy-start(f32[2,128]{1,0:T(2,128)} %param.11) | copy-start | bytes 3076
  57.5 72.5 %copy-start.4 = (f32[128,128]{1,0:T(8,128)S(1)}, f32[128,128]{1,0:T(8,128)}, u32[]{:S(2)}) copy-start(f32[128,128]{1,0:T(8,128)} %weights_ref.1) | copy-start | bytes 196612
  57.5 14.9 %all-to-all-start.1 = ((f32[16,8,1024]{2,1,0:T(8,128)}), f32[16,8,1024]{2,1,0:T(8,128)S(1)}, u32[]{:S(2)}, u32[]{:S(2)}) async-start(f32[16,8,1024]{2,1,0:T(8,128)} %convolution_bitcast_fusion), calls=%async_computation.1 | async-start | bytes 1048576 | tf_op jit(solution)/shard_map/all_to_all | solution.py:420
  61.2 93.3 %all-gather.9.cloned.1.call-start = ((), (), s32[]{:S(2)}) async-start(), calls=%async_computation.10 | async-start | bytes 1114112 | tf_op jit(solution)/shard_map/all_gather | solution.py:447
  72.6 9.9 %collective-permute-start = (f32[8,1024]{1,0:T(8,128)S(1)}, f32[8,1024]{1,0:T(8,128)S(1)}, u32[]{:S(2)}, u32[]{:S(2)}) collective-permute-start(f32[8,1024]{1,0:T(8,128)S(1)} %reduce_sum.28), channel_id=1, source_target_pairs={{10,0},{11,16},{8,32},{9,48},{14,64},{15,80},{12,96},{13,112},{2,1... | collective-permute-start | bytes 98312 | tf_op jit(solution)/shard_map/ppermute | solution.py:442
  106.8 5.5 %collective-permute-start.1 = (f32[8,8,1152]{2,1,0:T(8,128)S(1)}, f32[8,8,1152]{2,1,0:T(8,128)S(1)}, u32[]{:S(2)}, u32[]{:S(2)}) collective-permute-start(f32[8,8,1152]{2,1,0:T(8,128)S(1)} %all_to_all.47.own_ref), channel_id=1, source_target_pairs={{0,16},{16,0},{32,48},{48,32},{64,80},{80,64},{96,112},{112,96},{1... | collective-permute-start | bytes 884744 | tf_op jit(solution)/shard_map/ppermute | solution.py:431
  120.0 9.9 %all-to-all-start.4 = ((f32[16,8,128]{2,1,0:T(8,128)}), f32[16,8,128]{2,1,0:T(8,128)S(1)}, u32[]{:S(2)}, u32[]{:S(2)}) async-start(f32[16,8,128]{2,1,0:T(8,128)} %get-tuple-element.35), calls=%async_computation.4 | async-start | bytes 131072 | tf_op jit(solution)/shard_map/all_to_all | solution.py:420
  123.5 98.9 %all-gather.11.cloned.1.call-start = ((), (), s32[]{:S(2)}) async-start(), calls=%async_computation.11 | async-start | bytes 1114112 | tf_op jit(solution)/shard_map/all_gather | solution.py:447
  124.2 31.8 %copy-start.2 = (f32[128,1024]{1,0:T(8,128)}, f32[128,1024]{1,0:T(8,128)S(1)}, u32[]{:S(2)}) copy-start(f32[128,1024]{1,0:T(8,128)S(1)} %fusion.11.scaled_ref) | copy-start | bytes 1572868
  174.9 7.4 %collective-permute-start.2 = (f32[8,1024]{1,0:T(8,128)S(1)}, f32[8,1024]{1,0:T(8,128)S(1)}, u32[]{:S(2)}, u32[]{:S(2)}) collective-permute-start(f32[8,1024]{1,0:T(8,128)S(1)} %reduce_sum.29), channel_id=1, source_target_pairs={{10,0},{11,16},{8,32},{9,48},{14,64},{15,80},{12,96},{13,112},{2,1... | collective-permute-start | bytes 98312 | tf_op jit(solution)/shard_map/ppermute | solution.py:442
  207.1 6.2 %collective-permute-start.3 = (f32[8,8,1152]{2,1,0:T(8,128)S(1)}, f32[8,8,1152]{2,1,0:T(8,128)S(1)}, u32[]{:S(2)}, u32[]{:S(2)}) collective-permute-start(f32[8,8,1152]{2,1,0:T(8,128)S(1)} %all_to_all.50.own_ref), channel_id=1, source_target_pairs={{0,16},{16,0},{32,48},{48,32},{64,80},{80,64},{96,112},{112,96},{1... | collective-permute-start | bytes 884744 | tf_op jit(solution)/shard_map/ppermute | solution.py:431
  221.0 0.8 copy-start
  221.8 0.6 copy-start.1
  222.4 10.9 %all-to-all-start.8 = ((f32[16,8,128]{2,1,0:T(8,128)}), f32[16,8,128]{2,1,0:T(8,128)S(1)}, u32[]{:S(2)}, u32[]{:S(2)}) async-start(f32[16,8,128]{2,1,0:T(8,128)} %get-tuple-element.43), calls=%async_computation.8 | async-start | bytes 131072 | tf_op jit(solution)/shard_map/all_to_all | solution.py:420
  225.9 7.4 %copy-start.3 = (f32[128,128]{1,0:T(8,128)S(1)}, f32[128,128]{1,0:T(8,128)}, u32[]{:S(2)}) copy-start(f32[128,128]{1,0:T(8,128)} %bitcast_add_fusion.1.weights_ref) | copy-start | bytes 196612
Sparse Core Ops, SparseCore 0:
  10.5 52.9 all-gather.6
  77.8 41.9 all-gather.8
  175.0 41.6 all-gather.10

commit v7 on v6

--- a/solution.py
+++ b/solution.py
@@ -310,44 +310,47 @@
     )(atoms, vectors, masked, weights, bias)
 
 
-def downdate_kernel(cov_ref, first_ref, second_ref, scaled_ref, inverse_ref, gains_ref, out_ref, high, low):
-    groups = scaled_ref.shape[0]
+def downdate_kernel(scale, fresh, cov_ref, rows_ref, *rest):
+    out_ref, table = rest[-2:]
+    groups = table.shape[0] // 3
 
     @pl.when(pl.program_id(0) == 0)
     def _():
-        fresh = dot3(inverse_ref[...], gains_ref[...]) * (1.0 / forget_rate)
-        for place, value in ((0, scaled_ref[...] * (1.0 / forget_rate**2)), (groups, fresh)):
-            value_high, value_low = split(value)
-            high[place : place + groups, :] = value_high
-            low[place : place + groups, :] = value_low
-
-    def rows(ref):
-        return ref[:, :GROUP_LOCAL, :].reshape(groups, ref.shape[2])
-
-    left_high, left_low = split(jnp.concatenate([rows(first_ref), rows(second_ref)], axis=0).T)
-
-    def one(x, y):
-        return jnp.dot(x, y[...], preferred_element_type=jnp.float32)
-
-    change = one(left_high, high) + (one(left_high, low) + one(left_low, high))
-    out_ref[...] = cov_ref[...] * (1.0 / forget_rate**2) - change
-
-
-def downdate(cov, first, second, scaled, inverse, gains):
+        if fresh:
+            right = dot3(rest[0][...], rest[1][...]) * (1.0 / forget_rate)
+        else:
+            right = rest[0][...] * (1.0 / forget_rate**2)
+        high, low = split(right)
+        table[:groups, :] = high
+        table[groups : 2 * groups, :] = high
+        table[2 * groups :, :] = low
+
+    left = rows_ref[:, :GROUP_LOCAL, :].reshape(groups, rows_ref.shape[2]).T
+    high, low = split(left)
+    change = jnp.dot(jnp.concatenate([high, low], axis=1), table[: 2 * groups, :], preferred_element_type=jnp.float32)
+    change = change + jnp.dot(high, table[2 * groups :, :], preferred_element_type=jnp.float32)
+    cov = cov_ref[...]
+    out_ref[...] = (cov * scale if scale != 1.0 else cov) - change
+
+
+def downdate(cov, gathered_rows, right, scale):
     rows, width = cov.shape
     part = 256
-    cols, tall, _ = first.shape
-    block = pl.BlockSpec((cols, tall, part), lambda n: (0, 0, n))
+    cols, tall, _ = gathered_rows.shape
     return pl.pallas_call(
-        downdate_kernel,
+        functools.partial(downdate_kernel, scale, len(right) == 2),
         grid=(rows // part,),
         out_shape=f32(rows, width),
-        in_specs=[pl.BlockSpec((part, width), lambda n: (n, 0)), block, block, whole(), whole(), whole()],
+        in_specs=[
+            pl.BlockSpec((part, width), lambda n: (n, 0)),
+            pl.BlockSpec((cols, tall, part), lambda n: (0, 0, n)),
+        ]
+        + [whole()] * len(right),
         out_specs=pl.BlockSpec((part, width), lambda n: (n, 0)),
-        scratch_shapes=[pltpu.VMEM((2 * scaled.shape[0], width), jnp.bfloat16)] * 2,
-        compiler_params=params(60.1),
+        scratch_shapes=[pltpu.VMEM((3 * GROUP_LOCAL * cols, width), jnp.bfloat16)],
+        compiler_params=params(16 if len(right) == 2 else 60.1),
         name="downdate",
-    )(cov, first, second, scaled, inverse, gains)
+    )(cov, gathered_rows, *right)
 
 
 def pack_kernel(parts_ref, gains_ref, out_ref):
@@ -391,7 +394,7 @@
     coefficient = jnp.broadcast_to(jnp.sum(total(weighted), axis=0, keepdims=True), (SUB, n))
     gains = jnp.concatenate([both[p, :, :width] for p in places], axis=0)
     gains_ref[...] = gains
-    moved = exact(coefficient, gains)
+    moved = dot3(coefficient, gains)
     sub = lax.broadcasted_iota(jnp.int32, (SUB, FEATURES), 0)
     change = moved[:, :FEATURES]
     for r in range(1, width // FEATURES):
@@ -480,7 +483,10 @@
             gains = row_gains[0][:, :GROUP_LOCAL].reshape(groups, width)
             terms = (terms - dot(moved, gains, ((1,), (0,)), three)) / forget_rate
         own = exchange(terms.reshape(cols, groups // cols, width), "atm").sum(axis=0)
-        if step == 0:
+        if step:
+            base = downdate(covariance, row_gains[0], (scaled,), 1.0 / forget_rate**2)
+            own, base = together(own, base)
+        else:
             own, gathered, ordered = together(own, gathered, ordered)
         row_gains.append(gather_rows(own))
         other = swap(own, chunk_of_row)
@@ -493,12 +499,12 @@
             side, got_own, got_other, stacked, ordered[step], cols, order
         )
         if step == STEPS - 1:
-            change, *row_gains = together(change, *row_gains)
+            change, row_gains[1] = together(change, row_gains[1])
         change = exchange(change, "atm")
         current = current + change.reshape(FEATURES, FEATURES)
         if step == 0:
             scaled = dot(inverse, col_gains, ((1,), (0,)), precise)
-    covar = downdate(covariance, *row_gains, scaled, inverse, col_gains)
+    covar = downdate(base, row_gains[1], (inverse, col_gains), 1.0)
     return (covar, current)
 
 

time: 241 us -> 242 us (level)
  blocking collectives: 122 us -> 109 us
  waiting for transfers between devices: 24.2 us -> 29.3 us
  Pallas kernels: 36 us -> 38.9 us
  starting transfers between devices: 27.1 us -> 30 us
    all_to_all x4 -> x3, blocking collectives: 53.3 us -> 39.5 us  [exchange(): return lax.all_to_all(chunks, axis, 0, 0, tiled=True)]
    all_to_all x3 -> x4, waiting for transfers between devices: 17 us -> 21.8 us  [exchange(): return lax.all_to_all(chunks, axis, 0, 0, tiled=True)]
    all_to_all x3 -> x4, starting transfers between devices: 10.7 us -> 14.3 us  [exchange(): return lax.all_to_all(chunks, axis, 0, 0, tiled=True)]
    pallas_call x1 -> x2, Pallas kernels: 7.39 us -> 10.2 us  [downdate(): pl.pallas_call(functools.partial(downdate_kernel, scale, len(right) == 2)...]
  transfers between devices with their start and end apart: 10 -> 11, of which waited for: 5 -> 6; matrix products, arithmetic and copies ran while one was open for 4% -> 4% of each run, Pallas kernels for 14% -> 15%
where the time goes in v7:
time: 242 us; the launch traced here: 241 us
  blocking collectives  109 us (45%)
  Pallas kernels  38.9 us (16%)
  starting transfers between devices  30 us (12%)
  waiting for transfers between devices  29.3 us (12%)
  between operations  13.9 us (6%)
  matrix products  13.8 us (6%)
  local copies, waits for them, and re-layouts  3.56 us (1%)
  other arithmetic  2.64 us (1%)
    all_gather x2, blocking collectives, body(): stacked = lax.all_gather(chunk, 'grp', axis=0, tiled=True)  41.3 us
    all_to_all x3, blocking collectives, exchange(): return lax.all_to_all(chunks, axis, 0, 0, tiled=True)  39.5 us
    all_to_all x2, blocking collectives, gather_pair(): lax.all_to_all(copies, 'grp', 0, 0, tiled=True, axis_index_groups=lanes)  27.8 us
    all_to_all x4, waiting for transfers between devices, exchange(): return lax.all_to_all(chunks, axis, 0, 0, tiled=True)  21.8 us
    pallas_call x2, Pallas kernels, solve_update(): pl.pallas_call(functools.partial(update_kernel, order), grid=(1,), out_sh...  15.4 us
    all_to_all x4, starting transfers between devices, exchange(): return lax.all_to_all(chunks, axis, 0, 0, tiled=True)  14.3 us
    dot_general x7, matrix products, dot(): lax.dot_general(a, b, ((contract[0], contract[1]), ((), ())), precision=p...  13.8 us
    pallas_call x2, Pallas kernels, downdate(): pl.pallas_call(functools.partial(downdate_kernel, scale, len(right) == 2)...  10.2 us
  transfers between devices with their start and end apart: 11, of which 6 were waited for; matrix products, arithmetic and copies ran while one was open for 4% of the time, Pallas kernels for 15%

profile of v7, /device:TPU:1, one launch (start us, length us, event | category | flops | bytes accessed | tf_op | source)
XLA Modules:
  0.0 240.6 jit_solution(7673735464392036558)
XLA Ops:
  7.2 0.0 all-gather.7.cloned.1.call-start
  7.2 2.8 %first_terms.1 = (f32[16,8,1152]{2,1,0:T(8,128)}, f32[264,128]{1,0:T(8,128)}) custom-call(f32[2,256,128]{2,1,0:T(8,128)} %next_ref.1, f32[2,256,128]{2,1,0:T(8,128)} %next_ref.1, s32[2,256]{1,0:T(2,128)} %kinds_ref.1, s32[2,256]{1,0:T(2,128)} %member_ref.1, f32[128,128]{1,0:T(8,128)} %weights_ref.1, f32[1,128]{1,0:T(1,128)} %bitcast.33, f32[4,128]{1,0:T(4,128)} %readout_ref.3), custom_call_target="tpu_custom_call" | custom-call | tf_op jit(solution)/shard_map/first_terms/pallas_call | solution.py:183
  10.0 0.0 all-gather.7.cloned.1.call-update
  10.0 18.9 %all_to_all.45 = f32[16,8,1152]{2,1,0:T(8,128)S(1)} all-to-all(f32[16,8,1152]{2,1,0:T(8,128)} %get-tuple-element.24), channel_id=1, replica_groups=mesh['grp'=16,'atm'=16] {'atm'}, dimensions={0} | all-to-all | bytes 1179648 | tf_op jit(solution)/shard_map/all_to_all | solution.py:423
  28.9 23.4 %all_gather.24.energy_ref = f32[128,1152]{1,0:T(8,128)S(1)} all-gather(f32[8,1152]{1,0:T(8,128)S(1)} %reduce_sum.27), channel_id=1, replica_groups=mesh['grp'=16,'atm'=16] {'grp'}, dimensions={0}, use_global_device_ids=true | all-gather | bytes 626688 | tf_op jit(solution)/shard_map/all_gather | solution.py:478
  52.3 5.2 %convolution_bitcast_fusion = f32[16,8,1024]{2,1,0:T(8,128)} fusion(f32[1024,1024]{1,0:T(8,128)} %cov_ref.1, f32[128,1152]{1,0:T(8,128)S(1)} %all_gather.24.energy_ref), kind=kOutput, calls=%fused_computation.3 | convolution fusion | flops 805306368 | bytes 5242880 | tf_op jit(solution)/shard_map/dot_general | solution.py:23
  57.5 3.7 %all-to-all-start.1 = ((f32[16,8,1024]{2,1,0:T(8,128)}), f32[16,8,1024]{2,1,0:T(8,128)S(1)}, u32[]{:S(2)}, u32[]{:S(2)}) async-start(f32[16,8,1024]{2,1,0:T(8,128)} %convolution_bitcast_fusion), calls=%async_computation.1 | async-start | bytes 1048576 | tf_op jit(solution)/shard_map/all_to_all | solution.py:423
  61.2 0.0 all-gather.9.cloned.1.call-start
  61.3 11.1 %all-to-all-done.1 = f32[16,8,1024]{2,1,0:T(8,128)S(1)} async-done(((f32[16,8,1024]{2,1,0:T(8,128)}), f32[16,8,1024]{2,1,0:T(8,128)S(1)}, u32[]{:S(2)}, u32[]{:S(2)}) %all-to-all-start.1) | async-done | bytes 524320 | tf_op jit(solution)/shard_map/all_to_all | solution.py:423
  72.4 0.0 all-gather.7.cloned.1.call-done
  72.5 0.1 broadcast_in_dim.6
  72.6 4.4 %collective-permute-start = (f32[8,1024]{1,0:T(8,128)S(1)}, f32[8,1024]{1,0:T(8,128)S(1)}, u32[]{:S(2)}, u32[]{:S(2)}) collective-permute-start(f32[8,1024]{1,0:T(8,128)S(1)} %reduce_sum.28), channel_id=1, source_target_pairs={{10,0},{11,16},{8,32},{9,48},{14,64},{15,80},{12,96},{13,112},{2,1... | collective-permute-start | bytes 98312 | tf_op jit(solution)/shard_map/ppermute | solution.py:445
  77.0 0.6 pad_maximum_fusion
  77.6 4.9 %prepare_terms.1 = (bf16[4096,256]{1,0:T(8,128)(2,1)}, f32[4096,128]{1,0:T(8,128)}, bf16[144,4096]{1,0:T(8,128)(2,1)}) custom-call(s32[1]{0:T(128)} %bitcast.3.col_ref, f32[16,264,128]{2,1,0:T(8,128)} %bitcast.32, f32[4,128]{1,0:T(4,128)} %readout_ref.3), custom_call_target="tpu_custom_call" | custom-call | tf_op jit(solution)/shard_map/prepare_terms/pallas_call | solution.py:237
  82.5 0.5 fusion.3
  83.0 10.2 %all_to_all.46.parts_ref = f32[16,8,128]{2,1,0:T(8,128)S(1)} all-to-all(f32[16,8,128]{2,1,0:T(8,128)S(1)} %broadcast_in_dim.7), channel_id=1, replica_groups=mesh['grp'=16,'atm'=16] {'atm'}, dimensions={0} | all-to-all | bytes 131072 | tf_op jit(solution)/shard_map/all_to_all | solution.py:423
  93.3 13.5 %all_to_all.47.own_ref = f32[8,8,1152]{2,1,0:T(8,128)S(1)} all-to-all(f32[8,8,1152]{2,1,0:T(8,128)S(1)} %pack_gains.2), channel_id=1, replica_groups={{0,32,64,96,128,160,192,224},{16,48,80,112,144,176,208,240},{1,33,65,97..., dimensions={0} | all-to-all | bytes 589824 | tf_op jit(solution)/shard_map/all_to_all | solution.py:433
  106.8 4.3 %collective-permute-start.1 = (f32[8,8,1152]{2,1,0:T(8,128)S(1)}, f32[8,8,1152]{2,1,0:T(8,128)S(1)}, u32[]{:S(2)}, u32[]{:S(2)}) collective-permute-start(f32[8,8,1152]{2,1,0:T(8,128)S(1)} %all_to_all.47.own_ref), channel_id=1, source_target_pairs={{0,16},{16,0},{32,48},{48,32},{64,80},{80,64},{96,112},{112,96},{1... | collective-permute-start | bytes 884744 | tf_op jit(solution)/shard_map/ppermute | solution.py:434
  111.2 1.2 collective-permute-done.1.other_ref
  112.4 7.7 %inverse_and_change.2 = (f32[128,128]{1,0:T(8,128)S(1)}, f32[128,1024]{1,0:T(8,128)S(1)}, f32[16,8,128]{2,1,0:T(8,128)}) custom-call(s32[1]{0:T(128)} %bitcast.4.side_ref, f32[8,8,1152]{2,1,0:T(8,128)S(1)} %all_to_all.47.own_ref, f32[8,8,1152]{2,1,0:T(8,128)S(1)} %collective-permute-done.1.other_ref, f32[128,1152]{1,0:T(8,128)S(1)} %all_gather.24.energy_ref, ...), custom_call_target="tpu_custom_call" | custom-call | tf_op jit(solution)/shard_map/inverse_and_change/pallas_call | solution.py:410
  120.1 3.5 %all-to-all-start.4 = ((f32[16,8,128]{2,1,0:T(8,128)}), f32[16,8,128]{2,1,0:T(8,128)S(1)}, u32[]{:S(2)}, u32[]{:S(2)}) async-start(f32[16,8,128]{2,1,0:T(8,128)} %get-tuple-element.36), calls=%async_computation.4 | async-start | bytes 131072 | tf_op jit(solution)/shard_map/all_to_all | solution.py:423
  123.6 0.6 fusion.11.rest_0_
  124.2 5.9 %all-to-all-done.4 = f32[16,8,128]{2,1,0:T(8,128)S(1)} async-done(((f32[16,8,128]{2,1,0:T(8,128)}), f32[16,8,128]{2,1,0:T(8,128)S(1)}, u32[]{:S(2)}, u32[]{:S(2)}) %all-to-all-start.4) | async-done | bytes 65568 | tf_op jit(solution)/shard_map/all_to_all | solution.py:423
  130.0 0.6 bitcast_add_fusion.1.weights_ref
  130.6 5.6 %later_terms.1 = f32[8,1152]{1,0:T(8,128)} custom-call(bf16[4096,256]{1,0:T(8,128)(2,1)} %get-tuple-element.31.atoms_ref, f32[4096,128]{1,0:T(8,128)} %get-tuple-element.32.vectors_ref, bf16[144,4096]{1,0:T(8,128)(2,1)} %get-tuple-element.33.masked_ref, f32[128,128]{1,0:T(8,128)} %bitcast_add_fusion.1.weights_ref, f32[1,128]{1,0:T(1,128)} %bitcast.34), custom_call_target="tpu_custom_call" | custom-call | tf_op jit(solution)/shard_map/later_terms/pallas_call | solution.py:295
  136.3 17.9 %all_gather.27.energy_ref = f32[128,1152]{1,0:T(8,128)S(1)} all-gather(f32[8,1152]{1,0:T(8,128)} %later_terms.1), channel_id=1, replica_groups=mesh['grp'=16,'atm'=16] {'grp'}, dimensions={0}, use_global_device_ids=true | all-gather | bytes 626688 | tf_op jit(solution)/shard_map/all_gather | solution.py:478
  154.2 0.4 fusion.8
  154.5 0.0 all-gather.9.cloned.1.call-done
  154.6 1.4 fusion.2
  156.0 5.2 %fusion.1 = f32[16,8,1024]{2,1,0:T(8,128)} fusion(f32[128,1024]{1,0:T(8,128)S(1)} %fusion.2, f32[1024,1024]{1,0:T(8,128)} %cov_ref.1, f32[128,1152]{1,0:T(8,128)S(1)} %all_gather.27.energy_ref), kind=kOutput, calls=%fused_computation.2 | convolution fusion | flops 805568512 | bytes 5767168 | tf_op jit(solution)/shard_map/dot_general | solution.py:23
  161.2 3.6 %all-to-all-start.5 = ((f32[16,8,1024]{2,1,0:T(8,128)}), f32[16,8,1024]{2,1,0:T(8,128)S(1)}, u32[]{:S(2)}, u32[]{:S(2)}) async-start(f32[16,8,1024]{2,1,0:T(8,128)} %fusion.1), calls=%async_computation.5 | async-start | bytes 1048576 | tf_op jit(solution)/shard_map/all_to_all | solution.py:423
  164.8 0.0 all-gather.11.cloned.1.call-start
  164.8 6.4 %downdate.2.cov_ref = f32[1024,1024]{1,0:T(8,128)} custom-call(f32[1024,1024]{1,0:T(8,128)} %cov_ref.1, f32[16,16,1024]{2,1,0:T(8,128)} %bitcast.31, f32[128,1024]{1,0:T(8,128)} %copy-done.2), custom_call_target="tpu_custom_call" | custom-call | tf_op jit(solution)/shard_map/downdate/pallas_call | solution.py:340
  171.2 4.8 %all-to-all-done.5 = f32[16,8,1024]{2,1,0:T(8,128)S(1)} async-done(((f32[16,8,1024]{2,1,0:T(8,128)}), f32[16,8,1024]{2,1,0:T(8,128)S(1)}, u32[]{:S(2)}, u32[]{:S(2)}) %all-to-all-start.5) | async-done | bytes 524320 | tf_op jit(solution)/shard_map/all_to_all | solution.py:423
  176.0 0.6 pad_maximum_fusion.1
  176.7 2.3 collective-permute-start.2
  179.0 5.0 %collective-permute-done.2.gains_ref = f32[8,1024]{1,0:T(8,128)S(1)} collective-permute-done((f32[8,1024]{1,0:T(8,128)S(1)}, f32[8,1024]{1,0:T(8,128)S(1)}, u32[]{:S(2)}, u32[]{:S(2)}) %collective-permute-start.2) | collective-permute-done | bytes 32800 | tf_op jit(solution)/shard_map/ppermute | solution.py:445
  184.0 0.5 fusion.6
  184.5 10.4 %all_to_all.48.parts_ref = f32[16,8,128]{2,1,0:T(8,128)S(1)} all-to-all(f32[16,8,128]{2,1,0:T(8,128)S(1)} %broadcast_in_dim.8), channel_id=1, replica_groups=mesh['grp'=16,'atm'=16] {'atm'}, dimensions={0} | all-to-all | bytes 131072 | tf_op jit(solution)/shard_map/all_to_all | solution.py:423
  194.9 14.2 %all_to_all.49.own_ref = f32[8,8,1152]{2,1,0:T(8,128)S(1)} all-to-all(f32[8,8,1152]{2,1,0:T(8,128)S(1)} %pack_gains.3), channel_id=1, replica_groups={{0,32,64,96,128,160,192,224},{16,48,80,112,144,176,208,240},{1,33,65,97..., dimensions={0} | all-to-all | bytes 589824 | tf_op jit(solution)/shard_map/all_to_all | solution.py:433
  209.1 4.6 %collective-permute-start.3 = (f32[8,8,1152]{2,1,0:T(8,128)S(1)}, f32[8,8,1152]{2,1,0:T(8,128)S(1)}, u32[]{:S(2)}, u32[]{:S(2)}) collective-permute-start(f32[8,8,1152]{2,1,0:T(8,128)S(1)} %all_to_all.49.own_ref), channel_id=1, source_target_pairs={{0,16},{16,0},{32,48},{48,32},{64,80},{80,64},{96,112},{112,96},{1... | collective-permute-start | bytes 884744 | tf_op jit(solution)/shard_map/ppermute | solution.py:434
  213.8 1.2 collective-permute-done.3.other_ref
  215.0 7.7 %inverse_and_change.3 = (f32[128,128]{1,0:T(8,128)S(1)}, f32[128,1024]{1,0:T(8,128)S(1)}, f32[16,8,128]{2,1,0:T(8,128)}) custom-call(s32[1]{0:T(128)} %bitcast.4.side_ref, f32[8,8,1152]{2,1,0:T(8,128)S(1)} %all_to_all.49.own_ref, f32[8,8,1152]{2,1,0:T(8,128)S(1)} %collective-permute-done.3.other_ref, f32[128,1152]{1,0:T(8,128)S(1)} %all_gather.27.energy_ref, ...), custom_call_target="tpu_custom_call" | custom-call | tf_op jit(solution)/shard_map/inverse_and_change/pallas_call | solution.py:410
  222.7 3.5 %all-to-all-start.8 = ((f32[16,8,128]{2,1,0:T(8,128)}), f32[16,8,128]{2,1,0:T(8,128)S(1)}, u32[]{:S(2)}, u32[]{:S(2)}) async-start(f32[16,8,128]{2,1,0:T(8,128)} %get-tuple-element.45), calls=%async_computation.8 | async-start | bytes 131072 | tf_op jit(solution)/shard_map/all_to_all | solution.py:423
  226.2 2.2 copy-done
  228.4 1.2 copy-done.1
  229.6 3.9 %downdate.3 = f32[1024,1024]{1,0:T(8,128)} custom-call(f32[1024,1024]{1,0:T(8,128)S(1)} %copy-done, f32[16,16,1024]{2,1,0:T(8,128)S(1)} %bitcast.29, f32[128,128]{1,0:T(8,128)S(1)} %get-tuple-element.43.rest_0_, f32[128,1024]{1,0:T(8,128)S(1)} %get-tuple-element.44.rest_1_), custom_call_target="tpu_custom_call" | custom-call | tf_op jit(solution)/shard_map/downdate/pallas_call | solution.py:340
  233.4 0.6 bitcast_add_fusion
  (23 shorter events, 0.3 us)
Async XLA Ops:
  7.2 65.3 %all-gather.7.cloned.1.call-start = ((), (), s32[]{:S(2)}) async-start(), calls=%async_computation.9 | async-start | bytes 2297856 | tf_op jit(solution)/shard_map/all_gather | solution.py:474
  28.9 43.6 %copy-start.5 = (f32[2,128]{1,0:T(2,128)S(1)}, f32[2,128]{1,0:T(2,128)}, u32[]{:S(2)}) copy-start(f32[2,128]{1,0:T(2,128)} %param.11) | copy-start | bytes 3076
  57.5 72.5 %copy-start.4 = (f32[128,128]{1,0:T(8,128)S(1)}, f32[128,128]{1,0:T(8,128)}, u32[]{:S(2)}) copy-start(f32[128,128]{1,0:T(8,128)} %weights_ref.1) | copy-start | bytes 196612
  57.5 14.9 %all-to-all-start.1 = ((f32[16,8,1024]{2,1,0:T(8,128)}), f32[16,8,1024]{2,1,0:T(8,128)S(1)}, u32[]{:S(2)}, u32[]{:S(2)}) async-start(f32[16,8,1024]{2,1,0:T(8,128)} %convolution_bitcast_fusion), calls=%async_computation.1 | async-start | bytes 1048576 | tf_op jit(solution)/shard_map/all_to_all | solution.py:423
  61.2 93.4 %all-gather.9.cloned.1.call-start = ((), (), s32[]{:S(2)}) async-start(), calls=%async_computation.10 | async-start | bytes 1114112 | tf_op jit(solution)/shard_map/all_gather | solution.py:450
  72.6 9.9 %collective-permute-start = (f32[8,1024]{1,0:T(8,128)S(1)}, f32[8,1024]{1,0:T(8,128)S(1)}, u32[]{:S(2)}, u32[]{:S(2)}) collective-permute-start(f32[8,1024]{1,0:T(8,128)S(1)} %reduce_sum.28), channel_id=1, source_target_pairs={{10,0},{11,16},{8,32},{9,48},{14,64},{15,80},{12,96},{13,112},{2,1... | collective-permute-start | bytes 98312 | tf_op jit(solution)/shard_map/ppermute | solution.py:445
  106.8 5.5 %collective-permute-start.1 = (f32[8,8,1152]{2,1,0:T(8,128)S(1)}, f32[8,8,1152]{2,1,0:T(8,128)S(1)}, u32[]{:S(2)}, u32[]{:S(2)}) collective-permute-start(f32[8,8,1152]{2,1,0:T(8,128)S(1)} %all_to_all.47.own_ref), channel_id=1, source_target_pairs={{0,16},{16,0},{32,48},{48,32},{64,80},{80,64},{96,112},{112,96},{1... | collective-permute-start | bytes 884744 | tf_op jit(solution)/shard_map/ppermute | solution.py:434
  120.1 9.9 %all-to-all-start.4 = ((f32[16,8,128]{2,1,0:T(8,128)}), f32[16,8,128]{2,1,0:T(8,128)S(1)}, u32[]{:S(2)}, u32[]{:S(2)}) async-start(f32[16,8,128]{2,1,0:T(8,128)} %get-tuple-element.36), calls=%async_computation.4 | async-start | bytes 131072 | tf_op jit(solution)/shard_map/all_to_all | solution.py:423
  124.1 31.9 %copy-start.2 = (f32[128,1024]{1,0:T(8,128)}, f32[128,1024]{1,0:T(8,128)S(1)}, u32[]{:S(2)}) copy-start(f32[128,1024]{1,0:T(8,128)S(1)} %fusion.11.rest_0_) | copy-start | bytes 1572868
  161.2 14.8 %all-to-all-start.5 = ((f32[16,8,1024]{2,1,0:T(8,128)}), f32[16,8,1024]{2,1,0:T(8,128)S(1)}, u32[]{:S(2)}, u32[]{:S(2)}) async-start(f32[16,8,1024]{2,1,0:T(8,128)} %fusion.1), calls=%async_computation.5 | async-start | bytes 1048576 | tf_op jit(solution)/shard_map/all_to_all | solution.py:423
  164.8 57.9 %all-gather.11.cloned.1.call-start = ((), (), s32[]{:S(2)}) async-start(), calls=%async_computation.11 | async-start | bytes 1114112 | tf_op jit(solution)/shard_map/all_gather | solution.py:450
  176.7 7.3 %collective-permute-start.2 = (f32[8,1024]{1,0:T(8,128)S(1)}, f32[8,1024]{1,0:T(8,128)S(1)}, u32[]{:S(2)}, u32[]{:S(2)}) collective-permute-start(f32[8,1024]{1,0:T(8,128)S(1)} %reduce_sum.29), channel_id=1, source_target_pairs={{10,0},{11,16},{8,32},{9,48},{14,64},{15,80},{12,96},{13,112},{2,1... | collective-permute-start | bytes 98312 | tf_op jit(solution)/shard_map/ppermute | solution.py:445
  209.1 5.8 %collective-permute-start.3 = (f32[8,8,1152]{2,1,0:T(8,128)S(1)}, f32[8,8,1152]{2,1,0:T(8,128)S(1)}, u32[]{:S(2)}, u32[]{:S(2)}) collective-permute-start(f32[8,8,1152]{2,1,0:T(8,128)S(1)} %all_to_all.49.own_ref), channel_id=1, source_target_pairs={{0,16},{16,0},{32,48},{48,32},{64,80},{80,64},{96,112},{112,96},{1... | collective-permute-start | bytes 884744 | tf_op jit(solution)/shard_map/ppermute | solution.py:434
  222.7 10.8 %all-to-all-start.8 = ((f32[16,8,128]{2,1,0:T(8,128)}), f32[16,8,128]{2,1,0:T(8,128)S(1)}, u32[]{:S(2)}, u32[]{:S(2)}) async-start(f32[16,8,128]{2,1,0:T(8,128)} %get-tuple-element.45), calls=%async_computation.8 | async-start | bytes 131072 | tf_op jit(solution)/shard_map/all_to_all | solution.py:423
  226.2 2.2 copy-start
  228.4 1.2 copy-start.1
  229.6 3.9 %copy-start.3 = (f32[128,128]{1,0:T(8,128)S(1)}, f32[128,128]{1,0:T(8,128)}, u32[]{:S(2)}) copy-start(f32[128,128]{1,0:T(8,128)} %bitcast_add_fusion.1.weights_ref) | copy-start | bytes 196612
Sparse Core Ops, SparseCore 0:
  10.5 52.9 all-gather.6
  77.8 41.9 all-gather.8
  176.8 41.3 all-gather.10

commit v8 on v7

--- a/solution.py
+++ b/solution.py
@@ -348,7 +348,7 @@
         + [whole()] * len(right),
         out_specs=pl.BlockSpec((part, width), lambda n: (n, 0)),
         scratch_shapes=[pltpu.VMEM((3 * GROUP_LOCAL * cols, width), jnp.bfloat16)],
-        compiler_params=params(16 if len(right) == 2 else 60.1),
+        compiler_params=params(60.1),
         name="downdate",
     )(cov, gathered_rows, *right)
 
@@ -483,16 +483,16 @@
             gains = row_gains[0][:, :GROUP_LOCAL].reshape(groups, width)
             terms = (terms - dot(moved, gains, ((1,), (0,)), three)) / forget_rate
         own = exchange(terms.reshape(cols, groups // cols, width), "atm").sum(axis=0)
-        if step:
-            base = downdate(covariance, row_gains[0], (scaled,), 1.0 / forget_rate**2)
-            own, base = together(own, base)
-        else:
-            own, gathered, ordered = together(own, gathered, ordered)
+        if step == 0:
+            own, gathered = together(own, gathered)
         row_gains.append(gather_rows(own))
         other = swap(own, chunk_of_row)
         if step == 0:
             later = prepare(gathered, readout, col_index, local, width // FEATURES)
-            other, *later = together(other, *later)
+            other, ordered, *later = together(other, ordered, *later)
+        else:
+            base = downdate(covariance, row_gains[0], (scaled,), 1.0 / forget_rate**2)
+            other, base = together(other, base)
         part = spread(dot(other, jac, ((1,), (1,)), precise), "atm")
         got_own, got_other = gather_pair(pack(part, other, chips))
         inverse, col_gains, change = solve_update(

time: 242 us -> 242 us (level)
  blocking collectives: 109 us -> 123 us
  waiting for transfers between devices: 29.3 us -> 19.5 us
  starting transfers between devices: 30 us -> 26.2 us
  Pallas kernels: 38.9 us -> 41.4 us
    all_to_all x3 -> x4, blocking collectives: 39.5 us -> 54 us  [exchange(): return lax.all_to_all(chunks, axis, 0, 0, tiled=True)]
    ppermute x2, waiting for transfers between devices: 5.01 us -> 0.01 us  [swap(): return lax.ppermute(x, ('grp', 'atm'), pairs)]
    all_to_all x4 -> x3, waiting for transfers between devices: 21.8 us -> 17 us  [exchange(): return lax.all_to_all(chunks, axis, 0, 0, tiled=True)]
    all_to_all x4 -> x3, starting transfers between devices: 14.3 us -> 10.7 us  [exchange(): return lax.all_to_all(chunks, axis, 0, 0, tiled=True)]
    pallas_call x2, Pallas kernels: 10.2 us -> 12.7 us  [downdate(): pl.pallas_call(functools.partial(downdate_kernel, scale, len(right) == 2)...]
  transfers between devices with their start and end apart: 11 -> 10, of which waited for: 6 -> 5; matrix products, arithmetic and copies ran while one was open for 4% -> 4% of each run, Pallas kernels for 15% -> 16%
where the time goes in v8:
time: 242 us; the launch traced here: 241 us
  blocking collectives  123 us (51%)
  Pallas kernels  41.4 us (17%)
  starting transfers between devices  26.2 us (11%)
  waiting for transfers between devices  19.5 us (8%)
  between operations  13.9 us (6%)
  matrix products  13 us (5%)
  other arithmetic  2.64 us (1%)
    all_to_all x4, blocking collectives, exchange(): return lax.all_to_all(chunks, axis, 0, 0, tiled=True)  54 us
    all_gather x2, blocking collectives, body(): stacked = lax.all_gather(chunk, 'grp', axis=0, tiled=True)  41.3 us
    all_to_all x2, blocking collectives, gather_pair(): lax.all_to_all(copies, 'grp', 0, 0, tiled=True, axis_index_groups=lanes)  27.3 us
    all_to_all x3, waiting for transfers between devices, exchange(): return lax.all_to_all(chunks, axis, 0, 0, tiled=True)  17 us
    pallas_call x2, Pallas kernels, solve_update(): pl.pallas_call(functools.partial(update_kernel, order), grid=(1,), out_sh...  15.4 us
    dot_general x7, matrix products, dot(): lax.dot_general(a, b, ((contract[0], contract[1]), ((), ())), precision=p...  13 us
    pallas_call x2, Pallas kernels, downdate(): pl.pallas_call(functools.partial(downdate_kernel, scale, len(right) == 2)...  12.7 us
    all_to_all x3, starting transfers between devices, exchange(): return lax.all_to_all(chunks, axis, 0, 0, tiled=True)  10.7 us
  transfers between devices with their start and end apart: 10, of which 5 were waited for; matrix products, arithmetic and copies ran while one was open for 4% of the time, Pallas kernels for 16%

profile of v8, /device:TPU:1, one launch (start us, length us, event | category | flops | bytes accessed | tf_op | source)
XLA Modules:
  0.0 240.8 jit_solution(7492793077450517982)
XLA Ops:
  7.2 0.0 all-gather.7.cloned.1.call-start
  7.2 2.8 %first_terms.1 = (f32[16,8,1152]{2,1,0:T(8,128)}, f32[264,128]{1,0:T(8,128)}) custom-call(f32[2,256,128]{2,1,0:T(8,128)} %next_ref.1, f32[2,256,128]{2,1,0:T(8,128)} %next_ref.1, s32[2,256]{1,0:T(2,128)} %kinds_ref.1, s32[2,256]{1,0:T(2,128)} %member_ref.1, f32[128,128]{1,0:T(8,128)} %weights_ref.1, f32[1,128]{1,0:T(1,128)} %bitcast.33, f32[4,128]{1,0:T(4,128)} %readout_ref.3), custom_call_target="tpu_custom_call" | custom-call | tf_op jit(solution)/shard_map/first_terms/pallas_call | solution.py:183
  10.0 0.0 all-gather.7.cloned.1.call-update
  10.0 18.9 %all_to_all.45 = f32[16,8,1152]{2,1,0:T(8,128)S(1)} all-to-all(f32[16,8,1152]{2,1,0:T(8,128)} %get-tuple-element.24), channel_id=1, replica_groups=mesh['grp'=16,'atm'=16] {'atm'}, dimensions={0} | all-to-all | bytes 1179648 | tf_op jit(solution)/shard_map/all_to_all | solution.py:423
  28.9 23.4 %all_gather.24.energy_ref = f32[128,1152]{1,0:T(8,128)S(1)} all-gather(f32[8,1152]{1,0:T(8,128)S(1)} %reduce_sum.27), channel_id=1, replica_groups=mesh['grp'=16,'atm'=16] {'grp'}, dimensions={0}, use_global_device_ids=true | all-gather | bytes 626688 | tf_op jit(solution)/shard_map/all_gather | solution.py:478
  52.3 5.2 %convolution_bitcast_fusion = f32[16,8,1024]{2,1,0:T(8,128)} fusion(f32[1024,1024]{1,0:T(8,128)} %cov_ref.1, f32[128,1152]{1,0:T(8,128)S(1)} %all_gather.24.energy_ref), kind=kOutput, calls=%fused_computation.3 | convolution fusion | flops 805306368 | bytes 5242880 | tf_op jit(solution)/shard_map/dot_general | solution.py:23
  57.5 3.7 %all-to-all-start.1 = ((f32[16,8,1024]{2,1,0:T(8,128)}), f32[16,8,1024]{2,1,0:T(8,128)S(1)}, u32[]{:S(2)}, u32[]{:S(2)}) async-start(f32[16,8,1024]{2,1,0:T(8,128)} %convolution_bitcast_fusion), calls=%async_computation.1 | async-start | bytes 1048576 | tf_op jit(solution)/shard_map/all_to_all | solution.py:423
  61.2 0.0 all-gather.9.cloned.1.call-start
  61.3 11.2 %all-to-all-done.1 = f32[16,8,1024]{2,1,0:T(8,128)S(1)} async-done(((f32[16,8,1024]{2,1,0:T(8,128)}), f32[16,8,1024]{2,1,0:T(8,128)S(1)}, u32[]{:S(2)}, u32[]{:S(2)}) %all-to-all-start.1) | async-done | bytes 524320 | tf_op jit(solution)/shard_map/all_to_all | solution.py:423
  72.5 0.0 all-gather.7.cloned.1.call-done
  72.5 4.4 %collective-permute-start = (f32[8,1024]{1,0:T(8,128)S(1)}, f32[8,1024]{1,0:T(8,128)S(1)}, u32[]{:S(2)}, u32[]{:S(2)}) collective-permute-start(f32[8,1024]{1,0:T(8,128)S(1)} %reduce_sum.28), channel_id=1, source_target_pairs={{10,0},{11,16},{8,32},{9,48},{14,64},{15,80},{12,96},{13,112},{2,1... | collective-permute-start | bytes 98312 | tf_op jit(solution)/shard_map/ppermute | solution.py:445
  76.9 0.6 pad_maximum_fusion
  77.5 0.0 all-gather.9.cloned.1.call-update
  77.5 4.9 %prepare_terms.1 = (bf16[4096,256]{1,0:T(8,128)(2,1)}, f32[4096,128]{1,0:T(8,128)}, bf16[144,4096]{1,0:T(8,128)(2,1)}) custom-call(s32[1]{0:T(128)} %bitcast.3.col_ref, f32[16,264,128]{2,1,0:T(8,128)} %bitcast.31, f32[4,128]{1,0:T(4,128)} %readout_ref.3), custom_call_target="tpu_custom_call" | custom-call | tf_op jit(solution)/shard_map/prepare_terms/pallas_call | solution.py:237
  82.4 0.1 broadcast_in_dim.6
  82.5 0.5 fusion.3
  83.1 10.2 %all_to_all.46.parts_ref = f32[16,8,128]{2,1,0:T(8,128)S(1)} all-to-all(f32[16,8,128]{2,1,0:T(8,128)S(1)} %broadcast_in_dim.7), channel_id=1, replica_groups=mesh['grp'=16,'atm'=16] {'atm'}, dimensions={0} | all-to-all | bytes 131072 | tf_op jit(solution)/shard_map/all_to_all | solution.py:423
  93.3 13.5 %all_to_all.47.own_ref = f32[8,8,1152]{2,1,0:T(8,128)S(1)} all-to-all(f32[8,8,1152]{2,1,0:T(8,128)S(1)} %pack_gains.2), channel_id=1, replica_groups={{0,32,64,96,128,160,192,224},{16,48,80,112,144,176,208,240},{1,33,65,97..., dimensions={0} | all-to-all | bytes 589824 | tf_op jit(solution)/shard_map/all_to_all | solution.py:433
  106.8 4.3 %collective-permute-start.1 = (f32[8,8,1152]{2,1,0:T(8,128)S(1)}, f32[8,8,1152]{2,1,0:T(8,128)S(1)}, u32[]{:S(2)}, u32[]{:S(2)}) collective-permute-start(f32[8,8,1152]{2,1,0:T(8,128)S(1)} %all_to_all.47.own_ref), channel_id=1, source_target_pairs={{0,16},{16,0},{32,48},{48,32},{64,80},{80,64},{96,112},{112,96},{1... | collective-permute-start | bytes 884744 | tf_op jit(solution)/shard_map/ppermute | solution.py:434
  111.1 1.2 collective-permute-done.1.other_ref
  112.3 7.7 %inverse_and_change.2 = (f32[128,128]{1,0:T(8,128)S(1)}, f32[128,1024]{1,0:T(8,128)S(1)}, f32[16,8,128]{2,1,0:T(8,128)}) custom-call(s32[1]{0:T(128)} %bitcast.4.side_ref, f32[8,8,1152]{2,1,0:T(8,128)S(1)} %all_to_all.47.own_ref, f32[8,8,1152]{2,1,0:T(8,128)S(1)} %collective-permute-done.1.other_ref, f32[128,1152]{1,0:T(8,128)S(1)} %all_gather.24.energy_ref, ...), custom_call_target="tpu_custom_call" | custom-call | tf_op jit(solution)/shard_map/inverse_and_change/pallas_call | solution.py:410
  120.0 3.5 %all-to-all-start.4 = ((f32[16,8,128]{2,1,0:T(8,128)}), f32[16,8,128]{2,1,0:T(8,128)S(1)}, u32[]{:S(2)}, u32[]{:S(2)}) async-start(f32[16,8,128]{2,1,0:T(8,128)} %get-tuple-element.36), calls=%async_computation.4 | async-start | bytes 131072 | tf_op jit(solution)/shard_map/all_to_all | solution.py:423
  123.5 0.0 all-gather.11.cloned.1.call-start
  123.6 0.6 fusion.11.rest_0_
  124.2 5.8 %all-to-all-done.4 = f32[16,8,128]{2,1,0:T(8,128)S(1)} async-done(((f32[16,8,128]{2,1,0:T(8,128)}), f32[16,8,128]{2,1,0:T(8,128)S(1)}, u32[]{:S(2)}, u32[]{:S(2)}) %all-to-all-start.4) | async-done | bytes 65568 | tf_op jit(solution)/shard_map/all_to_all | solution.py:423
  130.0 0.6 bitcast_add_fusion.1.weights_ref
  130.6 5.6 %later_terms.1 = f32[8,1152]{1,0:T(8,128)} custom-call(bf16[4096,256]{1,0:T(8,128)(2,1)} %get-tuple-element.31.atoms_ref, f32[4096,128]{1,0:T(8,128)} %get-tuple-element.32.vectors_ref, bf16[144,4096]{1,0:T(8,128)(2,1)} %get-tuple-element.33.masked_ref, f32[128,128]{1,0:T(8,128)} %bitcast_add_fusion.1.weights_ref, f32[1,128]{1,0:T(1,128)} %bitcast.34), custom_call_target="tpu_custom_call" | custom-call | tf_op jit(solution)/shard_map/later_terms/pallas_call | solution.py:295
  136.2 17.9 %all_gather.27.energy_ref = f32[128,1152]{1,0:T(8,128)S(1)} all-gather(f32[8,1152]{1,0:T(8,128)} %later_terms.1), channel_id=1, replica_groups=mesh['grp'=16,'atm'=16] {'grp'}, dimensions={0}, use_global_device_ids=true | all-gather | bytes 626688 | tf_op jit(solution)/shard_map/all_gather | solution.py:478
  154.1 0.4 fusion.8
  154.5 0.0 all-gather.9.cloned.1.call-done
  154.5 1.4 fusion.2
  156.0 4.4 %fusion.1 = f32[16,8,1024]{2,1,0:T(8,128)S(1)} fusion(f32[128,1024]{1,0:T(8,128)S(1)} %fusion.2, f32[1024,1024]{1,0:T(8,128)} %cov_ref.1, f32[128,1152]{1,0:T(8,128)S(1)} %all_gather.27.energy_ref), kind=kOutput, calls=%fused_computation.2 | convolution fusion | flops 805568512 | bytes 5767168 | tf_op jit(solution)/shard_map/dot_general | solution.py:23
  160.4 13.8 %all_to_all.48 = f32[16,8,1024]{2,1,0:T(8,128)S(1)} all-to-all(f32[16,8,1024]{2,1,0:T(8,128)S(1)} %fusion.1), channel_id=1, replica_groups=mesh['grp'=16,'atm'=16] {'atm'}, dimensions={0} | all-to-all | bytes 1048576 | tf_op jit(solution)/shard_map/all_to_all | solution.py:423
  174.2 0.6 pad_maximum_fusion.1
  174.9 2.6 %collective-permute-start.2 = (f32[8,1024]{1,0:T(8,128)S(1)}, f32[8,1024]{1,0:T(8,128)S(1)}, u32[]{:S(2)}, u32[]{:S(2)}) collective-permute-start(f32[8,1024]{1,0:T(8,128)S(1)} %reduce_sum.29), channel_id=1, source_target_pairs={{10,0},{11,16},{8,32},{9,48},{14,64},{15,80},{12,96},{13,112},{2,1... | collective-permute-start | bytes 98312 | tf_op jit(solution)/shard_map/ppermute | solution.py:445
  177.5 6.4 %downdate.2.cov_ref = f32[1024,1024]{1,0:T(8,128)} custom-call(f32[1024,1024]{1,0:T(8,128)} %cov_ref.1, f32[16,16,1024]{2,1,0:T(8,128)} %bitcast.30, f32[128,1024]{1,0:T(8,128)} %copy-done.2), custom_call_target="tpu_custom_call" | custom-call | tf_op jit(solution)/shard_map/downdate/pallas_call | solution.py:340
  183.8 0.5 fusion.6
  184.4 11.1 %all_to_all.49.parts_ref = f32[16,8,128]{2,1,0:T(8,128)S(1)} all-to-all(f32[16,8,128]{2,1,0:T(8,128)S(1)} %broadcast_in_dim.8), channel_id=1, replica_groups=mesh['grp'=16,'atm'=16] {'atm'}, dimensions={0} | all-to-all | bytes 131072 | tf_op jit(solution)/shard_map/all_to_all | solution.py:423
  195.5 13.8 %all_to_all.50.own_ref = f32[8,8,1152]{2,1,0:T(8,128)S(1)} all-to-all(f32[8,8,1152]{2,1,0:T(8,128)S(1)} %pack_gains.3), channel_id=1, replica_groups={{0,32,64,96,128,160,192,224},{16,48,80,112,144,176,208,240},{1,33,65,97..., dimensions={0} | all-to-all | bytes 589824 | tf_op jit(solution)/shard_map/all_to_all | solution.py:433
  209.3 4.1 %collective-permute-start.3 = (f32[8,8,1152]{2,1,0:T(8,128)S(1)}, f32[8,8,1152]{2,1,0:T(8,128)S(1)}, u32[]{:S(2)}, u32[]{:S(2)}) collective-permute-start(f32[8,8,1152]{2,1,0:T(8,128)S(1)} %all_to_all.50.own_ref), channel_id=1, source_target_pairs={{0,16},{16,0},{32,48},{48,32},{64,80},{80,64},{96,112},{112,96},{1... | collective-permute-start | bytes 884744 | tf_op jit(solution)/shard_map/ppermute | solution.py:434
  213.4 1.2 collective-permute-done.3.other_ref
  214.6 7.7 %inverse_and_change.3 = (f32[128,128]{1,0:T(8,128)S(1)}, f32[128,1024]{1,0:T(8,128)S(1)}, f32[16,8,128]{2,1,0:T(8,128)}) custom-call(s32[1]{0:T(128)} %bitcast.4.side_ref, f32[8,8,1152]{2,1,0:T(8,128)S(1)} %all_to_all.50.own_ref, f32[8,8,1152]{2,1,0:T(8,128)S(1)} %collective-permute-done.3.other_ref, f32[128,1152]{1,0:T(8,128)S(1)} %all_gather.27.energy_ref, ...), custom_call_target="tpu_custom_call" | custom-call | tf_op jit(solution)/shard_map/inverse_and_change/pallas_call | solution.py:410
  222.3 0.8 copy-done
  223.1 0.6 copy-done.1
  223.7 3.5 %all-to-all-start.8 = ((f32[16,8,128]{2,1,0:T(8,128)}), f32[16,8,128]{2,1,0:T(8,128)S(1)}, u32[]{:S(2)}, u32[]{:S(2)}) async-start(f32[16,8,128]{2,1,0:T(8,128)} %get-tuple-element.45), calls=%async_computation.8 | async-start | bytes 131072 | tf_op jit(solution)/shard_map/all_to_all | solution.py:423
  227.2 6.4 %downdate.3 = f32[1024,1024]{1,0:T(8,128)} custom-call(f32[1024,1024]{1,0:T(8,128)} %downdate.2.cov_ref, f32[16,16,1024]{2,1,0:T(8,128)} %bitcast.32, f32[128,128]{1,0:T(8,128)} %copy-done.1, f32[128,1024]{1,0:T(8,128)} %copy-done), custom_call_target="tpu_custom_call" | custom-call | tf_op jit(solution)/shard_map/downdate/pallas_call | solution.py:340
  233.6 0.1 all-to-all-done.8
  233.7 0.6 bitcast_add_fusion
  (22 shorter events, 0.2 us)
Async XLA Ops:
  7.2 65.3 %all-gather.7.cloned.1.call-start = ((), (), s32[]{:S(2)}) async-start(), calls=%async_computation.9 | async-start | bytes 2297856 | tf_op jit(solution)/shard_map/all_gather | solution.py:474
  52.3 30.1 %copy-start.5 = (f32[2,128]{1,0:T(2,128)S(1)}, f32[2,128]{1,0:T(2,128)}, u32[]{:S(2)}) copy-start(f32[2,128]{1,0:T(2,128)} %param.11) | copy-start | bytes 3076
  57.5 72.5 %copy-start.4 = (f32[128,128]{1,0:T(8,128)S(1)}, f32[128,128]{1,0:T(8,128)}, u32[]{:S(2)}) copy-start(f32[128,128]{1,0:T(8,128)} %weights_ref.1) | copy-start | bytes 196612
  57.5 14.9 %all-to-all-start.1 = ((f32[16,8,1024]{2,1,0:T(8,128)}), f32[16,8,1024]{2,1,0:T(8,128)S(1)}, u32[]{:S(2)}, u32[]{:S(2)}) async-start(f32[16,8,1024]{2,1,0:T(8,128)} %convolution_bitcast_fusion), calls=%async_computation.1 | async-start | bytes 1048576 | tf_op jit(solution)/shard_map/all_to_all | solution.py:423
  61.2 93.3 %all-gather.9.cloned.1.call-start = ((), (), s32[]{:S(2)}) async-start(), calls=%async_computation.10 | async-start | bytes 1114112 | tf_op jit(solution)/shard_map/all_gather | solution.py:450
  72.5 9.9 %collective-permute-start = (f32[8,1024]{1,0:T(8,128)S(1)}, f32[8,1024]{1,0:T(8,128)S(1)}, u32[]{:S(2)}, u32[]{:S(2)}) collective-permute-start(f32[8,1024]{1,0:T(8,128)S(1)} %reduce_sum.28), channel_id=1, source_target_pairs={{10,0},{11,16},{8,32},{9,48},{14,64},{15,80},{12,96},{13,112},{2,1... | collective-permute-start | bytes 98312 | tf_op jit(solution)/shard_map/ppermute | solution.py:445
  106.8 5.5 %collective-permute-start.1 = (f32[8,8,1152]{2,1,0:T(8,128)S(1)}, f32[8,8,1152]{2,1,0:T(8,128)S(1)}, u32[]{:S(2)}, u32[]{:S(2)}) collective-permute-start(f32[8,8,1152]{2,1,0:T(8,128)S(1)} %all_to_all.47.own_ref), channel_id=1, source_target_pairs={{0,16},{16,0},{32,48},{48,32},{64,80},{80,64},{96,112},{112,96},{1... | collective-permute-start | bytes 884744 | tf_op jit(solution)/shard_map/ppermute | solution.py:434
  120.0 9.9 %all-to-all-start.4 = ((f32[16,8,128]{2,1,0:T(8,128)}), f32[16,8,128]{2,1,0:T(8,128)S(1)}, u32[]{:S(2)}, u32[]{:S(2)}) async-start(f32[16,8,128]{2,1,0:T(8,128)} %get-tuple-element.36), calls=%async_computation.4 | async-start | bytes 131072 | tf_op jit(solution)/shard_map/all_to_all | solution.py:423
  123.5 100.2 %all-gather.11.cloned.1.call-start = ((), (), s32[]{:S(2)}) async-start(), calls=%async_computation.11 | async-start | bytes 1114112 | tf_op jit(solution)/shard_map/all_gather | solution.py:450
  124.1 31.8 %copy-start.2 = (f32[128,1024]{1,0:T(8,128)}, f32[128,1024]{1,0:T(8,128)S(1)}, u32[]{:S(2)}) copy-start(f32[128,1024]{1,0:T(8,128)S(1)} %fusion.11.rest_0_) | copy-start | bytes 1572868
  174.9 9.0 %collective-permute-start.2 = (f32[8,1024]{1,0:T(8,128)S(1)}, f32[8,1024]{1,0:T(8,128)S(1)}, u32[]{:S(2)}, u32[]{:S(2)}) collective-permute-start(f32[8,1024]{1,0:T(8,128)S(1)} %reduce_sum.29), channel_id=1, source_target_pairs={{10,0},{11,16},{8,32},{9,48},{14,64},{15,80},{12,96},{13,112},{2,1... | collective-permute-start | bytes 98312 | tf_op jit(solution)/shard_map/ppermute | solution.py:445
  209.3 5.3 %collective-permute-start.3 = (f32[8,8,1152]{2,1,0:T(8,128)S(1)}, f32[8,8,1152]{2,1,0:T(8,128)S(1)}, u32[]{:S(2)}, u32[]{:S(2)}) collective-permute-start(f32[8,8,1152]{2,1,0:T(8,128)S(1)} %all_to_all.50.own_ref), channel_id=1, source_target_pairs={{0,16},{16,0},{32,48},{48,32},{64,80},{80,64},{96,112},{112,96},{1... | collective-permute-start | bytes 884744 | tf_op jit(solution)/shard_map/ppermute | solution.py:434
  222.3 0.8 copy-start
  223.1 0.6 copy-start.1
  223.7 10.0 %all-to-all-start.8 = ((f32[16,8,128]{2,1,0:T(8,128)}), f32[16,8,128]{2,1,0:T(8,128)S(1)}, u32[]{:S(2)}, u32[]{:S(2)}) async-start(f32[16,8,128]{2,1,0:T(8,128)} %get-tuple-element.45), calls=%async_computation.8 | async-start | bytes 131072 | tf_op jit(solution)/shard_map/all_to_all | solution.py:423
  227.2 6.5 %copy-start.3 = (f32[128,128]{1,0:T(8,128)S(1)}, f32[128,128]{1,0:T(8,128)}, u32[]{:S(2)}) copy-start(f32[128,128]{1,0:T(8,128)} %bitcast_add_fusion.1.weights_ref) | copy-start | bytes 196612
Sparse Core Ops, SparseCore 0:
  10.5 52.9 all-gather.6
  77.7 41.8 all-gather.8
  175.0 41.5 all-gather.10

commit v9 on v8

--- a/solution.py
+++ b/solution.py
@@ -250,10 +250,10 @@
     )(col_index, gathered, readout)
 
 
-def later_kernel(atoms_ref, vectors_ref, masked_ref, weights_ref, bias_ref, out_ref, acc):
+def later_kernel(atoms_ref, vectors_ref, masked_ref, weights_ref, change_ref, bias_ref, out_ref, acc):
     step = pl.program_id(0)
     rows = masked_ref.shape[0] - 2 * SUB
-    w_high, w_low = split(weights_ref[...])
+    w_high, w_low = split(weights_ref[...] + change_ref[...].reshape(FEATURES, FEATURES))
     table = jnp.concatenate(
         [jnp.concatenate([w_high, w_low], axis=1), jnp.concatenate([w_high, jnp.zeros_like(w_low)], axis=1)], axis=0
     )
@@ -286,7 +286,7 @@
         out_ref[:, high_rows // SUB * FEATURES :] = jnp.broadcast_to(total_energy, (GROUP_LOCAL, FEATURES))
 
 
-def later_terms(terms, weights, bias):
+def later_terms(terms, weights, change, bias):
     atoms, vectors, masked = terms
     parts = 4
     lines, count = masked.shape
@@ -302,12 +302,13 @@
             pl.BlockSpec((lines, each), lambda n: (0, n)),
             whole(),
             whole(),
+            whole(),
         ],
         out_specs=whole(),
         scratch_shapes=[pltpu.VMEM((lines, 2 * FEATURES), jnp.float32)],
         compiler_params=params(63),
         name="later_terms",
-    )(atoms, vectors, masked, weights, bias)
+    )(atoms, vectors, masked, weights, change, bias)
 
 
 def downdate_kernel(scale, fresh, cov_ref, rows_ref, *rest):
@@ -474,7 +475,7 @@
             gathered = lax.all_gather(packed, "atm", axis=0, tiled=False)
             chunk = exchange(chunks, "atm").sum(axis=0)
         else:
-            chunk = later_terms(later, current, bias)
+            chunk = later_terms(later, weights, change, bias)
         stacked = lax.all_gather(chunk, "grp", axis=0, tiled=True)
         jac = stacked[:, :width]
         terms = dot(jac, covariance, ((1,), (1,)), three)

time: 242 us -> 241 us (level)
  blocking collectives: 123 us -> 137 us
  waiting for transfers between devices: 19.5 us -> 8.37 us
  starting transfers between devices: 26.2 us -> 23.7 us
    all_to_all x4 -> x5, blocking collectives: 54 us -> 67.9 us  [exchange(): return lax.all_to_all(chunks, axis, 0, 0, tiled=True)]
    all_to_all x3 -> x2, waiting for transfers between devices: 17 us -> 5.87 us  [exchange(): return lax.all_to_all(chunks, axis, 0, 0, tiled=True)]
    all_to_all x3 -> x2, starting transfers between devices: 10.7 us -> 6.99 us  [exchange(): return lax.all_to_all(chunks, axis, 0, 0, tiled=True)]
  transfers between devices with their start and end apart: 10 -> 9, of which waited for: 5 -> 4; matrix products, arithmetic and copies ran while one was open for 4% -> 3% of each run, Pallas kernels for 16% -> 16%
where the time goes in v9:
time: 241 us
  blocking collectives  137 us (57%)
  Pallas kernels  41.4 us (17%)
  starting transfers between devices  23.7 us (10%)
  between operations  13.9 us (6%)
  matrix products  12.2 us (5%)
  waiting for transfers between devices  8.37 us (3%)
    all_to_all x5, blocking collectives, exchange(): return lax.all_to_all(chunks, axis, 0, 0, tiled=True)  67.9 us
    all_gather x2, blocking collectives, body(): stacked = lax.all_gather(chunk, 'grp', axis=0, tiled=True)  41.2 us
    all_to_all x2, blocking collectives, gather_pair(): lax.all_to_all(copies, 'grp', 0, 0, tiled=True, axis_index_groups=lanes)  27.5 us
    pallas_call x2, Pallas kernels, solve_update(): pl.pallas_call(functools.partial(update_kernel, order), grid=(1,), out_sh...  15.4 us
    pallas_call x2, Pallas kernels, downdate(): pl.pallas_call(functools.partial(downdate_kernel, scale, len(right) == 2)...  12.7 us
    dot_general x7, matrix products, dot(): lax.dot_general(a, b, ((contract[0], contract[1]), ((), ())), precision=p...  12.2 us
    ppermute x2, starting transfers between devices, gather_pair(): other = lax.ppermute(own, 'grp', [(i, i ^ 1) for i in range(2 * count)])  8.81 us
    ppermute x2, starting transfers between devices, swap(): return lax.ppermute(x, ('grp', 'atm'), pairs)  7.83 us
  transfers between devices with their start and end apart: 9, of which 4 were waited for; matrix products, arithmetic and copies ran while one was open for 3% of the time, Pallas kernels for 16%

profile of v9, /device:TPU:1, one launch (start us, length us, event | category | flops | bytes accessed | tf_op | source)
XLA Modules:
  0.0 240.5 jit_solution(4158703515026832613)
XLA Ops:
  7.2 0.0 all-gather.7.cloned.1.call-start
  7.2 2.8 %first_terms.1 = (f32[16,8,1152]{2,1,0:T(8,128)}, f32[264,128]{1,0:T(8,128)}) custom-call(f32[2,256,128]{2,1,0:T(8,128)} %next_ref.1, f32[2,256,128]{2,1,0:T(8,128)} %next_ref.1, s32[2,256]{1,0:T(2,128)} %kinds_ref.1, s32[2,256]{1,0:T(2,128)} %member_ref.1, f32[128,128]{1,0:T(8,128)} %weights_ref.3, f32[1,128]{1,0:T(1,128)} %bitcast.35, f32[4,128]{1,0:T(4,128)} %readout_ref.3), custom_call_target="tpu_custom_call" | custom-call | tf_op jit(solution)/shard_map/first_terms/pallas_call | solution.py:183
  10.0 0.0 all-gather.7.cloned.1.call-update
  10.0 0.0 all-gather.9.cloned.1.call-start
  10.0 18.9 %all_to_all.45 = f32[16,8,1152]{2,1,0:T(8,128)S(1)} all-to-all(f32[16,8,1152]{2,1,0:T(8,128)} %get-tuple-element.24), channel_id=1, replica_groups=mesh['grp'=16,'atm'=16] {'atm'}, dimensions={0} | all-to-all | bytes 1179648 | tf_op jit(solution)/shard_map/all_to_all | solution.py:424
  29.0 23.4 %all_gather.24.energy_ref = f32[128,1152]{1,0:T(8,128)S(1)} all-gather(f32[8,1152]{1,0:T(8,128)S(1)} %reduce_sum.27), channel_id=1, replica_groups=mesh['grp'=16,'atm'=16] {'grp'}, dimensions={0}, use_global_device_ids=true | all-gather | bytes 626688 | tf_op jit(solution)/shard_map/all_gather | solution.py:479
  52.3 4.4 %convolution_bitcast_fusion = f32[16,8,1024]{2,1,0:T(8,128)S(1)} fusion(f32[1024,1024]{1,0:T(8,128)} %cov_ref.1, f32[128,1152]{1,0:T(8,128)S(1)} %all_gather.24.energy_ref), kind=kOutput, calls=%fused_computation.3 | convolution fusion | flops 805306368 | bytes 5242880 | tf_op jit(solution)/shard_map/dot_general | solution.py:23
  56.8 14.1 %all_to_all.46 = f32[16,8,1024]{2,1,0:T(8,128)S(1)} all-to-all(f32[16,8,1024]{2,1,0:T(8,128)S(1)} %convolution_bitcast_fusion), channel_id=1, replica_groups=mesh['grp'=16,'atm'=16] {'atm'}, dimensions={0} | all-to-all | bytes 1048576 | tf_op jit(solution)/shard_map/all_to_all | solution.py:424
  71.0 0.0 all-gather.7.cloned.1.call-done
  71.0 0.6 pad_maximum_fusion
  71.6 0.0 all-gather.9.cloned.1.call-update
  71.6 5.2 %collective-permute-start = (f32[8,1024]{1,0:T(8,128)S(1)}, f32[8,1024]{1,0:T(8,128)S(1)}, u32[]{:S(2)}, u32[]{:S(2)}) collective-permute-start(f32[8,1024]{1,0:T(8,128)S(1)} %reduce_sum.28), channel_id=1, source_target_pairs={{10,0},{11,16},{8,32},{9,48},{14,64},{15,80},{12,96},{13,112},{2,1... | collective-permute-start | bytes 98312 | tf_op jit(solution)/shard_map/ppermute | solution.py:446
  76.9 4.8 %prepare_terms.1 = (bf16[4096,256]{1,0:T(8,128)(2,1)}, f32[4096,128]{1,0:T(8,128)}, bf16[144,4096]{1,0:T(8,128)(2,1)}) custom-call(s32[1]{0:T(128)} %bitcast.3.col_ref, f32[16,264,128]{2,1,0:T(8,128)} %bitcast.33, f32[4,128]{1,0:T(4,128)} %readout_ref.3), custom_call_target="tpu_custom_call" | custom-call | tf_op jit(solution)/shard_map/prepare_terms/pallas_call | solution.py:237
  81.7 0.1 broadcast_in_dim.6
  81.8 0.5 fusion.3
  82.4 9.9 %all_to_all.47.parts_ref = f32[16,8,128]{2,1,0:T(8,128)S(1)} all-to-all(f32[16,8,128]{2,1,0:T(8,128)S(1)} %broadcast_in_dim.7), channel_id=1, replica_groups=mesh['grp'=16,'atm'=16] {'atm'}, dimensions={0} | all-to-all | bytes 131072 | tf_op jit(solution)/shard_map/all_to_all | solution.py:424
  92.3 13.7 %all_to_all.48.own_ref = f32[8,8,1152]{2,1,0:T(8,128)S(1)} all-to-all(f32[8,8,1152]{2,1,0:T(8,128)S(1)} %pack_gains.2), channel_id=1, replica_groups={{0,32,64,96,128,160,192,224},{16,48,80,112,144,176,208,240},{1,33,65,97..., dimensions={0} | all-to-all | bytes 589824 | tf_op jit(solution)/shard_map/all_to_all | solution.py:434
  106.0 4.7 %collective-permute-start.1 = (f32[8,8,1152]{2,1,0:T(8,128)S(1)}, f32[8,8,1152]{2,1,0:T(8,128)S(1)}, u32[]{:S(2)}, u32[]{:S(2)}) collective-permute-start(f32[8,8,1152]{2,1,0:T(8,128)S(1)} %all_to_all.48.own_ref), channel_id=1, source_target_pairs={{0,16},{16,0},{32,48},{48,32},{64,80},{80,64},{96,112},{112,96},{1... | collective-permute-start | bytes 884744 | tf_op jit(solution)/shard_map/ppermute | solution.py:435
  110.8 1.2 collective-permute-done.1.other_ref
  112.0 7.7 %inverse_and_change.2 = (f32[128,128]{1,0:T(8,128)S(1)}, f32[128,1024]{1,0:T(8,128)S(1)}, f32[16,8,128]{2,1,0:T(8,128)}) custom-call(s32[1]{0:T(128)} %bitcast.4.side_ref, f32[8,8,1152]{2,1,0:T(8,128)S(1)} %all_to_all.48.own_ref, f32[8,8,1152]{2,1,0:T(8,128)S(1)} %collective-permute-done.1.other_ref, f32[128,1152]{1,0:T(8,128)S(1)} %all_gather.24.energy_ref, ...), custom_call_target="tpu_custom_call" | custom-call | tf_op jit(solution)/shard_map/inverse_and_change/pallas_call | solution.py:411
  119.6 3.5 %all-to-all-start.4 = ((f32[16,8,128]{2,1,0:T(8,128)}), f32[16,8,128]{2,1,0:T(8,128)S(1)}, u32[]{:S(2)}, u32[]{:S(2)}) async-start(f32[16,8,128]{2,1,0:T(8,128)} %get-tuple-element.36), calls=%async_computation.4 | async-start | bytes 131072 | tf_op jit(solution)/shard_map/all_to_all | solution.py:424
  123.1 0.0 all-gather.11.cloned.1.call-start
  123.2 0.6 fusion.11.rest_0_
  123.8 5.8 %all-to-all-done.4.change_ref = f32[16,8,128]{2,1,0:T(8,128)S(1)} async-done(((f32[16,8,128]{2,1,0:T(8,128)}), f32[16,8,128]{2,1,0:T(8,128)S(1)}, u32[]{:S(2)}, u32[]{:S(2)}) %all-to-all-start.4) | async-done | bytes 65568 | tf_op jit(solution)/shard_map/all_to_all | solution.py:424
  129.6 0.6 copy-done.3
  130.2 5.7 %later_terms.1 = f32[8,1152]{1,0:T(8,128)} custom-call(bf16[4096,256]{1,0:T(8,128)(2,1)} %get-tuple-element.31.atoms_ref, f32[4096,128]{1,0:T(8,128)} %get-tuple-element.32.vectors_ref, bf16[144,4096]{1,0:T(8,128)(2,1)} %get-tuple-element.33.masked_ref, f32[128,128]{1,0:T(8,128)} %weights_ref.3, f32[16,8,128]{2,1,0:T(8,128)} %copy-done.3, f32[1,128]{1,0:T(1,128)} %bitcast.36), custom_call_target="tpu_custom_call" | custom-call | tf_op jit(solution)/shard_map/later_terms/pallas_call | solution.py:295
  135.9 17.8 %all_gather.27.energy_ref = f32[128,1152]{1,0:T(8,128)S(1)} all-gather(f32[8,1152]{1,0:T(8,128)} %later_terms.1), channel_id=1, replica_groups=mesh['grp'=16,'atm'=16] {'grp'}, dimensions={0}, use_global_device_ids=true | all-gather | bytes 626688 | tf_op jit(solution)/shard_map/all_gather | solution.py:479
  153.7 0.4 fusion.8
  154.1 0.0 all-gather.9.cloned.1.call-done
  154.1 1.4 fusion.2
  155.6 4.4 %fusion.1 = f32[16,8,1024]{2,1,0:T(8,128)S(1)} fusion(f32[128,1024]{1,0:T(8,128)S(1)} %fusion.2, f32[1024,1024]{1,0:T(8,128)} %cov_ref.1, f32[128,1152]{1,0:T(8,128)S(1)} %all_gather.27.energy_ref), kind=kOutput, calls=%fused_computation.2 | convolution fusion | flops 805568512 | bytes 5767168 | tf_op jit(solution)/shard_map/dot_general | solution.py:23
  160.0 13.8 %all_to_all.49 = f32[16,8,1024]{2,1,0:T(8,128)S(1)} all-to-all(f32[16,8,1024]{2,1,0:T(8,128)S(1)} %fusion.1), channel_id=1, replica_groups=mesh['grp'=16,'atm'=16] {'atm'}, dimensions={0} | all-to-all | bytes 1048576 | tf_op jit(solution)/shard_map/all_to_all | solution.py:424
  173.8 0.6 pad_maximum_fusion.1
  174.4 0.0 all-gather.11.cloned.1.call-update
  174.5 2.6 %collective-permute-start.2 = (f32[8,1024]{1,0:T(8,128)S(1)}, f32[8,1024]{1,0:T(8,128)S(1)}, u32[]{:S(2)}, u32[]{:S(2)}) collective-permute-start(f32[8,1024]{1,0:T(8,128)S(1)} %reduce_sum.29), channel_id=1, source_target_pairs={{10,0},{11,16},{8,32},{9,48},{14,64},{15,80},{12,96},{13,112},{2,1... | collective-permute-start | bytes 98312 | tf_op jit(solution)/shard_map/ppermute | solution.py:446
  177.1 6.4 %downdate.2.cov_ref = f32[1024,1024]{1,0:T(8,128)} custom-call(f32[1024,1024]{1,0:T(8,128)} %cov_ref.1, f32[16,16,1024]{2,1,0:T(8,128)} %bitcast.32, f32[128,1024]{1,0:T(8,128)} %copy-done.2), custom_call_target="tpu_custom_call" | custom-call | tf_op jit(solution)/shard_map/downdate/pallas_call | solution.py:341
  183.5 0.5 fusion.6
  184.0 11.1 %all_to_all.50.parts_ref = f32[16,8,128]{2,1,0:T(8,128)S(1)} all-to-all(f32[16,8,128]{2,1,0:T(8,128)S(1)} %broadcast_in_dim.8), channel_id=1, replica_groups=mesh['grp'=16,'atm'=16] {'atm'}, dimensions={0} | all-to-all | bytes 131072 | tf_op jit(solution)/shard_map/all_to_all | solution.py:424
  195.1 13.8 %all_to_all.51.own_ref = f32[8,8,1152]{2,1,0:T(8,128)S(1)} all-to-all(f32[8,8,1152]{2,1,0:T(8,128)S(1)} %pack_gains.3), channel_id=1, replica_groups={{0,32,64,96,128,160,192,224},{16,48,80,112,144,176,208,240},{1,33,65,97..., dimensions={0} | all-to-all | bytes 589824 | tf_op jit(solution)/shard_map/all_to_all | solution.py:434
  208.9 4.1 %collective-permute-start.3 = (f32[8,8,1152]{2,1,0:T(8,128)S(1)}, f32[8,8,1152]{2,1,0:T(8,128)S(1)}, u32[]{:S(2)}, u32[]{:S(2)}) collective-permute-start(f32[8,8,1152]{2,1,0:T(8,128)S(1)} %all_to_all.51.own_ref), channel_id=1, source_target_pairs={{0,16},{16,0},{32,48},{48,32},{64,80},{80,64},{96,112},{112,96},{1... | collective-permute-start | bytes 884744 | tf_op jit(solution)/shard_map/ppermute | solution.py:435
  213.0 1.2 collective-permute-done.3.other_ref
  214.2 7.7 %inverse_and_change.3 = (f32[128,128]{1,0:T(8,128)S(1)}, f32[128,1024]{1,0:T(8,128)S(1)}, f32[16,8,128]{2,1,0:T(8,128)}) custom-call(s32[1]{0:T(128)} %bitcast.4.side_ref, f32[8,8,1152]{2,1,0:T(8,128)S(1)} %all_to_all.51.own_ref, f32[8,8,1152]{2,1,0:T(8,128)S(1)} %collective-permute-done.3.other_ref, f32[128,1152]{1,0:T(8,128)S(1)} %all_gather.27.energy_ref, ...), custom_call_target="tpu_custom_call" | custom-call | tf_op jit(solution)/shard_map/inverse_and_change/pallas_call | solution.py:411
  221.9 0.8 copy-done
  222.7 0.6 copy-done.1
  223.4 3.5 %all-to-all-start.8 = ((f32[16,8,128]{2,1,0:T(8,128)}), f32[16,8,128]{2,1,0:T(8,128)S(1)}, u32[]{:S(2)}, u32[]{:S(2)}) async-start(f32[16,8,128]{2,1,0:T(8,128)} %get-tuple-element.45), calls=%async_computation.8 | async-start | bytes 131072 | tf_op jit(solution)/shard_map/all_to_all | solution.py:424
  226.9 6.4 %downdate.3 = f32[1024,1024]{1,0:T(8,128)} custom-call(f32[1024,1024]{1,0:T(8,128)} %downdate.2.cov_ref, f32[16,16,1024]{2,1,0:T(8,128)} %bitcast.34, f32[128,128]{1,0:T(8,128)} %copy-done.1, f32[128,1024]{1,0:T(8,128)} %copy-done), custom_call_target="tpu_custom_call" | custom-call | tf_op jit(solution)/shard_map/downdate/pallas_call | solution.py:341
  233.3 0.1 all-to-all-done.8
  233.3 0.6 bitcast_add_fusion
  (22 shorter events, 0.2 us)
Async XLA Ops:
  7.2 63.8 %all-gather.7.cloned.1.call-start = ((), (), s32[]{:S(2)}) async-start(), calls=%async_computation.9 | async-start | bytes 2297856 | tf_op jit(solution)/shard_map/all_gather | solution.py:475
  10.0 144.1 %all-gather.9.cloned.1.call-start = ((), (), s32[]{:S(2)}) async-start(), calls=%async_computation.10 | async-start | bytes 1114112 | tf_op jit(solution)/shard_map/all_gather | solution.py:451
  52.3 29.4 %copy-start.6 = (f32[2,128]{1,0:T(2,128)S(1)}, f32[2,128]{1,0:T(2,128)}, u32[]{:S(2)}) copy-start(f32[2,128]{1,0:T(2,128)} %param.11) | copy-start | bytes 3076
  71.6 10.1 %collective-permute-start = (f32[8,1024]{1,0:T(8,128)S(1)}, f32[8,1024]{1,0:T(8,128)S(1)}, u32[]{:S(2)}, u32[]{:S(2)}) collective-permute-start(f32[8,1024]{1,0:T(8,128)S(1)} %reduce_sum.28), channel_id=1, source_target_pairs={{10,0},{11,16},{8,32},{9,48},{14,64},{15,80},{12,96},{13,112},{2,1... | collective-permute-start | bytes 98312 | tf_op jit(solution)/shard_map/ppermute | solution.py:446
  106.0 5.9 %collective-permute-start.1 = (f32[8,8,1152]{2,1,0:T(8,128)S(1)}, f32[8,8,1152]{2,1,0:T(8,128)S(1)}, u32[]{:S(2)}, u32[]{:S(2)}) collective-permute-start(f32[8,8,1152]{2,1,0:T(8,128)S(1)} %all_to_all.48.own_ref), channel_id=1, source_target_pairs={{0,16},{16,0},{32,48},{48,32},{64,80},{80,64},{96,112},{112,96},{1... | collective-permute-start | bytes 884744 | tf_op jit(solution)/shard_map/ppermute | solution.py:435
  119.6 10.0 %all-to-all-start.4 = ((f32[16,8,128]{2,1,0:T(8,128)}), f32[16,8,128]{2,1,0:T(8,128)S(1)}, u32[]{:S(2)}, u32[]{:S(2)}) async-start(f32[16,8,128]{2,1,0:T(8,128)} %get-tuple-element.36), calls=%async_computation.4 | async-start | bytes 131072 | tf_op jit(solution)/shard_map/all_to_all | solution.py:424
  123.1 100.2 %all-gather.11.cloned.1.call-start = ((), (), s32[]{:S(2)}) async-start(), calls=%async_computation.11 | async-start | bytes 1114112 | tf_op jit(solution)/shard_map/all_gather | solution.py:451
  123.8 31.8 %copy-start.2 = (f32[128,1024]{1,0:T(8,128)}, f32[128,1024]{1,0:T(8,128)S(1)}, u32[]{:S(2)}) copy-start(f32[128,1024]{1,0:T(8,128)S(1)} %fusion.11.rest_0_) | copy-start | bytes 1572868
  129.6 0.6 copy-start.3
  174.5 9.0 %collective-permute-start.2 = (f32[8,1024]{1,0:T(8,128)S(1)}, f32[8,1024]{1,0:T(8,128)S(1)}, u32[]{:S(2)}, u32[]{:S(2)}) collective-permute-start(f32[8,1024]{1,0:T(8,128)S(1)} %reduce_sum.29), channel_id=1, source_target_pairs={{10,0},{11,16},{8,32},{9,48},{14,64},{15,80},{12,96},{13,112},{2,1... | collective-permute-start | bytes 98312 | tf_op jit(solution)/shard_map/ppermute | solution.py:446
  208.9 5.3 %collective-permute-start.3 = (f32[8,8,1152]{2,1,0:T(8,128)S(1)}, f32[8,8,1152]{2,1,0:T(8,128)S(1)}, u32[]{:S(2)}, u32[]{:S(2)}) collective-permute-start(f32[8,8,1152]{2,1,0:T(8,128)S(1)} %all_to_all.51.own_ref), channel_id=1, source_target_pairs={{0,16},{16,0},{32,48},{48,32},{64,80},{80,64},{96,112},{112,96},{1... | collective-permute-start | bytes 884744 | tf_op jit(solution)/shard_map/ppermute | solution.py:435
  221.9 0.8 copy-start
  222.7 0.6 copy-start.1
  223.4 10.0 %all-to-all-start.8 = ((f32[16,8,128]{2,1,0:T(8,128)}), f32[16,8,128]{2,1,0:T(8,128)S(1)}, u32[]{:S(2)}, u32[]{:S(2)}) async-start(f32[16,8,128]{2,1,0:T(8,128)} %get-tuple-element.45), calls=%async_computation.8 | async-start | bytes 131072 | tf_op jit(solution)/shard_map/all_to_all | solution.py:424
  226.9 6.5 %copy-start.4 = (f32[16,8,128]{2,1,0:T(8,128)S(1)}, f32[16,8,128]{2,1,0:T(8,128)}, u32[]{:S(2)}) copy-start(f32[16,8,128]{2,1,0:T(8,128)} %copy-done.3) | copy-start | bytes 196612
  226.9 6.4 %copy-start.5 = (f32[128,128]{1,0:T(8,128)S(1)}, f32[128,128]{1,0:T(8,128)}, u32[]{:S(2)}) copy-start(f32[128,128]{1,0:T(8,128)} %weights_ref.3) | copy-start | bytes 196612
Sparse Core Ops, SparseCore 0:
  10.5 54.7 all-gather.6
  71.8 45.8 all-gather.8
  174.6 41.6 all-gather.10
